TPU v7x, 32 devices: a whole 2x2x4 slice. The times are simulated.
32 devices in a mesh: dom: 8 (over z, y), bin: 4 (over x, core).
Axes of the slice: x: 2, y: 2, z: 4, core: 2. Of those that a mesh axis runs over, the one named last changes fastest.
Arguments:
- field_in: float32 [8, 131072], P(None, ('dom', 'bin')), may hold values from -6 to 6
- heading_in: float32 [3, 131072], P(None, ('dom', 'bin')), may hold values from -3 to 3
- launch_domain: int32 [131072, 1], P(('dom', 'bin')), may hold values from 0 to 7; in each aligned block of 4096 rows (0 to 4095, 4096 to 8191, ...) at most 1024 rows name the same one
- hop_domain: int32 [3, 131072, 1], P(None, ('dom', 'bin')), may hold values from 0 to 7; in each aligned block of 4096 rows (0 to 4095, 4096 to 8191, ..., all dimensions but the last counted through in order) at most 1024 rows name the same one
- hit_facet: int32 [4, 131072], P(None, ('dom', 'bin')), may hold values from 0 to 8191
- path_phase: float32 [4, 131072], P(None, ('dom', 'bin')), may hold values from -3.140625 to 3.140625
- facet_polar: float32 [65536], P('dom'), may hold values from -3.140625 to 3.140625
- facet_azimuth: float32 [65536], P('dom'), may hold values from -3.140625 to 3.140625
- facet_tilt: float32 [65536], P('dom'), may hold values from -3.140625 to 3.140625
- surface_resistance: float32 [65536], P('dom'), may hold values from 0.2 to 5
- surface_reactance: float32 [65536], P('dom'), may hold values from -1 to 1
- kernel: bfloat16 [2, 65536, 1024], P(None, ('dom', 'bin')), may hold values from -0.005859375 to 0.005859375
Outputs:
- far_field: float32 [8, 1024], P(None, ('dom', 'bin'))
- exit_field: float32 [8, 131072], P(None, ('dom', 'bin'))
Inputs may be any that keep to these rules, and one draw needn't show every extreme that they name: `launch_domain`: among the 4096 tubes launched from one device (aligned blocks of the tube dimension), each domain is named at most 1024 times in each bounce, and exactly 1024 times by some domain in some blocks. `hop_domain`: among the 4096 tubes launched from one device, each domain is named at most 1024 times in each bounce, and exactly 1024 times by some domain in some blocks.
All inputs are finite; a program needn't handle non-finite values.
Results may differ from a plain program's by a relative error of at most 0.0029.
Values sent between devices are 32-bit elements; how exact they have to be, the bound alone decides.
No kernel may reach another device: no remote copies, remote signals or barrier semaphores. Data moves between devices by JAX's collectives and lax.ppermute only.
A program may use at most 128 MiB of HBM per device.

v0:
```python
import jax
import jax.numpy as jnp
from jax import lax
from jax.sharding import PartitionSpec as P

BOUNCES = 4


def facet_frame(polar_angle, azimuth, tilt_angle, resistance, reactance):
    return jnp.stack(
        [
            jnp.sin(polar_angle) * jnp.cos(azimuth),
            jnp.sin(polar_angle) * jnp.sin(azimuth),
            jnp.cos(polar_angle),
            resistance,
            reactance,
            jnp.cos(tilt_angle),
            jnp.sin(tilt_angle),
        ],
        axis=0,
    )


def divide(top_real, top_imag, low_real, low_imag):
    modulus = low_real * low_real + low_imag * low_imag
    return (
        (top_real * low_real + top_imag * low_imag) / modulus,
        (top_imag * low_real - top_real * low_imag) / modulus,
    )


def turn_phase(tube_field, phase_angle):
    phase_cos = jnp.cos(phase_angle)
    phase_sin = jnp.sin(phase_angle)
    return jnp.concatenate(
        [
            phase_cos * tube_field[0:4] - phase_sin * tube_field[4:8],
            phase_sin * tube_field[0:4] + phase_cos * tube_field[4:8],
        ],
        axis=0,
    )


def reflect(tube_field, heading, facet_rows):
    normal = facet_rows[0:3]
    incidence = jnp.sum(heading * normal, axis=0)
    cosine = jnp.abs(incidence)
    eta_real = facet_rows[3]
    eta_imag = facet_rows[4]
    tilt_cos = facet_rows[5]
    tilt_sin = facet_rows[6]
    te_real, te_imag = divide(cosine - eta_real, -eta_imag, cosine + eta_real, eta_imag)
    tm_real, tm_imag = divide(
        eta_real * cosine - 1.0, eta_imag * cosine, eta_real * cosine + 1.0, eta_imag * cosine
    )
    upper_real = tilt_cos * tube_field[0:2] + tilt_sin * tube_field[2:4]
    lower_real = tilt_cos * tube_field[2:4] - tilt_sin * tube_field[0:2]
    upper_imag = tilt_cos * tube_field[4:6] + tilt_sin * tube_field[6:8]
    lower_imag = tilt_cos * tube_field[6:8] - tilt_sin * tube_field[4:6]
    result = jnp.concatenate(
        [
            te_real * upper_real - te_imag * upper_imag,
            tm_real * lower_real - tm_imag * lower_imag,
            te_real * upper_imag + te_imag * upper_real,
            tm_real * lower_imag + tm_imag * lower_real,
        ],
        axis=0,
    )
    turned = heading - 2.0 * incidence * normal
    return (result, turned)


def body(
    field_in,
    heading_in,
    launch_domain,
    hop_domain,
    hit_facet,
    path_phase,
    facet_polar,
    facet_azimuth,
    facet_tilt,
    surface_resistance,
    surface_reactance,
    kernel,
):
    domains = lax.axis_size("dom")
    facet_count = facet_polar.shape[0]
    tube_field = field_in
    heading = heading_in
    tables = lax.all_gather(
        jnp.stack(
            [facet_polar, facet_azimuth, facet_tilt, surface_resistance, surface_reactance], axis=0
        ),
        "dom",
        axis=1,
        tiled=True,
    )
    frame_all = facet_frame(tables[0], tables[1], tables[2], tables[3], tables[4])
    facet_sums = jnp.zeros((8, facet_count * domains), jnp.float32)
    for bounce in range(BOUNCES):
        if bounce == 0:
            target = launch_domain[:, 0]
        else:
            target = hop_domain[bounce - 1, :, 0]
        facet_ids = hit_facet[bounce]
        phased = turn_phase(tube_field, path_phase[bounce])
        global_facet = target * facet_count + facet_ids
        facet_rows = jnp.take(frame_all, global_facet, axis=1)
        tube_field, heading = reflect(phased, heading, facet_rows)
        facet_sums = facet_sums.at[:, global_facet].add(tube_field)
    quarter = lax.psum_scatter(facet_sums, ("dom", "bin"), scatter_dimension=1, tiled=True)
    rounded = quarter.astype(jnp.bfloat16)
    real_part = jnp.dot(rounded, kernel[0], preferred_element_type=jnp.float32)
    imag_part = jnp.dot(rounded, kernel[1], preferred_element_type=jnp.float32)
    partial_value = jnp.concatenate(
        [real_part[0:4] - imag_part[4:8], imag_part[0:4] + real_part[4:8]], axis=0
    )
    far_field = lax.psum_scatter(partial_value, ("dom", "bin"), scatter_dimension=1, tiled=True)
    return (far_field, tube_field)


def solution(mesh):
    in_specs = (
        P(None, ("dom", "bin")),
        P(None, ("dom", "bin")),
        P(("dom", "bin"), None),
        P(None, ("dom", "bin"), None),
        P(None, ("dom", "bin")),
        P(None, ("dom", "bin")),
        P("dom"),
        P("dom"),
        P("dom"),
        P("dom"),
        P("dom"),
        P(None, ("dom", "bin"), None),
    )
    out_specs = (P(None, ("dom", "bin")), P(None, ("dom", "bin")))
    return jax.shard_map(body, mesh=mesh, in_specs=in_specs, out_specs=out_specs, check_vma=False)
```

profile of v0, /device:TPU:0, one launch (start us, length us, event | category | flops | bytes accessed | tf_op | source)
XLA Modules:
  0.0 883.2 jit_solution(7729979386592521378)
XLA Ops:
  7.2 1.7 stack.32
  9.0 0.8 slice_multiply_fusion.1
  9.8 1.1 fusion.27
  10.9 0.6 compare_and_fusion.2
  11.5 0.6 compare_and_fusion
  12.1 0.6 broadcast_clamp_fusion
  12.7 1.8 compare_select_fusion
  14.5 0.6 compare_and_fusion.1
  15.1 0.6 compare_and_fusion.3
  15.7 0.6 broadcast_clamp_fusion.1
  16.3 0.6 broadcast_clamp_fusion.3
  16.9 3.4 slice_cosine_fusion.2
  20.3 1.0 multiply_add_fusion.3
  21.4 40.8 %all-gather.2.cloned.1.call-done = f32[5,65536]{1,0:T(8,128)} async-done(((f32[5,8192]{1,0:T(8,128)}), f32[5,65536]{1,0:T(8,128)}) %all-gather.2.cloned.1.call-update) | async-done | bytes 1310736 | tf_op jit(solution)/shard_map/all_gather | solution.py:91
  62.1 1.9 slice.284
  64.0 24.4 %slice_sine_fusion = (f32[1,65536]{1,0:T(1,128)S(1)}, f32[1,65536]{1,0:T(1,128)S(1)}, f32[1,65536]{1,0:T(1,128)S(1)}, f32[1,65536]{1,0:T(1,128)}, f32[1,65536]{1,0:T(1,128)}) fusion(f32[5,65536]{1,0:T(8,128)} %all-gather.2.cloned.1.call-done), kind=kLoop, calls=%fused_computation.20 | loop fusion | flops 131072 | bytes 2097152 | tf_op jit(solution)/shard_map/sin | solution.py:18
  88.4 4.6 stack.33
  93.0 16.9 %copy.100 = f32[7,65536]{0,1:T(8,128)} copy(f32[7,65536]{1,0:T(8,128)S(1)} %stack.33) | data formatting | bytes 3670016 | tf_op jit(solution)/shard_map/stack | solution.py:10
  109.9 21.3 %gather_fusion.3 = f32[4096,7]{1,0:T(8,128)S(1)} fusion(f32[7,65536]{0,1:T(8,128)} %copy.100, s32[4096]{0:T(1024)S(1)} %copy-done.3), kind=kCustom, calls=%fused_computation.3.clone | custom fusion | bytes 245760 | tf_op jit(solution)/shard_map/jit(_take)/gather | solution.py:109
  131.3 0.6 copy.110
  131.9 21.3 %gather_fusion.2 = f32[4096,7]{1,0:T(8,128)S(1)} fusion(f32[7,65536]{0,1:T(8,128)} %copy.100, s32[4096]{0:T(1024)S(1)} %copy-done.5), kind=kCustom, calls=%fused_computation.2.clone | custom fusion | bytes 245760 | tf_op jit(solution)/shard_map/jit(_take)/gather | solution.py:109
  153.2 0.6 copy.107
  153.9 21.3 %gather_fusion.1 = f32[4096,7]{1,0:T(8,128)S(1)} fusion(f32[7,65536]{0,1:T(8,128)} %copy.100, s32[4096]{0:T(1024)S(1)} %broadcast_clamp_fusion.2), kind=kCustom, calls=%fused_computation.1.clone | custom fusion | bytes 245760 | tf_op jit(solution)/shard_map/jit(_take)/gather | solution.py:109
  175.2 24.7 %gather_fusion = f32[4096,7]{1,0:T(8,128)} fusion(f32[7,65536]{0,1:T(8,128)} %copy.100, s32[4096]{0:T(1024)S(1)} %copy-done.4), kind=kCustom, calls=%fused_computation.clone | custom fusion | bytes 245760 | tf_op jit(solution)/shard_map/jit(_take)/gather | solution.py:109
  200.0 2.3 copy.101
  202.2 0.6 copy.104
  202.9 0.1 select_bitcast_fusion.2
  203.0 0.1 multiply_reduce_fusion.1
  203.1 0.2 fusion.12
  203.3 0.2 fusion.16
  203.5 0.1 multiply_reduce_fusion
  203.6 0.1 fusion.10
  203.7 0.2 fusion.24
  203.9 0.2 fusion.20
  204.0 0.1 multiply_subtract_fusion.18
  204.1 0.1 multiply_subtract_fusion.21
  204.2 0.1 maximum_bitcast_fusion
  204.3 0.1 multiply_add_fusion.2
  204.4 0.1 multiply_subtract_fusion.17
  204.5 0.1 multiply_subtract_fusion.14
  204.6 0.1 maximum_bitcast_fusion.1
  204.7 0.1 multiply_add_fusion.1
  204.7 0.1 multiply_subtract_fusion.13
  204.8 0.1 multiply_subtract_fusion.10
  204.9 0.1 maximum_bitcast_fusion.2
  205.0 0.6 copy.108
  205.6 2.0 copy.105
  207.6 1.9 copy.102
  209.5 0.1 multiply_add_fusion
  209.6 0.1 multiply_subtract_fusion.9
  209.6 0.1 multiply_subtract_fusion.6
  209.7 0.1 pad_maximum_fusion
  209.8 1.9 copy.111
  211.7 36.0 %scatter_custom_fusion = f32[8,65536]{0,1:T(8,128)} fusion(s32[4096]{0:T(1024)} %bitcast.169, f32[4096,8]{1,0:T(8,128)} %copy.102, f32[]{:T(128)} %constant.4.clone.1), kind=kCustom, calls=%fused_computation.8 | custom fusion | flops 32768 | bytes 2097664 | tf_op jit(solution)/shard_map/scatter-add | solution.py:111
  247.7 42.0 %scatter_fusion = f32[8,65536]{0,1:T(8,128)} fusion(f32[8,65536]{0,1:T(8,128)} %scatter_custom_fusion, s32[4096]{0:T(1024)S(1)} %bitcast.134, f32[4096,8]{1,0:T(8,128)} %copy.105), kind=kCustom, calls=%fused_computation.5 | custom fusion | flops 32768 | bytes 409600 | tf_op jit(solution)/shard_map/scatter-add | solution.py:111
  289.7 41.7 %scatter_fusion.1 = f32[8,65536]{0,1:T(8,128)} fusion(f32[8,65536]{0,1:T(8,128)} %scatter_fusion, s32[4096]{0:T(1024)S(1)} %bitcast.133, f32[4096,8]{1,0:T(8,128)S(1)} %copy.108), kind=kCustom, calls=%fused_computation.6 | custom fusion | flops 32768 | bytes 409600 | tf_op jit(solution)/shard_map/scatter-add | solution.py:111
  331.4 42.0 %scatter_fusion.2 = f32[8,65536]{0,1:T(8,128)} fusion(f32[8,65536]{0,1:T(8,128)} %scatter_fusion.1, s32[4096]{0:T(1024)S(1)} %bitcast.132, f32[4096,8]{1,0:T(8,128)} %copy.111), kind=kCustom, calls=%fused_computation.7 | custom fusion | flops 32768 | bytes 409600 | tf_op jit(solution)/shard_map/scatter-add | solution.py:111
  373.4 0.0 reduce-scatter.7.cloned.1.call-start
  373.5 352.6 %reduce-scatter.5.cloned.1.call-done = f32[8,2048]{0,1:T(8,128)} async-done(((f32[8,65536]{0,1:T(8,128)}), f32[8,2048]{0,1:T(8,128)}) %reduce-scatter.5.cloned.1.call-update) | async-done | bytes 65552 | tf_op jit(solution)/shard_map/reduce_scatter | solution.py:112
  726.1 3.3 fusion.2
  729.4 2.9 fusion.4
  732.4 1.0 copy.112
  733.4 141.9 %reduce-scatter.7.cloned.1.call-done = f32[32,8]{1,0:T(8,128)} async-done(((f32[1024,8]{1,0:T(8,128)}), f32[32,8]{1,0:T(8,128)}) %reduce-scatter.7.cloned.1.call-update) | async-done | bytes 1040
  875.3 1.4 copy.113
  (52 shorter events, 0.4 us)
Async XLA Ops:
  7.2 55.0 %all-gather.2.cloned.1.call-start = ((), (), s32[]{:S(2)}) async-start(), calls=%async_computation.2 | async-start | bytes 2359296 | tf_op jit(solution)/shard_map/all_gather | solution.py:91
  9.0 717.1 %reduce-scatter.5.cloned.1.call-start = ((), (), s32[]{:S(2)}) async-start(), calls=%async_computation.3 | async-start | bytes 34603008 | tf_op jit(solution)/shard_map/reduce_scatter | solution.py:112
  93.0 16.9 %copy-start.3 = (s32[4096]{0:T(1024)S(1)}, s32[4096]{0:T(1024)}, u32[]{:S(2)}) copy-start(s32[4096]{0:T(1024)} %broadcast_clamp_fusion) | copy-start | bytes 49156
  93.0 38.9 %copy-start.5 = (s32[4096]{0:T(1024)S(1)}, s32[4096]{0:T(1024)}, u32[]{:S(2)}) copy-start(s32[4096]{0:T(1024)} %broadcast_clamp_fusion.1) | copy-start | bytes 49156
  109.9 65.3 %copy-start.4 = (s32[4096]{0:T(1024)S(1)}, s32[4096]{0:T(1024)}, u32[]{:S(2)}) copy-start(s32[4096]{0:T(1024)} %broadcast_clamp_fusion.3) | copy-start | bytes 49156
  153.2 49.6 %copy-start.17 = (pred[4096]{0:T(1024)(128)(4,1)S(1)}, pred[4096]{0:T(1024)(128)(4,1)}, u32[]{:S(2)}) copy-start(pred[4096]{0:T(1024)(128)(4,1)} %compare_and_fusion.2) | copy-start | bytes 12292
  153.2 49.6 %copy-start.18 = (pred[4096]{0:T(1024)(128)(4,1)S(1)}, pred[4096]{0:T(1024)(128)(4,1)}, u32[]{:S(2)}) copy-start(pred[4096]{0:T(1024)(128)(4,1)} %compare_and_fusion.3) | copy-start | bytes 12292
  153.9 49.0 %copy-start.1 = (f32[3,4096]{1,0:T(4,128)S(1)}, f32[3,4096]{1,0:T(4,128)}, u32[]{:S(2)}) copy-start(f32[3,4096]{1,0:T(4,128)} %param.15) | copy-start | bytes 147460
  153.9 49.6 %copy-start.15 = (pred[4096]{0:T(1024)(128)(4,1)S(1)}, pred[4096]{0:T(1024)(128)(4,1)}, u32[]{:S(2)}) copy-start(pred[4096]{0:T(1024)(128)(4,1)} %compare_and_fusion) | copy-start | bytes 12292
  153.9 49.6 %copy-start.16 = (pred[4096]{0:T(1024)(128)(4,1)S(1)}, pred[4096]{0:T(1024)(128)(4,1)}, u32[]{:S(2)}) copy-start(pred[4096]{0:T(1024)(128)(4,1)} %compare_and_fusion.1) | copy-start | bytes 12292
  199.9 4.3 copy-start.13
  199.9 4.3 copy-start.14
  200.0 4.7 copy-start.11
  200.0 4.7 copy-start.12
  204.5 5.0 copy-start.9
  204.5 5.0 copy-start.10
  209.8 37.9 %copy-start.2 = (f32[8,4096]{1,0:T(8,128)}, f32[8,4096]{1,0:T(8,128)S(1)}, u32[]{:S(2)}) copy-start(f32[8,4096]{1,0:T(8,128)S(1)} %pad_maximum_fusion) | copy-start | bytes 393220
  211.7 36.0 %copy-start.8 = (s32[4096,1]{0,1:T(1,128)S(1)}, s32[4096,1]{0,1:T(1,128)}, u32[]{:S(2)}) copy-start(s32[4096,1]{0,1:T(1,128)} %get-tuple-element.59) | copy-start | bytes 49156
  211.7 78.0 %copy-start.7 = (s32[4096,1]{0,1:T(1,128)S(1)}, s32[4096,1]{0,1:T(1,128)}, u32[]{:S(2)}) copy-start(s32[4096,1]{0,1:T(1,128)} %get-tuple-element.60) | copy-start | bytes 49156
  247.7 83.7 %copy-start.6 = (s32[4096,1]{0,1:T(1,128)S(1)}, s32[4096,1]{0,1:T(1,128)}, u32[]{:S(2)}) copy-start(s32[4096,1]{0,1:T(1,128)} %get-tuple-element.58) | copy-start | bytes 49156
  373.4 501.9 %reduce-scatter.7.cloned.1.call-start = ((), (), s32[]{:S(2)}) async-start(), calls=%async_computation.4 | async-start | bytes 540672
  726.1 3.3 copy-start
Sparse Core Ops, SparseCore 0:
  10.1 51.9 all-gather.1
  373.6 352.5 reduce-scatter.4
  733.5 141.7 reduce-scatter.6
where the time goes:
time: 884 us; the launch traced here: 883 us
  waiting for transfers between devices  535 us (61%)
  other arithmetic  196 us (22%)
  local copies, waits for them, and re-layouts  131 us (15%)
  between operations  14.1 us (2%)
    reduce_scatter x1, waiting for transfers between devices, body(): lax.psum_scatter(facet_sums, ('dom', 'bin'), scatter_dimension=1, tiled=T...  353 us
    scatter-add x4, other arithmetic, body(): facet_sums = facet_sums.at[:, global_facet].add(tube_field)  162 us
    unnamed x4, waiting for transfers between devices  142 us
    gather x8, local copies, waits for them, and re-layouts, body(): facet_rows = jnp.take(frame_all, global_facet, axis=1)  92.8 us
    all_gather x1, waiting for transfers between devices, body(): lax.all_gather(jnp.stack([facet_polar, facet_azimuth, facet_tilt, surface...  40.8 us
    sin x1, other arithmetic, facet_frame(): jnp.sin(tilt_angle)  24.4 us
    another operation x2, local copies, waits for them, and re-layouts, facet_frame(): jnp.stack([jnp.sin(polar_angle) * jnp.cos(azimuth), jnp.sin(polar_angle)...  21.5 us
  transfers between devices with their start and end apart: 3, of which 3 were waited for; matrix products, arithmetic and copies ran while one was open for 1% of the time, Pallas kernels for 0%

commit v1 on v0

v1 whole, which is shorter than its diff:
```python
import functools

import jax
import jax.numpy as jnp
from jax import lax
from jax.experimental import pallas as pl
from jax.experimental.pallas import tpu as pltpu
from jax.sharding import PartitionSpec as P

BOUNCES = 4
LANES = 128
VALUES = 8
GROUPS = LANES // VALUES
VMEM = pl.BlockSpec(memory_space=pltpu.VMEM)
SMEM = pl.BlockSpec(memory_space=pltpu.SMEM)
ANY = pl.BlockSpec(memory_space=pl.ANY)
F32 = jnp.float32


def bits_of(count):
    assert count & (count - 1) == 0
    return count.bit_length() - 1


def sum_phases(bits):
    phases = [[0]]
    rest = list(range(1, bits))
    while rest:
        phases.append(rest[:2])
        rest = rest[2:]
    return phases


def spread(digit, phase):
    return sum(((digit >> place) & 1) << bit for place, bit in enumerate(phase))


def place_of(offset, phases):
    place = 0
    for phase in phases:
        for bit in reversed(phase):
            place = place * 2 + ((offset >> bit) & 1)
    return place


def send(value, mask, axes, count):
    return lax.ppermute(value, axes, [(i, i ^ mask) for i in range(count)])


def sine_cosine(angle):
    turns = jnp.floor(angle * 0.6366197723675814 + 0.5)
    rest = angle - turns * 1.5703125
    rest = rest - turns * 4.837512969970703e-4
    rest = rest - turns * 7.54978995489188e-8
    square = rest * rest
    sine = rest + rest * square * (
        -1.6666654611e-1 + square * (8.3321608736e-3 - square * 1.9515295891e-4)
    )
    cosine = 1.0 - 0.5 * square + square * square * (
        4.166664568298827e-2 + square * (-1.388731625493765e-3 + square * 2.443315711809948e-5)
    )
    quarter = turns.astype(jnp.int32)
    odd = (quarter & 1) == 1
    first = jnp.where(odd, cosine, sine)
    second = jnp.where(odd, sine, cosine)
    return (
        jnp.where((quarter & 2) == 2, -first, first),
        jnp.where(((quarter + 1) & 2) == 2, -second, second),
    )


def divide(top_real, top_imag, low_real, low_imag):
    scale = 1.0 / (low_real * low_real + low_imag * low_imag)
    return (
        (top_real * low_real + top_imag * low_imag) * scale,
        (top_imag * low_real - top_real * low_imag) * scale,
    )


def bounce_once(field, heading, facet, phase):
    sine, cosine = sine_cosine(phase)
    real = [cosine * field[i] - sine * field[4 + i] for i in range(4)]
    imag = [sine * field[i] + cosine * field[4 + i] for i in range(4)]
    normal = facet[0:3]
    eta_real, eta_imag, tilt_cos, tilt_sin = facet[3:7]
    incidence = heading[0] * normal[0] + heading[1] * normal[1] + heading[2] * normal[2]
    slant = jnp.abs(incidence)
    te_real, te_imag = divide(slant - eta_real, -eta_imag, slant + eta_real, eta_imag)
    tm_real, tm_imag = divide(
        eta_real * slant - 1.0, eta_imag * slant, eta_real * slant + 1.0, eta_imag * slant
    )
    out_real, out_imag = [None] * 4, [None] * 4
    for i in range(2):
        upper_real = tilt_cos * real[i] + tilt_sin * real[2 + i]
        lower_real = tilt_cos * real[2 + i] - tilt_sin * real[i]
        upper_imag = tilt_cos * imag[i] + tilt_sin * imag[2 + i]
        lower_imag = tilt_cos * imag[2 + i] - tilt_sin * imag[i]
        out_real[i] = te_real * upper_real - te_imag * upper_imag
        out_real[2 + i] = tm_real * lower_real - tm_imag * lower_imag
        out_imag[i] = te_real * upper_imag + te_imag * upper_real
        out_imag[2 + i] = tm_real * lower_imag + tm_imag * lower_real
    twice = 2.0 * incidence
    return out_real + out_imag, [heading[k] - twice * normal[k] for k in range(3)]


def trace_kernel(meta, *refs):
    (tubes, pieces, piece_rows, bins, depth, phases, parts, copies, axes) = meta
    rows_ref, group_ref, phase_ref, field_ref, heading_ref = refs[:5]
    piece_refs = refs[5 : 5 + pieces]
    part_refs = refs[5 + pieces : 5 + pieces + parts]
    exit_ref = refs[5 + pieces + parts]
    scratch = refs[6 + pieces + parts :]
    table, frame, wide, turn, flat, arrive, leave = scratch[:7]
    sums = scratch[7:]
    blocks = tubes // LANES
    total = sums[0].shape[0]

    loads = [
        pltpu.make_async_copy(piece_refs[i], table.at[i], arrive.at[i]) for i in range(pieces)
    ]
    for load in loads:
        load.start()

    clear = 256
    zeros = jnp.zeros((clear, LANES), F32)

    def wipe(i, carry):
        for ref in sums:
            ref[pl.ds(pl.multiple_of(i * clear, clear), clear), :] = zeros
        return carry

    lax.fori_loop(0, total // clear, wipe, 0)
    for load in loads:
        load.wait()

    me = lax.axis_index(axes[1])
    low = me & 1
    quarters = bins // 2
    per_quarter = piece_rows // quarters
    steps = depth // LANES

    def build(i, carry):
        polar, azimuth, tilt = table[i, 0], table[i, 1], table[i, 2]
        polar_sin, polar_cos = sine_cosine(polar)
        azimuth_sin, azimuth_cos = sine_cosine(azimuth)
        tilt_sin, tilt_cos = sine_cosine(tilt)
        values = [
            polar_sin * azimuth_cos,
            polar_sin * azimuth_sin,
            polar_cos,
            table[i, 3],
            table[i, 4],
            tilt_cos,
            tilt_sin,
            tilt_sin,
        ]
        for k in range(VALUES):
            frame[k * piece_rows : (k + 1) * piece_rows, :] = values[k]
        half = (i & 1) ^ low
        for quarter in range(quarters):
            owner = half * quarters + quarter
            place = place_of((i >> 1) * bins + (owner ^ me), phases)
            for m in range(steps):
                tall = jnp.concatenate(
                    [
                        frame[
                            pl.ds(quarter * per_quarter + j * steps + m, VALUES, stride=piece_rows),
                            :,
                        ]
                        for j in range(GROUPS)
                    ],
                    axis=0,
                )
                at = pl.multiple_of(place * depth + m * LANES, LANES)
                flat[pl.ds(at, LANES), :] = tall.T
        return carry

    lax.fori_loop(0, pieces, build, 0)

    unroll = 32

    def fetch(i, carry):
        for u in range(unroll):
            hit = i * unroll + u
            wide[pl.ds(hit, 1), :] = flat[pl.ds(rows_ref[hit], 1), :]
        return carry

    lax.fori_loop(0, BOUNCES * tubes // unroll, fetch, 0)

    def spread_in(ref, count):
        for k in range(blocks):
            turn[k * VALUES : k * VALUES + count, :] = ref[:, k * LANES : (k + 1) * LANES]
        return [turn[pl.ds(c, blocks, stride=VALUES), :] for c in range(count)]

    field = spread_in(field_ref, 8)
    heading = spread_in(heading_ref, 3)
    for bounce in range(BOUNCES):

        def pick(k, carry, bounce=bounce):
            at = pl.multiple_of((bounce * blocks + k) * LANES, LANES)
            tall = wide[pl.ds(at, LANES), :].T.reshape(GROUPS, VALUES, LANES)
            group = group_ref[bounce, pl.ds(k, 1), :]
            left = [tall[j] for j in range(GROUPS)]
            level = 0
            while len(left) > 1:
                odd = jnp.broadcast_to((group >> level) & 1, (VALUES, LANES)) == 1
                left = [jnp.where(odd, left[2 * n + 1], left[2 * n]) for n in range(len(left) // 2)]
                level += 1
            turn[pl.ds(pl.multiple_of(k * VALUES, VALUES), VALUES), :] = left[0]
            return carry

        lax.fori_loop(0, blocks, pick, 0)
        facet = [turn[pl.ds(c, blocks, stride=VALUES), :] for c in range(7)]
        field, heading = bounce_once(field, heading, facet, phase_ref[bounce])
        for c in range(VALUES):
            turn[c * blocks : (c + 1) * blocks, :] = field[c]

        def widen(k, carry, bounce=bounce):
            at = pl.multiple_of((bounce * blocks + k) * LANES, LANES)
            own = turn[pl.ds(k, VALUES, stride=blocks), :]
            group = jnp.broadcast_to(group_ref[bounce, pl.ds(k, 1), :], (VALUES, LANES))
            tall = jnp.concatenate([jnp.where(group == j, own, 0.0) for j in range(GROUPS)], axis=0)
            wide[pl.ds(at, LANES), :] = tall.T
            if bounce == BOUNCES - 1:
                exit_ref[:, pl.ds(pl.multiple_of(k * LANES, LANES), LANES)] = own
            return carry

        lax.fori_loop(0, blocks, widen, 0)

    share = BOUNCES * tubes // copies
    inner = 32 // copies

    def add(i, carry):
        for u in range(inner):
            fresh = []
            for c in range(copies):
                hit = c * share + i * inner + u
                row = rows_ref[hit]
                fresh.append((row, sums[c][pl.ds(row, 1), :] + wide[pl.ds(hit, 1), :]))
            for c in range(copies):
                sums[c][pl.ds(fresh[c][0], 1), :] = fresh[c][1]
        return carry

    lax.fori_loop(0, share // inner, add, 0)

    size = total // parts
    outs = []
    for part in range(parts):

        def merge(i, carry, part=part):
            at = pl.ds(pl.multiple_of(part * size + i * LANES, LANES), LANES)
            sums[0][at, :] = functools.reduce(lambda a, b: a + b, [ref[at, :] for ref in sums])
            return carry

        if copies > 1:
            lax.fori_loop(0, size // LANES, merge, 0)
        outs.append(
            pltpu.make_async_copy(
                sums[0].at[pl.ds(part * size, size), :], part_refs[part], leave.at[part]
            )
        )
        outs[-1].start()
    for out in outs:
        out.wait()


def field_kernel(meta, *refs):
    (terms, tiles, low_bits, axes) = meta
    kernel_ref = refs[terms]
    outs = refs[terms + 1 : terms + 1 + tiles]
    (held,) = refs[terms + 1 + tiles :]
    total = functools.reduce(lambda a, b: a + b, [ref[...] for ref in refs[:terms]])
    depth = total.shape[0]
    rounded = []
    tall = [
        total[m * LANES : (m + 1) * LANES, :].T.reshape(GROUPS, VALUES, LANES)
        for m in range(depth // LANES)
    ]
    for j in range(GROUPS):
        for m in range(depth // LANES):
            rounded.append(tall[m][j])
    left = jnp.concatenate(rounded, axis=1).astype(jnp.bfloat16)
    real = jnp.dot(left, kernel_ref[0], preferred_element_type=F32)
    imag = jnp.dot(left, kernel_ref[1], preferred_element_type=F32)
    far = jnp.concatenate([real[0:4] - imag[4:8], imag[0:4] + real[4:8]], axis=0)
    width = far.shape[1] // tiles
    for t in range(tiles):
        held[t] = far[:, t * width : (t + 1) * width]
    me = lax.axis_index(axes) >> low_bits
    for t in range(tiles):
        outs[t][...] = held[me ^ t]


def body(
    axes,
    sizes,
    field_in,
    heading_in,
    launch_domain,
    hop_domain,
    hit_facet,
    path_phase,
    facet_polar,
    facet_azimuth,
    facet_tilt,
    surface_resistance,
    surface_reactance,
    kernel,
):
    domains, bins = sizes
    count = domains * bins
    phases = sum_phases(bits_of(count))
    me = lax.axis_index(axes)
    low = lax.axis_index(axes[1]) & 1
    tubes = field_in.shape[1]
    facets = facet_polar.shape[0]
    owned = kernel.shape[1]
    depth = owned // GROUPS
    blocks = tubes // LANES
    total = count * depth

    rows = facets // LANES
    half = rows // 2
    mine = jnp.stack(
        [facet_polar, facet_azimuth, facet_tilt, surface_resistance, surface_reactance], axis=0
    ).reshape(5, rows, LANES)
    near = lax.dynamic_slice_in_dim(mine, low * half, half, 1)
    far = lax.dynamic_slice_in_dim(mine, (1 - low) * half, half, 1)
    held = [near]
    bit = 0
    while bit < bits_of(domains):
        span = min(3, bits_of(domains) - bit)
        held = [
            piece if e == 0 else send(piece, (e << bit), axes[0], domains)
            for e in range(1 << span)
            for piece in held
        ]
        bit += span
    pieces = []
    for e, piece in enumerate(held):
        pieces += [piece, far if e == 0 else send(piece, 1, axes[1], bins)]

    domain = jnp.concatenate([launch_domain.reshape(1, tubes), hop_domain.reshape(BOUNCES - 1, tubes)])
    owner = domain * bins + hit_facet // owned
    within = hit_facet % owned
    place = place_of(owner ^ me, phases)
    hit_rows = (place * depth + within % depth).reshape(BOUNCES * tubes)
    hit_groups = (within // depth).reshape(BOUNCES, blocks, LANES)
    phase = path_phase.reshape(BOUNCES, blocks, LANES)

    parts = 1 << len(phases[0])
    copies = 1
    while copies < 8 and copies * 2 * total * LANES * 4 <= 16 * 2**20:
        copies *= 2
    meta = (tubes, len(pieces), half, bins, depth, phases, parts, copies, axes)
    *sums, exit_field = pl.pallas_call(
        functools.partial(trace_kernel, meta),
        out_shape=[jax.ShapeDtypeStruct((total // parts, LANES), F32)] * parts
        + [jax.ShapeDtypeStruct((8, tubes), F32)],
        in_specs=[SMEM, VMEM, VMEM, VMEM, VMEM] + [ANY] * len(pieces),
        out_specs=[ANY] * parts + [VMEM],
        scratch_shapes=[
            pltpu.VMEM((len(pieces), 5, half, LANES), F32),
            pltpu.VMEM((VALUES * half, LANES), F32),
            pltpu.VMEM((BOUNCES * tubes, LANES), F32),
            pltpu.VMEM((VALUES * blocks, LANES), F32),
            pltpu.VMEM((total, LANES), F32),
            pltpu.SemaphoreType.DMA((len(pieces),)),
            pltpu.SemaphoreType.DMA((parts,)),
        ]
        + [pltpu.VMEM((total, LANES), F32)] * copies,
        compiler_params=pltpu.CompilerParams(vmem_limit_bytes=60 * 2**20),
    )(hit_rows, hit_groups, phase, field_in, heading_in, *pieces)

    for n, phase_bits in enumerate(phases):
        terms = [sums[0]] + [
            send(sums[d], spread(d, phase_bits), axes, count) for d in range(1, len(sums))
        ]
        if n + 1 < len(phases):
            parts = 1 << len(phases[n + 1])
            size = terms[0].shape[0] // parts
            sums = [
                functools.reduce(lambda a, b: a + b, [t[p * size : (p + 1) * size] for t in terms])
                for p in range(parts)
            ]

    columns = kernel.shape[2]
    tiles = columns // LANES
    low_bits = bits_of(count) - bits_of(tiles)
    partial = pl.pallas_call(
        functools.partial(field_kernel, (len(terms), tiles, low_bits, axes)),
        out_shape=[jax.ShapeDtypeStruct((8, LANES), F32)] * tiles,
        in_specs=[VMEM] * (len(terms) + 1),
        out_specs=[VMEM] * tiles,
        scratch_shapes=[pltpu.VMEM((tiles, 8, LANES), F32)],
        compiler_params=pltpu.CompilerParams(vmem_limit_bytes=40 * 2**20),
    )(*terms, kernel)
    tile = functools.reduce(
        lambda a, b: a + b,
        [partial[0]] + [send(partial[e], e << low_bits, axes, count) for e in range(1, tiles)],
    )
    bit = 0
    while bit < low_bits:
        span = min(2, low_bits - bit)
        tile = functools.reduce(
            lambda a, b: a + b,
            [tile] + [send(tile, e << bit, axes, count) for e in range(1, 1 << span)],
        )
        bit += span
    width = columns // count
    far_field = lax.dynamic_slice_in_dim(tile, (me & ((1 << low_bits) - 1)) * width, width, 1)
    return far_field, exit_field


def solution(mesh):
    both = ("dom", "bin")
    in_specs = (
        P(None, both),
        P(None, both),
        P(both, None),
        P(None, both, None),
        P(None, both),
        P(None, both),
        P("dom"),
        P("dom"),
        P("dom"),
        P("dom"),
        P("dom"),
        P(None, both, None),
    )
    out_specs = (P(None, both), P(None, both))
    sizes = (mesh.shape["dom"], mesh.shape["bin"])
    return jax.shard_map(
        functools.partial(body, both, sizes),
        mesh=mesh,
        in_specs=in_specs,
        out_specs=out_specs,
        check_vma=False,
    )
```

time: 884 us -> 154 us (0.17)
  waiting for transfers between devices: 535 us -> 28.1 us
  other arithmetic: 196 us -> 2.56 us
  local copies, waits for them, and re-layouts: 131 us -> 12.7 us
  Pallas kernels: 0 us -> 69.2 us
  starting transfers between devices: 0.12 us -> 39.4 us
  between operations: 14.1 us -> 0.86 us
    reduce_scatter x1 -> x0, waiting for transfers between devices: 353 us -> none  [body(): lax.psum_scatter(facet_sums, ('dom', 'bin'), scatter_dimension=1, tiled=T...]
    scatter-add x4 -> x0, other arithmetic: 162 us -> none  [body(): facet_sums = facet_sums.at[:, global_facet].add(tube_field)]
    unnamed x4 -> x0, waiting for transfers between devices: 142 us -> none
    gather x8 -> x0, local copies, waits for them, and re-layouts: 92.8 us -> none  [body(): facet_rows = jnp.take(frame_all, global_facet, axis=1)]
    pallas_call x0 -> x2, Pallas kernels: none -> 69.2 us  [the longest x1 68 us: body(): pl.pallas_call(functools.partial(trace_kernel, meta), out_shape=[jax.Shap...]
    all_gather x1 -> x0, waiting for transfers between devices: 40.8 us -> none  [body(): lax.all_gather(jnp.stack([facet_polar, facet_azimuth, facet_tilt, surface...]
    ppermute x0 -> x31, starting transfers between devices: none -> 39.4 us  [send(): return lax.ppermute(value, axes, [(i, i ^ mask) for i in range(count)])]
    ppermute x0 -> x31, waiting for transfers between devices: none -> 28.1 us  [send(): return lax.ppermute(value, axes, [(i, i ^ mask) for i in range(count)])]
  transfers between devices with their start and end apart: 3 -> 31, of which waited for: 3 -> 11; matrix products, arithmetic and copies ran while one was open for 1% -> 3% of each run, Pallas kernels for 0% -> 0%
where the time goes in v1:
time: 154 us; the launch traced here: 153 us
  Pallas kernels  69.2 us (45%)
  starting transfers between devices  39.4 us (26%)
  waiting for transfers between devices  28.1 us (18%)
  local copies, waits for them, and re-layouts  12.7 us (8%)
  other arithmetic  2.56 us (2%)
    pallas_call x1, Pallas kernels, body(): pl.pallas_call(functools.partial(trace_kernel, meta), out_shape=[jax.Shap...  68 us
    ppermute x31, starting transfers between devices, send(): return lax.ppermute(value, axes, [(i, i ^ mask) for i in range(count)])  39.4 us
    ppermute x31, waiting for transfers between devices, send(): return lax.ppermute(value, axes, [(i, i ^ mask) for i in range(count)])  28.1 us
    unnamed x40, local copies, waits for them, and re-layouts  10.6 us
  transfers between devices with their start and end apart: 31, of which 11 were waited for; matrix products, arithmetic and copies ran while one was open for 3% of the time, Pallas kernels for 0%

profile of v1, /device:TPU:0, one launch (start us, length us, event | category | flops | bytes accessed | tf_op | source)
XLA Modules:
  0.0 152.9 jit_solution(2261273717527101187)
XLA Ops:
  0.6 0.8 bitcast_dynamic-update-slice_fusion.4
  1.4 0.8 bitcast_dynamic-update-slice_fusion.3
  2.2 0.8 bitcast_dynamic-update-slice_fusion.2
  2.9 0.8 bitcast_dynamic-update-slice_fusion.1
  3.7 0.8 bitcast_dynamic-update-slice_fusion
  4.4 0.6 constant_dynamic-slice_fusion.1
  5.1 6.0 %collective-permute-start.12 = (f32[5,32,128]{2,1,0:T(8,128)S(1)}, f32[5,32,128]{2,1,0:T(8,128)S(1)}, u32[]{:S(2)}, u32[]{:S(2)}) collective-permute-start(f32[5,32,128]{2,1,0:T(8,128)S(1)} %get-tuple-element.33.refs_5_), channel_id=1, source_target_pairs={{0,28},{4,24},{8,20},{12,16},{16,12},{20,8},{24,4},{28,0},{1,29},{... | collective-permute-start | bytes 245768 | tf_op jit(solution)/shard_map/ppermute | solution.py:47
  11.1 0.2 collective-permute-start.10
  11.3 0.7 collective-permute-start.8
  12.1 2.0 %collective-permute-start.6 = (f32[5,32,128]{2,1,0:T(8,128)S(1)}, f32[5,32,128]{2,1,0:T(8,128)S(1)}, u32[]{:S(2)}, u32[]{:S(2)}) collective-permute-start(f32[5,32,128]{2,1,0:T(8,128)S(1)} %get-tuple-element.33.refs_5_), channel_id=1, source_target_pairs={{0,16},{4,20},{8,24},{12,28},{16,0},{20,4},{24,8},{28,12},{1,17},{... | collective-permute-start | bytes 245768 | tf_op jit(solution)/shard_map/ppermute | solution.py:47
  14.0 2.4 %collective-permute-start.4 = (f32[5,32,128]{2,1,0:T(8,128)S(1)}, f32[5,32,128]{2,1,0:T(8,128)S(1)}, u32[]{:S(2)}, u32[]{:S(2)}) collective-permute-start(f32[5,32,128]{2,1,0:T(8,128)S(1)} %get-tuple-element.33.refs_5_), channel_id=1, source_target_pairs={{0,12},{4,8},{8,4},{12,0},{16,28},{20,24},{24,20},{28,16},{1,13},{... | collective-permute-start | bytes 245768 | tf_op jit(solution)/shard_map/ppermute | solution.py:47
  16.4 0.0 collective-permute-done.12.refs_19_
  16.4 3.8 %collective-permute-start.2 = (f32[5,32,128]{2,1,0:T(8,128)S(1)}, f32[5,32,128]{2,1,0:T(8,128)S(1)}, u32[]{:S(2)}, u32[]{:S(2)}) collective-permute-start(f32[5,32,128]{2,1,0:T(8,128)S(1)} %get-tuple-element.33.refs_5_), channel_id=1, source_target_pairs={{0,8},{4,12},{8,0},{12,4},{16,24},{20,28},{24,16},{28,20},{1,9},{5... | collective-permute-start | bytes 245768 | tf_op jit(solution)/shard_map/ppermute | solution.py:47
  20.2 0.0 collective-permute-done.10.refs_17_
  20.2 1.4 collective-permute-start
  21.7 2.5 %collective-permute-done.8.refs_15_ = f32[5,32,128]{2,1,0:T(8,128)S(1)} collective-permute-done((f32[5,32,128]{2,1,0:T(8,128)S(1)}, f32[5,32,128]{2,1,0:T(8,128)S(1)}, u32[]{:S(2)}, u32[]{:S(2)}) %collective-permute-start.8) | collective-permute-done | bytes 81952 | tf_op jit(solution)/shard_map/ppermute | solution.py:47
  24.2 0.0 collective-permute-start.13
  24.2 0.9 collective-permute-done.6.refs_13_
  25.1 0.9 copy.23
  26.0 0.5 collective-permute-start.9
  26.5 0.1 collective-permute-start.7
  26.6 0.4 collective-permute-start.5
  27.0 0.1 collective-permute-start.3
  27.1 0.4 collective-permute-start.1
  27.6 1.2 fusion.4
  28.7 0.6 copy.22
  29.4 0.6 copy.15
  30.0 1.5 copy.21
  31.6 0.5 copy-done.11
  32.1 0.0 copy-done.12
  32.1 0.0 copy-done.13
  32.2 0.0 copy-done.14
  32.2 0.0 copy-done.15
  32.2 68.0 %shard_map.131 = (f32[2048,128]{1,0:T(8,128)}, f32[2048,128]{1,0:T(8,128)}, f32[8,4096]{1,0:T(8,128)}) custom-call(s32[16384]{0:T(1024)} %bitcast.28, s32[4,32,128]{2,1,0:T(8,128)} %bitcast.27, f32[4,32,128]{2,1,0:T(8,128)} %bitcast.29, f32[8,4096]{1,0:T(8,128)} %refs_3_.1, f32[3,4096]{1,0:T(4,128)} %refs_4_.2, f32[5,32,128]{2,1,0:T(8,128)} %copy-done.1, ...), custom_call_target="tpu_custom_call" | custom-call | tf_op jit(solution)/shard_map/pallas_call | solution.py:356
  100.2 0.2 collective-permute-start.14
  100.4 2.8 %collective-permute-done.14 = f32[2048,128]{1,0:T(8,128)S(1)} collective-permute-done((f32[2048,128]{1,0:T(8,128)}, f32[2048,128]{1,0:T(8,128)S(1)}, u32[]{:S(2)}, u32[]{:S(2)}) %collective-permute-start.14) | collective-permute-done | bytes 1048608 | tf_op jit(solution)/shard_map/ppermute | solution.py:47
  103.1 1.3 slice_add_fusion.3
  104.4 1.7 %collective-permute-start.17 = (f32[512,128]{1,0:T(8,128)S(1)}, f32[512,128]{1,0:T(8,128)S(1)}, u32[]{:S(2)}, u32[]{:S(2)}) collective-permute-start(f32[512,128]{1,0:T(8,128)S(1)} %get-tuple-element.25), channel_id=1, source_target_pairs={{0,6},{1,7},{2,4},{3,5},{4,2},{5,3},{6,0},{7,1},{8,14},{9,15},{10,... | collective-permute-start | bytes 786440 | tf_op jit(solution)/shard_map/ppermute | solution.py:47
  106.2 1.3 collective-permute-start.16
  107.5 0.5 collective-permute-start.15
  108.0 6.6 %collective-permute-done.17 = f32[512,128]{1,0:T(8,128)S(1)} collective-permute-done((f32[512,128]{1,0:T(8,128)S(1)}, f32[512,128]{1,0:T(8,128)S(1)}, u32[]{:S(2)}, u32[]{:S(2)}) %collective-permute-start.17) | collective-permute-done | bytes 262176 | tf_op jit(solution)/shard_map/ppermute | solution.py:47
  114.6 4.8 %collective-permute-done.16 = f32[512,128]{1,0:T(8,128)S(1)} collective-permute-done((f32[512,128]{1,0:T(8,128)S(1)}, f32[512,128]{1,0:T(8,128)S(1)}, u32[]{:S(2)}, u32[]{:S(2)}) %collective-permute-start.16) | collective-permute-done | bytes 262176 | tf_op jit(solution)/shard_map/ppermute | solution.py:47
  119.4 0.1 slice_add_fusion.4
  119.4 2.5 %collective-permute-start.20 = (f32[128,128]{1,0:T(8,128)S(1)}, f32[128,128]{1,0:T(8,128)S(1)}, u32[]{:S(2)}, u32[]{:S(2)}) collective-permute-start(f32[128,128]{1,0:T(8,128)S(1)} %get-tuple-element.28), channel_id=1, source_target_pairs={{0,24},{1,25},{2,26},{3,27},{4,28},{5,29},{6,30},{7,31},{8,16},{9,... | collective-permute-start | bytes 196616 | tf_op jit(solution)/shard_map/ppermute | solution.py:47
  122.0 1.9 %collective-permute-start.18 = (f32[128,128]{1,0:T(8,128)S(1)}, f32[128,128]{1,0:T(8,128)S(1)}, u32[]{:S(2)}, u32[]{:S(2)}) collective-permute-start(f32[128,128]{1,0:T(8,128)S(1)} %get-tuple-element.30), channel_id=1, source_target_pairs={{0,8},{1,9},{2,10},{3,11},{4,12},{5,13},{6,14},{7,15},{8,0},{9,1},... | collective-permute-start | bytes 196616 | tf_op jit(solution)/shard_map/ppermute | solution.py:47
  123.9 2.3 %collective-permute-done.20.refs_3_ = f32[128,128]{1,0:T(8,128)S(1)} collective-permute-done((f32[128,128]{1,0:T(8,128)S(1)}, f32[128,128]{1,0:T(8,128)S(1)}, u32[]{:S(2)}, u32[]{:S(2)}) %collective-permute-start.20) | collective-permute-done | bytes 65568 | tf_op jit(solution)/shard_map/ppermute | solution.py:47
  126.2 2.0 %collective-permute-done.19.refs_2_ = f32[128,128]{1,0:T(8,128)S(1)} collective-permute-done((f32[128,128]{1,0:T(8,128)S(1)}, f32[128,128]{1,0:T(8,128)S(1)}, u32[]{:S(2)}, u32[]{:S(2)}) %collective-permute-start.19) | collective-permute-done | bytes 65568 | tf_op jit(solution)/shard_map/ppermute | solution.py:47
  128.2 3.4 %copy-done = bf16[2,2048,1024]{2,1,0:T(8,128)(2,1)S(1)} copy-done((bf16[2,2048,1024]{2,1,0:T(8,128)(2,1)S(1)}, bf16[2,2048,1024]{2,1,0:T(8,128)(2,1)}, u32[]{:S(2)}) %copy-start) | copy-done | bytes 8388632
  131.6 1.2 shard_map.132
  132.9 0.9 collective-permute-start.21
  133.8 0.7 collective-permute-start.22
  134.5 1.9 %collective-permute-start.23 = (f32[8,128]{1,0:T(8,128)S(1)}, f32[8,128]{1,0:T(8,128)S(1)}, u32[]{:S(2)}, u32[]{:S(2)}) collective-permute-start(f32[8,128]{1,0:T(8,128)S(1)} %get-tuple-element.18), channel_id=1, source_target_pairs={{0,12},{1,13},{2,14},{3,15},{4,8},{5,9},{6,10},{7,11},{8,4},{9,5},... | collective-permute-start | bytes 12296 | tf_op jit(solution)/shard_map/ppermute | solution.py:47
  136.4 1.2 collective-permute-start.24
  137.6 2.0 %collective-permute-start.25 = (f32[8,128]{1,0:T(8,128)S(1)}, f32[8,128]{1,0:T(8,128)S(1)}, u32[]{:S(2)}, u32[]{:S(2)}) collective-permute-start(f32[8,128]{1,0:T(8,128)S(1)} %get-tuple-element.20), channel_id=1, source_target_pairs={{0,20},{1,21},{2,22},{3,23},{4,16},{5,17},{6,18},{7,19},{8,28},{9,... | collective-permute-start | bytes 12296 | tf_op jit(solution)/shard_map/ppermute | solution.py:47
  139.6 2.5 %collective-permute-start.26 = (f32[8,128]{1,0:T(8,128)S(1)}, f32[8,128]{1,0:T(8,128)S(1)}, u32[]{:S(2)}, u32[]{:S(2)}) collective-permute-start(f32[8,128]{1,0:T(8,128)S(1)} %get-tuple-element.21), channel_id=1, source_target_pairs={{0,24},{1,25},{2,26},{3,27},{4,28},{5,29},{6,30},{7,31},{8,16},{9,... | collective-permute-start | bytes 12296 | tf_op jit(solution)/shard_map/ppermute | solution.py:47
  142.1 2.0 %collective-permute-start.27 = (f32[8,128]{1,0:T(8,128)S(1)}, f32[8,128]{1,0:T(8,128)S(1)}, u32[]{:S(2)}, u32[]{:S(2)}) collective-permute-start(f32[8,128]{1,0:T(8,128)S(1)} %get-tuple-element.22), channel_id=1, source_target_pairs={{0,28},{1,29},{2,30},{3,31},{4,24},{5,25},{6,26},{7,27},{8,20},{9,... | collective-permute-start | bytes 12296 | tf_op jit(solution)/shard_map/ppermute | solution.py:47
  144.1 1.0 collective-permute-done.26
  145.1 3.4 %collective-permute-done.27 = f32[8,128]{1,0:T(8,128)S(1)} collective-permute-done((f32[8,128]{1,0:T(8,128)S(1)}, f32[8,128]{1,0:T(8,128)S(1)}, u32[]{:S(2)}, u32[]{:S(2)}) %collective-permute-start.27) | collective-permute-done | bytes 4128 | tf_op jit(solution)/shard_map/ppermute | solution.py:47
  148.4 0.1 collective-permute-start.30
  148.5 1.5 collective-permute-start.29
  150.0 0.4 collective-permute-start.28
  150.4 1.2 collective-permute-done.30
  151.5 0.7 collective-permute-done.29
  152.2 0.7 constant_dynamic-slice_fusion
  (48 shorter events, 0.1 us)
Async XLA Ops:
  5.1 26.5 %copy-start.1 = (f32[5,32,128]{2,1,0:T(8,128)}, f32[5,32,128]{2,1,0:T(8,128)S(1)}, u32[]{:S(2)}) copy-start(f32[5,32,128]{2,1,0:T(8,128)S(1)} %get-tuple-element.33.refs_5_) | copy-start | bytes 245764
  5.1 11.3 %collective-permute-start.12 = (f32[5,32,128]{2,1,0:T(8,128)S(1)}, f32[5,32,128]{2,1,0:T(8,128)S(1)}, u32[]{:S(2)}, u32[]{:S(2)}) collective-permute-start(f32[5,32,128]{2,1,0:T(8,128)S(1)} %get-tuple-element.33.refs_5_), channel_id=1, source_target_pairs={{0,28},{4,24},{8,20},{12,16},{16,12},{20,8},{24,4},{28,0},{1,29},{... | collective-permute-start | bytes 245768 | tf_op jit(solution)/shard_map/ppermute | solution.py:47
  11.1 9.1 %collective-permute-start.10 = (f32[5,32,128]{2,1,0:T(8,128)S(1)}, f32[5,32,128]{2,1,0:T(8,128)S(1)}, u32[]{:S(2)}, u32[]{:S(2)}) collective-permute-start(f32[5,32,128]{2,1,0:T(8,128)S(1)} %get-tuple-element.33.refs_5_), channel_id=1, source_target_pairs={{0,24},{4,28},{8,16},{12,20},{16,8},{20,12},{24,0},{28,4},{1,25},{... | collective-permute-start | bytes 245768 | tf_op jit(solution)/shard_map/ppermute | solution.py:47
  11.3 12.8 %collective-permute-start.8 = (f32[5,32,128]{2,1,0:T(8,128)S(1)}, f32[5,32,128]{2,1,0:T(8,128)S(1)}, u32[]{:S(2)}, u32[]{:S(2)}) collective-permute-start(f32[5,32,128]{2,1,0:T(8,128)S(1)} %get-tuple-element.33.refs_5_), channel_id=1, source_target_pairs={{0,20},{4,16},{8,28},{12,24},{16,4},{20,0},{24,12},{28,8},{1,21},{... | collective-permute-start | bytes 245768 | tf_op jit(solution)/shard_map/ppermute | solution.py:47
  12.1 13.0 %collective-permute-start.6 = (f32[5,32,128]{2,1,0:T(8,128)S(1)}, f32[5,32,128]{2,1,0:T(8,128)S(1)}, u32[]{:S(2)}, u32[]{:S(2)}) collective-permute-start(f32[5,32,128]{2,1,0:T(8,128)S(1)} %get-tuple-element.33.refs_5_), channel_id=1, source_target_pairs={{0,16},{4,20},{8,24},{12,28},{16,0},{20,4},{24,8},{28,12},{1,17},{... | collective-permute-start | bytes 245768 | tf_op jit(solution)/shard_map/ppermute | solution.py:47
  14.0 11.9 %collective-permute-start.4 = (f32[5,32,128]{2,1,0:T(8,128)S(1)}, f32[5,32,128]{2,1,0:T(8,128)S(1)}, u32[]{:S(2)}, u32[]{:S(2)}) collective-permute-start(f32[5,32,128]{2,1,0:T(8,128)S(1)} %get-tuple-element.33.refs_5_), channel_id=1, source_target_pairs={{0,12},{4,8},{8,4},{12,0},{16,28},{20,24},{24,20},{28,16},{1,13},{... | collective-permute-start | bytes 245768 | tf_op jit(solution)/shard_map/ppermute | solution.py:47
  16.4 15.2 %copy-start.2 = (f32[5,32,128]{2,1,0:T(8,128)}, f32[5,32,128]{2,1,0:T(8,128)S(1)}, u32[]{:S(2)}) copy-start(f32[5,32,128]{2,1,0:T(8,128)S(1)} %collective-permute-done.12.refs_19_) | copy-start | bytes 245764
  16.4 10.1 %collective-permute-start.2 = (f32[5,32,128]{2,1,0:T(8,128)S(1)}, f32[5,32,128]{2,1,0:T(8,128)S(1)}, u32[]{:S(2)}, u32[]{:S(2)}) collective-permute-start(f32[5,32,128]{2,1,0:T(8,128)S(1)} %get-tuple-element.33.refs_5_), channel_id=1, source_target_pairs={{0,8},{4,12},{8,0},{12,4},{16,24},{20,28},{24,16},{28,20},{1,9},{5... | collective-permute-start | bytes 245768 | tf_op jit(solution)/shard_map/ppermute | solution.py:47
  20.2 11.3 %copy-start.3 = (f32[5,32,128]{2,1,0:T(8,128)}, f32[5,32,128]{2,1,0:T(8,128)S(1)}, u32[]{:S(2)}) copy-start(f32[5,32,128]{2,1,0:T(8,128)S(1)} %collective-permute-done.10.refs_17_) | copy-start | bytes 245764
  20.2 6.4 %collective-permute-start = (f32[5,32,128]{2,1,0:T(8,128)S(1)}, f32[5,32,128]{2,1,0:T(8,128)S(1)}, u32[]{:S(2)}, u32[]{:S(2)}) collective-permute-start(f32[5,32,128]{2,1,0:T(8,128)S(1)} %get-tuple-element.33.refs_5_), channel_id=1, source_target_pairs={{0,4},{4,0},{8,12},{12,8},{16,20},{20,16},{24,28},{28,24},{1,5},{5... | collective-permute-start | bytes 245768 | tf_op jit(solution)/shard_map/ppermute | solution.py:47
  24.2 7.4 %copy-start.4 = (f32[5,32,128]{2,1,0:T(8,128)}, f32[5,32,128]{2,1,0:T(8,128)S(1)}, u32[]{:S(2)}) copy-start(f32[5,32,128]{2,1,0:T(8,128)S(1)} %collective-permute-done.8.refs_15_) | copy-start | bytes 245764
  24.2 2.9 %collective-permute-start.13 = (f32[5,32,128]{2,1,0:T(8,128)S(1)}, f32[5,32,128]{2,1,0:T(8,128)S(1)}, u32[]{:S(2)}, u32[]{:S(2)}) collective-permute-start(f32[5,32,128]{2,1,0:T(8,128)S(1)} %collective-permute-done.12.refs_19_), channel_id=1, source_target_pairs={{0,1},{1,0},{2,3},{3,2},{4,5},{5,4},{6,7},{7,6},{8,9},{9,8},{10,11... | collective-permute-start | bytes 245768 | tf_op jit(solution)/shard_map/ppermute | solution.py:47
  25.1 6.5 %copy-start.5 = (f32[5,32,128]{2,1,0:T(8,128)}, f32[5,32,128]{2,1,0:T(8,128)S(1)}, u32[]{:S(2)}) copy-start(f32[5,32,128]{2,1,0:T(8,128)S(1)} %collective-permute-done.6.refs_13_) | copy-start | bytes 245764
  25.1 2.1 %collective-permute-start.11 = (f32[5,32,128]{2,1,0:T(8,128)S(1)}, f32[5,32,128]{2,1,0:T(8,128)S(1)}, u32[]{:S(2)}, u32[]{:S(2)}) collective-permute-start(f32[5,32,128]{2,1,0:T(8,128)S(1)} %collective-permute-done.10.refs_17_), channel_id=1, source_target_pairs={{0,1},{1,0},{2,3},{3,2},{4,5},{5,4},{6,7},{7,6},{8,9},{9,8},{10,11... | collective-permute-start | bytes 245768 | tf_op jit(solution)/shard_map/ppermute | solution.py:47
  26.0 5.6 %copy-start.6 = (f32[5,32,128]{2,1,0:T(8,128)}, f32[5,32,128]{2,1,0:T(8,128)S(1)}, u32[]{:S(2)}) copy-start(f32[5,32,128]{2,1,0:T(8,128)S(1)} %collective-permute-done.4.refs_11_) | copy-start | bytes 245764
  26.0 5.5 %collective-permute-start.9 = (f32[5,32,128]{2,1,0:T(8,128)S(1)}, f32[5,32,128]{2,1,0:T(8,128)S(1)}, u32[]{:S(2)}, u32[]{:S(2)}) collective-permute-start(f32[5,32,128]{2,1,0:T(8,128)S(1)} %collective-permute-done.8.refs_15_), channel_id=1, source_target_pairs={{0,1},{1,0},{2,3},{3,2},{4,5},{5,4},{6,7},{7,6},{8,9},{9,8},{10,11... | collective-permute-start | bytes 245768 | tf_op jit(solution)/shard_map/ppermute | solution.py:47
  26.5 5.1 %copy-start.7 = (f32[5,32,128]{2,1,0:T(8,128)}, f32[5,32,128]{2,1,0:T(8,128)S(1)}, u32[]{:S(2)}) copy-start(f32[5,32,128]{2,1,0:T(8,128)S(1)} %collective-permute-done.2.refs_9_) | copy-start | bytes 245764
  26.5 4.9 %collective-permute-start.7 = (f32[5,32,128]{2,1,0:T(8,128)S(1)}, f32[5,32,128]{2,1,0:T(8,128)S(1)}, u32[]{:S(2)}, u32[]{:S(2)}) collective-permute-start(f32[5,32,128]{2,1,0:T(8,128)S(1)} %collective-permute-done.6.refs_13_), channel_id=1, source_target_pairs={{0,1},{1,0},{2,3},{3,2},{4,5},{5,4},{6,7},{7,6},{8,9},{9,8},{10,11... | collective-permute-start | bytes 245768 | tf_op jit(solution)/shard_map/ppermute | solution.py:47
  26.6 5.0 %copy-start.8 = (f32[5,32,128]{2,1,0:T(8,128)}, f32[5,32,128]{2,1,0:T(8,128)S(1)}, u32[]{:S(2)}) copy-start(f32[5,32,128]{2,1,0:T(8,128)S(1)} %collective-permute-done.refs_7_) | copy-start | bytes 245764
  26.6 4.9 %collective-permute-start.5 = (f32[5,32,128]{2,1,0:T(8,128)S(1)}, f32[5,32,128]{2,1,0:T(8,128)S(1)}, u32[]{:S(2)}, u32[]{:S(2)}) collective-permute-start(f32[5,32,128]{2,1,0:T(8,128)S(1)} %collective-permute-done.4.refs_11_), channel_id=1, source_target_pairs={{0,1},{1,0},{2,3},{3,2},{4,5},{5,4},{6,7},{7,6},{8,9},{9,8},{10,11... | collective-permute-start | bytes 245768 | tf_op jit(solution)/shard_map/ppermute | solution.py:47
  27.0 4.6 %copy-start.9 = (f32[5,32,128]{2,1,0:T(8,128)}, f32[5,32,128]{2,1,0:T(8,128)S(1)}, u32[]{:S(2)}) copy-start(f32[5,32,128]{2,1,0:T(8,128)S(1)} %collective-permute-done.13.refs_20_) | copy-start | bytes 245764
  27.0 4.5 %collective-permute-start.3 = (f32[5,32,128]{2,1,0:T(8,128)S(1)}, f32[5,32,128]{2,1,0:T(8,128)S(1)}, u32[]{:S(2)}, u32[]{:S(2)}) collective-permute-start(f32[5,32,128]{2,1,0:T(8,128)S(1)} %collective-permute-done.2.refs_9_), channel_id=1, source_target_pairs={{0,1},{1,0},{2,3},{3,2},{4,5},{5,4},{6,7},{7,6},{8,9},{9,8},{10,11... | collective-permute-start | bytes 245768 | tf_op jit(solution)/shard_map/ppermute | solution.py:47
  27.1 4.5 %copy-start.10 = (f32[5,32,128]{2,1,0:T(8,128)}, f32[5,32,128]{2,1,0:T(8,128)S(1)}, u32[]{:S(2)}) copy-start(f32[5,32,128]{2,1,0:T(8,128)S(1)} %collective-permute-done.11.refs_18_) | copy-start | bytes 245764
  27.1 4.4 %collective-permute-start.1 = (f32[5,32,128]{2,1,0:T(8,128)S(1)}, f32[5,32,128]{2,1,0:T(8,128)S(1)}, u32[]{:S(2)}, u32[]{:S(2)}) collective-permute-start(f32[5,32,128]{2,1,0:T(8,128)S(1)} %collective-permute-done.refs_7_), channel_id=1, source_target_pairs={{0,1},{1,0},{2,3},{3,2},{4,5},{5,4},{6,7},{7,6},{8,9},{9,8},{10,11... | collective-permute-start | bytes 245768 | tf_op jit(solution)/shard_map/ppermute | solution.py:47
  31.5 0.6 copy-start.11
  31.5 0.6 copy-start.12
  31.5 0.7 copy-start.13
  31.5 0.7 copy-start.14
  31.5 0.7 copy-start.15
  100.2 2.9 %collective-permute-start.14 = (f32[2048,128]{1,0:T(8,128)}, f32[2048,128]{1,0:T(8,128)S(1)}, u32[]{:S(2)}, u32[]{:S(2)}) collective-permute-start(f32[2048,128]{1,0:T(8,128)} %get-tuple-element.14), channel_id=1, source_target_pairs={{0,1},{1,0},{2,3},{3,2},{4,5},{5,4},{6,7},{7,6},{8,9},{9,8},{10,11... | collective-permute-start | bytes 3145736 | tf_op jit(solution)/shard_map/ppermute | solution.py:47
  104.4 10.2 %collective-permute-start.17 = (f32[512,128]{1,0:T(8,128)S(1)}, f32[512,128]{1,0:T(8,128)S(1)}, u32[]{:S(2)}, u32[]{:S(2)}) collective-permute-start(f32[512,128]{1,0:T(8,128)S(1)} %get-tuple-element.25), channel_id=1, source_target_pairs={{0,6},{1,7},{2,4},{3,5},{4,2},{5,3},{6,0},{7,1},{8,14},{9,15},{10,... | collective-permute-start | bytes 786440 | tf_op jit(solution)/shard_map/ppermute | solution.py:47
  106.2 13.2 %collective-permute-start.16 = (f32[512,128]{1,0:T(8,128)S(1)}, f32[512,128]{1,0:T(8,128)S(1)}, u32[]{:S(2)}, u32[]{:S(2)}) collective-permute-start(f32[512,128]{1,0:T(8,128)S(1)} %get-tuple-element.26), channel_id=1, source_target_pairs={{0,4},{1,5},{2,6},{3,7},{4,0},{5,1},{6,2},{7,3},{8,12},{9,13},{10,... | collective-permute-start | bytes 786440 | tf_op jit(solution)/shard_map/ppermute | solution.py:47
  107.5 11.9 %collective-permute-start.15 = (f32[512,128]{1,0:T(8,128)S(1)}, f32[512,128]{1,0:T(8,128)S(1)}, u32[]{:S(2)}, u32[]{:S(2)}) collective-permute-start(f32[512,128]{1,0:T(8,128)S(1)} %get-tuple-element.27), channel_id=1, source_target_pairs={{0,2},{1,3},{2,0},{3,1},{4,6},{5,7},{6,4},{7,5},{8,10},{9,11},{10,... | collective-permute-start | bytes 786440 | tf_op jit(solution)/shard_map/ppermute | solution.py:47
  119.4 6.8 %collective-permute-start.20 = (f32[128,128]{1,0:T(8,128)S(1)}, f32[128,128]{1,0:T(8,128)S(1)}, u32[]{:S(2)}, u32[]{:S(2)}) collective-permute-start(f32[128,128]{1,0:T(8,128)S(1)} %get-tuple-element.28), channel_id=1, source_target_pairs={{0,24},{1,25},{2,26},{3,27},{4,28},{5,29},{6,30},{7,31},{8,16},{9,... | collective-permute-start | bytes 196616 | tf_op jit(solution)/shard_map/ppermute | solution.py:47
  122.0 6.2 %collective-permute-start.19 = (f32[128,128]{1,0:T(8,128)S(1)}, f32[128,128]{1,0:T(8,128)S(1)}, u32[]{:S(2)}, u32[]{:S(2)}) collective-permute-start(f32[128,128]{1,0:T(8,128)S(1)} %get-tuple-element.29), channel_id=1, source_target_pairs={{0,16},{1,17},{2,18},{3,19},{4,20},{5,21},{6,22},{7,23},{8,24},{9,... | collective-permute-start | bytes 196616 | tf_op jit(solution)/shard_map/ppermute | solution.py:47
  122.0 6.2 %collective-permute-start.18 = (f32[128,128]{1,0:T(8,128)S(1)}, f32[128,128]{1,0:T(8,128)S(1)}, u32[]{:S(2)}, u32[]{:S(2)}) collective-permute-start(f32[128,128]{1,0:T(8,128)S(1)} %get-tuple-element.30), channel_id=1, source_target_pairs={{0,8},{1,9},{2,10},{3,11},{4,12},{5,13},{6,14},{7,15},{8,0},{9,1},... | collective-permute-start | bytes 196616 | tf_op jit(solution)/shard_map/ppermute | solution.py:47
  128.2 3.4 %copy-start = (bf16[2,2048,1024]{2,1,0:T(8,128)(2,1)S(1)}, bf16[2,2048,1024]{2,1,0:T(8,128)(2,1)}, u32[]{:S(2)}) copy-start(bf16[2,2048,1024]{2,1,0:T(8,128)(2,1)} %refs_4_.3) | copy-start | bytes 25165828
  132.9 6.8 %collective-permute-start.21 = (f32[8,128]{1,0:T(8,128)S(1)}, f32[8,128]{1,0:T(8,128)S(1)}, u32[]{:S(2)}, u32[]{:S(2)}) collective-permute-start(f32[8,128]{1,0:T(8,128)S(1)} %get-tuple-element.16), channel_id=1, source_target_pairs={{0,4},{1,5},{2,6},{3,7},{4,0},{5,1},{6,2},{7,3},{8,12},{9,13},{10,... | collective-permute-start | bytes 12296 | tf_op jit(solution)/shard_map/ppermute | solution.py:47
  133.8 8.3 %collective-permute-start.22 = (f32[8,128]{1,0:T(8,128)S(1)}, f32[8,128]{1,0:T(8,128)S(1)}, u32[]{:S(2)}, u32[]{:S(2)}) collective-permute-start(f32[8,128]{1,0:T(8,128)S(1)} %get-tuple-element.17), channel_id=1, source_target_pairs={{0,8},{1,9},{2,10},{3,11},{4,12},{5,13},{6,14},{7,15},{8,0},{9,1},... | collective-permute-start | bytes 12296 | tf_op jit(solution)/shard_map/ppermute | solution.py:47
  134.5 9.6 %collective-permute-start.23 = (f32[8,128]{1,0:T(8,128)S(1)}, f32[8,128]{1,0:T(8,128)S(1)}, u32[]{:S(2)}, u32[]{:S(2)}) collective-permute-start(f32[8,128]{1,0:T(8,128)S(1)} %get-tuple-element.18), channel_id=1, source_target_pairs={{0,12},{1,13},{2,14},{3,15},{4,8},{5,9},{6,10},{7,11},{8,4},{9,5},... | collective-permute-start | bytes 12296 | tf_op jit(solution)/shard_map/ppermute | solution.py:47
  136.4 7.7 %collective-permute-start.24 = (f32[8,128]{1,0:T(8,128)S(1)}, f32[8,128]{1,0:T(8,128)S(1)}, u32[]{:S(2)}, u32[]{:S(2)}) collective-permute-start(f32[8,128]{1,0:T(8,128)S(1)} %get-tuple-element.19), channel_id=1, source_target_pairs={{0,16},{1,17},{2,18},{3,19},{4,20},{5,21},{6,22},{7,23},{8,24},{9,... | collective-permute-start | bytes 12296 | tf_op jit(solution)/shard_map/ppermute | solution.py:47
  137.6 6.5 %collective-permute-start.25 = (f32[8,128]{1,0:T(8,128)S(1)}, f32[8,128]{1,0:T(8,128)S(1)}, u32[]{:S(2)}, u32[]{:S(2)}) collective-permute-start(f32[8,128]{1,0:T(8,128)S(1)} %get-tuple-element.20), channel_id=1, source_target_pairs={{0,20},{1,21},{2,22},{3,23},{4,16},{5,17},{6,18},{7,19},{8,28},{9,... | collective-permute-start | bytes 12296 | tf_op jit(solution)/shard_map/ppermute | solution.py:47
  139.6 5.4 %collective-permute-start.26 = (f32[8,128]{1,0:T(8,128)S(1)}, f32[8,128]{1,0:T(8,128)S(1)}, u32[]{:S(2)}, u32[]{:S(2)}) collective-permute-start(f32[8,128]{1,0:T(8,128)S(1)} %get-tuple-element.21), channel_id=1, source_target_pairs={{0,24},{1,25},{2,26},{3,27},{4,28},{5,29},{6,30},{7,31},{8,16},{9,... | collective-permute-start | bytes 12296 | tf_op jit(solution)/shard_map/ppermute | solution.py:47
  142.1 6.3 %collective-permute-start.27 = (f32[8,128]{1,0:T(8,128)S(1)}, f32[8,128]{1,0:T(8,128)S(1)}, u32[]{:S(2)}, u32[]{:S(2)}) collective-permute-start(f32[8,128]{1,0:T(8,128)S(1)} %get-tuple-element.22), channel_id=1, source_target_pairs={{0,28},{1,29},{2,30},{3,31},{4,24},{5,25},{6,26},{7,27},{8,20},{9,... | collective-permute-start | bytes 12296 | tf_op jit(solution)/shard_map/ppermute | solution.py:47
  148.4 3.1 %collective-permute-start.30 = (f32[8,128]{1,0:T(8,128)S(1)}, f32[8,128]{1,0:T(8,128)S(1)}, u32[]{:S(2)}, u32[]{:S(2)}) collective-permute-start(f32[8,128]{1,0:T(8,128)S(1)} %add_add_fusion.1), channel_id=1, source_target_pairs={{0,3},{1,2},{2,1},{3,0},{4,7},{5,6},{6,5},{7,4},{8,11},{9,10},{10,... | collective-permute-start | bytes 12296 | tf_op jit(solution)/shard_map/ppermute | solution.py:47
  148.5 3.7 %collective-permute-start.29 = (f32[8,128]{1,0:T(8,128)S(1)}, f32[8,128]{1,0:T(8,128)S(1)}, u32[]{:S(2)}, u32[]{:S(2)}) collective-permute-start(f32[8,128]{1,0:T(8,128)S(1)} %add_add_fusion.1), channel_id=1, source_target_pairs={{0,2},{1,3},{2,0},{3,1},{4,6},{5,7},{6,4},{7,5},{8,10},{9,11},{10,... | collective-permute-start | bytes 12296 | tf_op jit(solution)/shard_map/ppermute | solution.py:47
  150.0 2.2 %collective-permute-start.28 = (f32[8,128]{1,0:T(8,128)S(1)}, f32[8,128]{1,0:T(8,128)S(1)}, u32[]{:S(2)}, u32[]{:S(2)}) collective-permute-start(f32[8,128]{1,0:T(8,128)S(1)} %add_add_fusion.1), channel_id=1, source_target_pairs={{0,1},{1,0},{2,3},{3,2},{4,5},{5,4},{6,7},{7,6},{8,9},{9,8},{10,11... | collective-permute-start | bytes 12296 | tf_op jit(solution)/shard_map/ppermute | solution.py:47

commit v2 on v1

v2 whole, which is shorter than its diff:
```python
import functools

import jax
import jax.numpy as jnp
from jax import lax
from jax.experimental import pallas as pl
from jax.experimental.pallas import tpu as pltpu
from jax.sharding import PartitionSpec as P

BOUNCES = 4
MOST_COPIES = 8
SMALL = 4 * 2**20
LARGE = 60 * 2**20
CHUNKS = 8
LANES = 128
VALUES = 8
GROUPS = LANES // VALUES
VMEM = pl.BlockSpec(memory_space=pltpu.VMEM)
SMEM = pl.BlockSpec(memory_space=pltpu.SMEM)
ANY = pl.BlockSpec(memory_space=pl.ANY)
F32 = jnp.float32


def bits_of(count):
    assert count & (count - 1) == 0
    return count.bit_length() - 1


def sum_phases(bits):
    phases = [[0]]
    rest = list(range(1, bits))
    while rest:
        phases.append(rest[:2])
        rest = rest[2:]
    return phases


def spread(digit, phase):
    return sum(((digit >> place) & 1) << bit for place, bit in enumerate(phase))


def place_of(offset, phases):
    place = 0
    for phase in phases:
        for bit in reversed(phase):
            place = place * 2 + ((offset >> bit) & 1)
    return place


def send(value, mask, axes, count):
    return lax.ppermute(value, axes, [(i, i ^ mask) for i in range(count)])


def sine_cosine(angle):
    turns = jnp.floor(angle * 0.6366197723675814 + 0.5)
    rest = angle - turns * 1.5703125
    rest = rest - turns * 4.837512969970703e-4
    rest = rest - turns * 7.54978995489188e-8
    square = rest * rest
    sine = rest + rest * square * (
        -1.6666654611e-1 + square * (8.3321608736e-3 - square * 1.9515295891e-4)
    )
    cosine = 1.0 - 0.5 * square + square * square * (
        4.166664568298827e-2 + square * (-1.388731625493765e-3 + square * 2.443315711809948e-5)
    )
    quarter = turns.astype(jnp.int32)
    odd = (quarter & 1) == 1
    first = jnp.where(odd, cosine, sine)
    second = jnp.where(odd, sine, cosine)
    return (
        jnp.where((quarter & 2) == 2, -first, first),
        jnp.where(((quarter + 1) & 2) == 2, -second, second),
    )


def divide(top_real, top_imag, low_real, low_imag):
    scale = 1.0 / (low_real * low_real + low_imag * low_imag)
    return (
        (top_real * low_real + top_imag * low_imag) * scale,
        (top_imag * low_real - top_real * low_imag) * scale,
    )


def bounce_once(field, heading, facet, sine, cosine):
    real = [cosine * field[i] - sine * field[4 + i] for i in range(4)]
    imag = [sine * field[i] + cosine * field[4 + i] for i in range(4)]
    normal = facet[0:3]
    eta_real, eta_imag, tilt_cos, tilt_sin = facet[3:7]
    incidence = heading[0] * normal[0] + heading[1] * normal[1] + heading[2] * normal[2]
    slant = jnp.abs(incidence)
    te_real, te_imag = divide(slant - eta_real, -eta_imag, slant + eta_real, eta_imag)
    tm_real, tm_imag = divide(
        eta_real * slant - 1.0, eta_imag * slant, eta_real * slant + 1.0, eta_imag * slant
    )
    out_real, out_imag = [None] * 4, [None] * 4
    for i in range(2):
        upper_real = tilt_cos * real[i] + tilt_sin * real[2 + i]
        lower_real = tilt_cos * real[2 + i] - tilt_sin * real[i]
        upper_imag = tilt_cos * imag[i] + tilt_sin * imag[2 + i]
        lower_imag = tilt_cos * imag[2 + i] - tilt_sin * imag[i]
        out_real[i] = te_real * upper_real - te_imag * upper_imag
        out_real[2 + i] = tm_real * lower_real - tm_imag * lower_imag
        out_imag[i] = te_real * upper_imag + te_imag * upper_real
        out_imag[2 + i] = tm_real * lower_imag + tm_imag * lower_real
    twice = 2.0 * incidence
    return out_real + out_imag, [heading[k] - twice * normal[k] for k in range(3)]


def pack_kernel(axes, rows, *refs):
    share, arrive = refs[5], refs[6]
    at = pl.multiple_of(lax.axis_index(axes[1]) * rows, rows)
    loads = [
        pltpu.make_async_copy(refs[k].at[pl.ds(at, rows), :], share.at[k], arrive.at[k])
        for k in range(5)
    ]
    for load in loads:
        load.start()
    for load in loads:
        load.wait()


def build_kernel(depth, *refs):
    out, frame = refs[-2], refs[-1]
    steps = depth // LANES
    base = 0
    for ref in refs[:-2]:
        pieces, _, rows, _ = ref.shape

        def build(n, carry, ref=ref, rows=rows, base=base):
            polar_sin, polar_cos = sine_cosine(ref[n, 0])
            azimuth_sin, azimuth_cos = sine_cosine(ref[n, 1])
            tilt_sin, tilt_cos = sine_cosine(ref[n, 2])
            values = [
                polar_sin * azimuth_cos,
                polar_sin * azimuth_sin,
                polar_cos,
                ref[n, 3],
                ref[n, 4],
                tilt_cos,
                tilt_sin,
                tilt_sin,
            ]
            for k in range(VALUES):
                frame[n % 2, k * rows : (k + 1) * rows, :] = values[k]
            for m in range(steps):
                tall = jnp.concatenate(
                    [
                        frame[n % 2, pl.ds(j * steps + m, VALUES, stride=rows), :]
                        for j in range(GROUPS)
                    ],
                    axis=0,
                )
                at = pl.multiple_of((base + n) * depth + m * LANES, LANES)
                out[pl.ds(at, LANES), :] = tall.T
            return carry

        lax.fori_loop(0, pieces, build, 0)
        base += pieces


def prepare_kernel(meta, launch, hop, hit, angle, field, heading, *refs):
    (owned, bins, depth, phases, axes) = meta
    rows, groups, sines, cosines, fields, headings, facets, angles = refs
    blocks = launch.shape[0]
    for k in range(blocks):
        lanes = slice(k * LANES, (k + 1) * LANES)
        facets[pl.ds(k, BOUNCES, stride=blocks), :] = hit[:, lanes]
        angles[pl.ds(k, BOUNCES, stride=blocks), :] = angle[:, lanes]
        fields[pl.ds(k, 8, stride=blocks), :] = field[:, lanes]
        headings[pl.ds(k, 3, stride=blocks), :] = heading[:, lanes]
    me = lax.axis_index(axes)
    for bounce in range(BOUNCES):
        at = slice(bounce * blocks, (bounce + 1) * blocks)
        domain = launch[...] if bounce == 0 else hop[(bounce - 1) * blocks : bounce * blocks, :]
        facet = facets[at, :]
        quarter = facet >> bits_of(owned)
        within = facet & (owned - 1)
        place = place_of((domain * bins + quarter) ^ me, phases)
        rows[at, :] = place * depth + (within & (depth - 1))
        groups[at, :] = within >> bits_of(depth)
        sine, cosine = sine_cosine(angles[at, :])
        sines[at, :] = sine
        cosines[at, :] = cosine


def trace_kernel(meta, *refs):
    (blocks, shares, parts, copies) = meta
    rows_ref, group_ref, sine_ref, cosine_ref, field_ref, heading_ref = refs[:6]
    share_refs = refs[6 : 6 + shares]
    part_refs = refs[6 + shares : 6 + shares + parts]
    exit_ref = refs[6 + shares + parts]
    scratch = refs[7 + shares + parts :]
    even, odd, even_held, odd_held, picked, fields, flat, arrive, leave = scratch[:9]
    sums = scratch[9:]
    total = sums[0].shape[0]
    count = BOUNCES * blocks

    loads = [
        pltpu.make_async_copy(
            share_refs[i],
            flat.at[pl.ds(i * (total // shares), total // shares), :],
            arrive.at[i],
        )
        for i in range(shares)
    ]
    for load in loads:
        load.start()

    clear = 64
    zeros = jnp.zeros((clear, LANES), F32)

    def wipe(i, carry):
        for ref in sums:
            ref[pl.ds(pl.multiple_of(i * clear, clear), clear), :] = zeros
        return carry

    lax.fori_loop(0, total // clear, wipe, 0)

    for load in loads:
        load.wait()

    def fetch(block, into):
        for u in range(LANES):
            into[u : u + 1, :] = flat[pl.ds(rows_ref[block * LANES + u], 1), :]

    def group_of(block):
        return jnp.broadcast_to(group_ref[pl.ds(block, 1), :], (VALUES, LANES))

    def pick(block, source):
        group = group_of(jnp.maximum(block, 0))
        tall = source[...].T.reshape(GROUPS, VALUES, LANES)
        left = [tall[j] for j in range(GROUPS)]
        level = 0
        while len(left) > 1:
            upper = ((group >> level) & 1) == 1
            left = [jnp.where(upper, left[2 * n + 1], left[2 * n]) for n in range(len(left) // 2)]
            level += 1
        picked[pl.ds(pl.multiple_of((block + 2) * VALUES, VALUES), VALUES), :] = left[0]

    def gather(i, carry):
        pick(2 * i - 2, even_held)
        pick(2 * i - 1, odd_held)
        fetch(2 * i, even)
        fetch(2 * i + 1, odd)
        even_held[...] = even[...]
        odd_held[...] = odd[...]
        return carry

    lax.fori_loop(0, count // 2, gather, 0)
    pick(count - 2, even_held)
    pick(count - 1, odd_held)

    field = [field_ref[c * blocks : (c + 1) * blocks, :] for c in range(8)]
    heading = [heading_ref[c * blocks : (c + 1) * blocks, :] for c in range(3)]
    for bounce in range(BOUNCES):
        facet = [
            picked[pl.ds((bounce * blocks + 2) * VALUES + c, blocks, stride=VALUES), :]
            for c in range(7)
        ]
        at = slice(bounce * blocks, (bounce + 1) * blocks)
        field, heading = bounce_once(field, heading, facet, sine_ref[at, :], cosine_ref[at, :])
        for c in range(VALUES):
            fields[bounce, c * blocks : (c + 1) * blocks, :] = field[c]
    for k in range(blocks):
        exit_ref[:, k * LANES : (k + 1) * LANES] = fields[
            BOUNCES - 1, pl.ds(k, VALUES, stride=blocks), :
        ]

    def widen(block, into):
        own = fields[block // blocks, pl.ds(block % blocks, VALUES, stride=blocks), :]
        group = group_of(block)
        tall = jnp.concatenate([jnp.where(group == j, own, 0.0) for j in range(GROUPS)], axis=0)
        into[...] = tall.T

    def add(block, source):
        for u in range(0, LANES, copies):
            fresh = []
            for c in range(copies):
                row = rows_ref[block * LANES + u + c]
                fresh.append((row, sums[c][pl.ds(row, 1), :] + source[u + c : u + c + 1, :]))
            for c in range(copies):
                sums[c][pl.ds(fresh[c][0], 1), :] = fresh[c][1]

    widen(0, even)

    def scatter(i, carry):
        widen(2 * i + 1, odd)
        add(2 * i, even)
        widen(jnp.minimum(2 * i + 2, count - 1), even)
        add(2 * i + 1, odd)
        return carry

    lax.fori_loop(0, count // 2, scatter, 0)

    size = total // parts
    outs = []
    for part in reversed(range(parts)):

        def merge(i, carry, part=part):
            at = pl.ds(pl.multiple_of(part * size + i * LANES, LANES), LANES)
            sums[0][at, :] = functools.reduce(lambda a, b: a + b, [ref[at, :] for ref in sums])
            return carry

        if copies > 1:
            lax.fori_loop(0, size // LANES, merge, 0)
        outs.append(
            pltpu.make_async_copy(
                sums[0].at[pl.ds(part * size, size), :], part_refs[part], leave.at[part]
            )
        )
        outs[-1].start()
    for out in outs:
        out.wait()


def field_kernel(meta, *refs):
    (terms, tiles, chunks) = meta
    kernel_ref, out, stream, arrive = refs[terms:]
    size = kernel_ref.shape[1] // chunks
    loads = [
        [
            pltpu.make_async_copy(
                kernel_ref.at[h, pl.ds(i * size, size), :],
                stream.at[h, pl.ds(i * size, size), :],
                arrive.at[i, h],
            )
            for h in range(2)
        ]
        for i in range(chunks)
    ]
    for pair in loads:
        for load in pair:
            load.start()
    total = functools.reduce(lambda a, b: a + b, [ref[...] for ref in refs[:terms]])
    depth = total.shape[0]
    rounded = []
    tall = [
        total[m * LANES : (m + 1) * LANES, :].T.reshape(GROUPS, VALUES, LANES)
        for m in range(depth // LANES)
    ]
    for j in range(GROUPS):
        for m in range(depth // LANES):
            rounded.append(tall[m][j])
    left = jnp.concatenate(rounded, axis=1).astype(jnp.bfloat16)
    real = jnp.zeros((VALUES, kernel_ref.shape[2]), F32)
    imag = real
    for i in range(chunks):
        for load in loads[i]:
            load.wait()
        piece = left[:, i * size : (i + 1) * size]
        real += jnp.dot(piece, stream[0, i * size : (i + 1) * size, :], preferred_element_type=F32)
        imag += jnp.dot(piece, stream[1, i * size : (i + 1) * size, :], preferred_element_type=F32)
    far = jnp.concatenate([real[0:4] - imag[4:8], imag[0:4] + real[4:8]], axis=0)
    count = out.shape[0]
    for i in range(count):
        tile = i * tiles // count
        out[i] = far[:, tile * LANES : (tile + 1) * LANES]


def body(
    axes,
    sizes,
    field_in,
    heading_in,
    launch_domain,
    hop_domain,
    hit_facet,
    path_phase,
    facet_polar,
    facet_azimuth,
    facet_tilt,
    surface_resistance,
    surface_reactance,
    kernel,
):
    domains, bins = sizes
    count = domains * bins
    phases = sum_phases(bits_of(count))
    me = lax.axis_index(axes)
    tubes = field_in.shape[1]
    facets = facet_polar.shape[0]
    owned = kernel.shape[1]
    depth = owned // GROUPS
    blocks = tubes // LANES
    total = count * depth

    lines = owned // LANES
    geometry = (facet_polar, facet_azimuth, facet_tilt, surface_resistance, surface_reactance)
    share = pl.pallas_call(
        functools.partial(pack_kernel, axes, lines),
        out_shape=jax.ShapeDtypeStruct((5, lines, LANES), F32),
        in_specs=[ANY] * 5,
        out_specs=VMEM,
        scratch_shapes=[pltpu.SemaphoreType.DMA((5,))],
        compiler_params=pltpu.CompilerParams(vmem_limit_bytes=LARGE),
    )(*[value.reshape(facets // LANES, LANES) for value in geometry])
    held = [share[None]]
    for phase_bits in reversed(phases[1:]):
        mine = held[0] if len(held) == 1 else jnp.concatenate(held)
        held = [mine] + [
            send(mine, spread(d, phase_bits), axes, count) for d in range(1, 1 << len(phase_bits))
        ]
    parts = 1 << len(phases[0])
    mine = pl.pallas_call(
        functools.partial(build_kernel, depth),
        out_shape=jax.ShapeDtypeStruct((total // parts, LANES), F32),
        in_specs=[VMEM] * len(held),
        out_specs=VMEM,
        scratch_shapes=[pltpu.VMEM((2, VALUES * lines, LANES), F32)],
        compiler_params=pltpu.CompilerParams(vmem_limit_bytes=SMALL + 8 * LANES * total),
    )(*held)
    tables = [mine] + [send(mine, spread(d, phases[0]), axes, count) for d in range(1, parts)]

    rows = BOUNCES * blocks
    whole = jax.ShapeDtypeStruct((rows, LANES), F32)
    marks = jax.ShapeDtypeStruct((rows, LANES), jnp.int32)
    hit_rows, *prepared = pl.pallas_call(
        functools.partial(prepare_kernel, (owned, bins, depth, phases, axes)),
        out_shape=[
            marks,
            marks,
            whole,
            whole,
            jax.ShapeDtypeStruct((8 * blocks, LANES), F32),
            jax.ShapeDtypeStruct((3 * blocks, LANES), F32),
        ],
        in_specs=[VMEM] * 6,
        out_specs=[VMEM] * 6,
        scratch_shapes=[pltpu.VMEM((rows, LANES), jnp.int32), pltpu.VMEM((rows, LANES), F32)],
        compiler_params=pltpu.CompilerParams(vmem_limit_bytes=LARGE),
    )(
        launch_domain.reshape(blocks, LANES),
        hop_domain.reshape((BOUNCES - 1) * blocks, LANES),
        hit_facet,
        path_phase,
        field_in,
        heading_in,
    )

    copies = 1
    while copies < MOST_COPIES and copies * 2 * total * LANES * 4 <= 16 * 2**20:
        copies *= 2
    meta = (blocks, len(tables), parts, copies)
    buffers = [
        ((LANES, LANES), F32),
        ((LANES, LANES), F32),
        ((LANES, LANES), F32),
        ((LANES, LANES), F32),
        ((VALUES * (rows + 2), LANES), F32),
        ((BOUNCES, VALUES * blocks, LANES), F32),
        ((total, LANES), F32),
    ]
    sum_buffers = [((total, LANES), F32)] * copies
    *sums, exit_field = pl.pallas_call(
        functools.partial(trace_kernel, meta),
        out_shape=[jax.ShapeDtypeStruct((total // parts, LANES), F32)] * parts
        + [jax.ShapeDtypeStruct((8, tubes), F32)],
        in_specs=[SMEM] + [VMEM] * 5 + [ANY] * len(tables),
        out_specs=[ANY] * parts + [VMEM],
        scratch_shapes=[pltpu.VMEM(*buffer) for buffer in buffers]
        + [
            pltpu.SemaphoreType.DMA((len(tables),)),
            pltpu.SemaphoreType.DMA((parts,)),
        ]
        + [pltpu.VMEM(*buffer) for buffer in sum_buffers],
        compiler_params=pltpu.CompilerParams(vmem_limit_bytes=LARGE),
    )(hit_rows.reshape(rows * LANES), *prepared, *tables)

    for n, phase_bits in enumerate(phases):
        terms = [sums[0]] + [
            send(sums[d], spread(d, phase_bits), axes, count) for d in range(1, len(sums))
        ]
        if n + 1 < len(phases):
            parts = 1 << len(phases[n + 1])
            size = terms[0].shape[0] // parts
            sums = [
                functools.reduce(lambda a, b: a + b, [t[p * size : (p + 1) * size] for t in terms])
                for p in range(parts)
            ]

    columns = kernel.shape[2]
    tiles = columns // LANES
    partial = pl.pallas_call(
        functools.partial(field_kernel, (len(terms), tiles, CHUNKS)),
        out_shape=jax.ShapeDtypeStruct((count, 8, LANES), F32),
        in_specs=[VMEM] * len(terms) + [ANY],
        out_specs=VMEM,
        scratch_shapes=[
            pltpu.VMEM(kernel.shape, kernel.dtype),
            pltpu.SemaphoreType.DMA((CHUNKS, 2)),
        ],
        compiler_params=pltpu.CompilerParams(vmem_limit_bytes=LARGE),
    )(*terms, kernel)
    tile = jnp.sum(lax.all_to_all(partial, axes, 0, 0, tiled=True), axis=0)
    width = columns // count
    far_field = lax.dynamic_slice_in_dim(tile, (me & (count // tiles - 1)) * width, width, 1)
    return far_field, exit_field


def solution(mesh):
    both = ("dom", "bin")
    in_specs = (
        P(None, both),
        P(None, both),
        P(both, None),
        P(None, both, None),
        P(None, both),
        P(None, both),
        P("dom"),
        P("dom"),
        P("dom"),
        P("dom"),
        P("dom"),
        P(None, both, None),
    )
    out_specs = (P(None, both), P(None, both))
    sizes = (mesh.shape["dom"], mesh.shape["bin"])
    return jax.shard_map(
        functools.partial(body, both, sizes),
        mesh=mesh,
        in_specs=in_specs,
        out_specs=out_specs,
        check_vma=False,
    )
```

time: 154 us -> 115 us (0.75)
  Pallas kernels: 69.2 us -> 49 us
  starting transfers between devices: 39.4 us -> 20.4 us
  waiting for transfers between devices: 28.1 us -> 38.9 us
  local copies, waits for them, and re-layouts: 12.7 us -> 2.28 us
    pallas_call x1, Pallas kernels: 68 us -> 37.6 us  [body(): pl.pallas_call(functools.partial(trace_kernel, meta), out_shape=[jax.Shap...]
    ppermute x31 -> x14, starting transfers between devices: 39.4 us -> 17.5 us  [send(): return lax.ppermute(value, axes, [(i, i ^ mask) for i in range(count)])]
    pallas_call x1 -> x4, Pallas kernels: 1.24 us -> 11.4 us  [the longest x1 5.35 us: body(): pl.pallas_call(functools.partial(field_kernel, (len(terms), tiles, CHUNKS...]
    unnamed x40 -> x10, local copies, waits for them, and re-layouts: 10.6 us -> 1.61 us
    all_to_all x0 -> x1, waiting for transfers between devices: none -> 8.22 us  [body(): tile = jnp.sum(lax.all_to_all(partial, axes, 0, 0, tiled=True), axis=0)]
    all_to_all x0 -> x1, starting transfers between devices: none -> 2.94 us  [body(): tile = jnp.sum(lax.all_to_all(partial, axes, 0, 0, tiled=True), axis=0)]
    ppermute x31 -> x14, waiting for transfers between devices: 28.1 us -> 30.7 us  [send(): return lax.ppermute(value, axes, [(i, i ^ mask) for i in range(count)])]
  transfers between devices with their start and end apart: 31 -> 15, of which waited for: 11 -> 12; matrix products, arithmetic and copies ran while one was open for 3% -> 0% of each run, Pallas kernels for 0% -> 2%
where the time goes in v2:
time: 115 us; the launch traced here: 114 us
  Pallas kernels  49 us (43%)
  waiting for transfers between devices  38.9 us (34%)
  starting transfers between devices  20.4 us (18%)
  other arithmetic  2.82 us (2%)
  local copies, waits for them, and re-layouts  2.28 us (2%)
    pallas_call x1, Pallas kernels, body(): pl.pallas_call(functools.partial(trace_kernel, meta), out_shape=[jax.Shap...  37.6 us
    ppermute x14, waiting for transfers between devices, send(): return lax.ppermute(value, axes, [(i, i ^ mask) for i in range(count)])  30.7 us
    ppermute x14, starting transfers between devices, send(): return lax.ppermute(value, axes, [(i, i ^ mask) for i in range(count)])  17.5 us
    all_to_all x1, waiting for transfers between devices, body(): tile = jnp.sum(lax.all_to_all(partial, axes, 0, 0, tiled=True), axis=0)  8.22 us
    pallas_call x1, Pallas kernels, body(): pl.pallas_call(functools.partial(field_kernel, (len(terms), tiles, CHUNKS...  5.35 us
    all_to_all x1, starting transfers between devices, body(): tile = jnp.sum(lax.all_to_all(partial, axes, 0, 0, tiled=True), axis=0)  2.94 us
    pallas_call x1, Pallas kernels, body(): pl.pallas_call(functools.partial(prepare_kernel, (owned, bins, depth, pha...  2.35 us
  transfers between devices with their start and end apart: 15, of which 12 were waited for; matrix products, arithmetic and copies ran while one was open for 0% of the time, Pallas kernels for 2%

profile of v2, /device:TPU:0, one launch (start us, length us, event | category | flops | bytes accessed | tf_op | source)
XLA Modules:
  0.0 114.1 jit_solution(10203644507426362981)
XLA Ops:
  0.6 1.4 %shard_map.132 = f32[5,16,128]{2,1,0:T(8,128)} custom-call(f32[64,128]{1,0:T(8,128)} %bitcast.15, f32[64,128]{1,0:T(8,128)} %bitcast.16, f32[64,128]{1,0:T(8,128)} %bitcast.17, f32[64,128]{1,0:T(8,128)} %bitcast.18, f32[64,128]{1,0:T(8,128)} %bitcast.19), custom_call_target="tpu_custom_call" | custom-call | tf_op jit(solution)/shard_map/pallas_call | solution.py:389
  2.1 3.1 %collective-permute-start = (f32[1,5,16,128]{3,2,1,0:T(8,128)}, f32[1,5,16,128]{3,2,1,0:T(8,128)S(1)}, u32[]{:S(2)}, u32[]{:S(2)}) collective-permute-start(f32[1,5,16,128]{3,2,1,0:T(8,128)} %bitcast.9), channel_id=1, source_target_pairs={{0,8},{1,9},{2,10},{3,11},{4,12},{5,13},{6,14},{7,15},{8,0},{9,1},... | collective-permute-start | bytes 122888 | tf_op jit(solution)/shard_map/ppermute | solution.py:51
  5.2 2.6 %collective-permute-start.1 = (f32[1,5,16,128]{3,2,1,0:T(8,128)}, f32[1,5,16,128]{3,2,1,0:T(8,128)S(1)}, u32[]{:S(2)}, u32[]{:S(2)}) collective-permute-start(f32[1,5,16,128]{3,2,1,0:T(8,128)} %bitcast.10), channel_id=1, source_target_pairs={{0,16},{1,17},{2,18},{3,19},{4,20},{5,21},{6,22},{7,23},{8,24},{9,... | collective-permute-start | bytes 122888 | tf_op jit(solution)/shard_map/ppermute | solution.py:51
  7.7 0.0 collective-permute-start.2
  7.8 0.0 collective-permute-done
  7.8 3.3 %collective-permute-done.1 = f32[1,5,16,128]{3,2,1,0:T(8,128)S(1)} collective-permute-done((f32[1,5,16,128]{3,2,1,0:T(8,128)}, f32[1,5,16,128]{3,2,1,0:T(8,128)S(1)}, u32[]{:S(2)}, u32[]{:S(2)}) %collective-permute-start.1) | collective-permute-done | bytes 40992 | tf_op jit(solution)/shard_map/ppermute | solution.py:51
  11.0 2.7 %collective-permute-done.2 = f32[1,5,16,128]{3,2,1,0:T(8,128)S(1)} collective-permute-done((f32[1,5,16,128]{3,2,1,0:T(8,128)}, f32[1,5,16,128]{3,2,1,0:T(8,128)S(1)}, u32[]{:S(2)}, u32[]{:S(2)}) %collective-permute-start.2) | collective-permute-done | bytes 40992 | tf_op jit(solution)/shard_map/ppermute | solution.py:51
  13.8 0.8 pad_maximum_fusion.refs_0_
  14.6 1.6 %collective-permute-start.3 = (f32[4,5,16,128]{3,2,1,0:T(8,128)S(1)}, f32[4,5,16,128]{3,2,1,0:T(8,128)S(1)}, u32[]{:S(2)}, u32[]{:S(2)}) collective-permute-start(f32[4,5,16,128]{3,2,1,0:T(8,128)S(1)} %pad_maximum_fusion.refs_0_), channel_id=1, source_target_pairs={{0,2},{1,3},{2,0},{3,1},{4,6},{5,7},{6,4},{7,5},{8,10},{9,11},{10,... | collective-permute-start | bytes 491528 | tf_op jit(solution)/shard_map/ppermute | solution.py:51
  16.1 1.5 %collective-permute-start.4 = (f32[4,5,16,128]{3,2,1,0:T(8,128)S(1)}, f32[4,5,16,128]{3,2,1,0:T(8,128)S(1)}, u32[]{:S(2)}, u32[]{:S(2)}) collective-permute-start(f32[4,5,16,128]{3,2,1,0:T(8,128)S(1)} %pad_maximum_fusion.refs_0_), channel_id=1, source_target_pairs={{0,4},{1,5},{2,6},{3,7},{4,0},{5,1},{6,2},{7,3},{8,12},{9,13},{10,... | collective-permute-start | bytes 491528 | tf_op jit(solution)/shard_map/ppermute | solution.py:51
  17.6 0.5 collective-permute-start.5
  18.1 3.2 %collective-permute-done.3.refs_1_ = f32[4,5,16,128]{3,2,1,0:T(8,128)S(1)} collective-permute-done((f32[4,5,16,128]{3,2,1,0:T(8,128)S(1)}, f32[4,5,16,128]{3,2,1,0:T(8,128)S(1)}, u32[]{:S(2)}, u32[]{:S(2)}) %collective-permute-start.3) | collective-permute-done | bytes 163872 | tf_op jit(solution)/shard_map/ppermute | solution.py:51
  21.3 3.0 %collective-permute-done.4.refs_2_ = f32[4,5,16,128]{3,2,1,0:T(8,128)S(1)} collective-permute-done((f32[4,5,16,128]{3,2,1,0:T(8,128)S(1)}, f32[4,5,16,128]{3,2,1,0:T(8,128)S(1)}, u32[]{:S(2)}, u32[]{:S(2)}) %collective-permute-start.4) | collective-permute-done | bytes 163872 | tf_op jit(solution)/shard_map/ppermute | solution.py:51
  24.3 0.0 collective-permute-done.5.refs_3_
  24.3 2.2 %shard_map.133.refs_6_ = f32[2048,128]{1,0:T(8,128)S(1)} custom-call(f32[4,5,16,128]{3,2,1,0:T(8,128)S(1)} %pad_maximum_fusion.refs_0_, f32[4,5,16,128]{3,2,1,0:T(8,128)S(1)} %collective-permute-done.3.refs_1_, f32[4,5,16,128]{3,2,1,0:T(8,128)S(1)} %collective-permute-done.4.refs_2_, f32[4,5,16,128]{3,2,1,0:T(8,128)S(1)} %collective-permute-done.5.refs_3_), custom_call_target="tpu_custom_call" | custom-call | tf_op jit(solution)/shard_map/pallas_call | solution.py:404
  26.6 0.0 copy-start
  26.6 0.1 collective-permute-start.6
  26.7 2.4 %shard_map.131 = (s32[128,128]{1,0:T(8,128)}, s32[128,128]{1,0:T(8,128)}, f32[128,128]{1,0:T(8,128)}, f32[128,128]{1,0:T(8,128)}, f32[256,128]{1,0:T(8,128)}, /*index=5*/f32[96,128]{1,0:T(8,128)}) custom-call(s32[32,128]{1,0:T(8,128)} %bitcast.20, s32[96,128]{1,0:T(8,128)} %bitcast.14, s32[4,4096]{1,0:T(4,128)} %hit.1, f32[4,4096]{1,0:T(4,128)} %angle.1, ...), custom_call_target="tpu_custom_call" | custom-call | tf_op jit(solution)/shard_map/pallas_call | solution.py:417
  29.0 0.3 collective-permute-done.6.refs_7_
  29.3 0.0 copy-start.1
  29.3 0.0 copy-done
  29.3 1.0 copy-done.1
  30.3 37.6 %shard_map.134 = (f32[2048,128]{1,0:T(8,128)}, f32[2048,128]{1,0:T(8,128)}, f32[8,4096]{1,0:T(8,128)}) custom-call(s32[16384]{0:T(1024)} %bitcast.13, s32[128,128]{1,0:T(8,128)} %get-tuple-element.12.refs_1_, f32[128,128]{1,0:T(8,128)} %get-tuple-element.13.refs_2_, f32[128,128]{1,0:T(8,128)} %get-tuple-element.14.refs_3_, ...), custom_call_target="tpu_custom_call" | custom-call | tf_op jit(solution)/shard_map/pallas_call | solution.py:454
  67.9 0.2 collective-permute-start.7
  68.2 2.7 %collective-permute-done.7 = f32[2048,128]{1,0:T(8,128)S(1)} collective-permute-done((f32[2048,128]{1,0:T(8,128)}, f32[2048,128]{1,0:T(8,128)S(1)}, u32[]{:S(2)}, u32[]{:S(2)}) %collective-permute-start.7) | collective-permute-done | bytes 1048608 | tf_op jit(solution)/shard_map/ppermute | solution.py:51
  70.9 1.3 %slice_add_fusion.3 = (f32[512,128]{1,0:T(8,128)S(1)}, f32[512,128]{1,0:T(8,128)S(1)}, f32[512,128]{1,0:T(8,128)S(1)}, f32[512,128]{1,0:T(8,128)S(1)}) fusion(f32[2048,128]{1,0:T(8,128)S(1)} %collective-permute-done.7, f32[2048,128]{1,0:T(8,128)} %get-tuple-element.17), kind=kLoop, calls=%fused_computation.3 | loop fusion | flops 262144 | bytes 3145728 | tf_op jit(solution)/shard_map/add | solution.py:477
  72.2 0.9 collective-permute-start.10
  73.1 1.6 %collective-permute-start.8 = (f32[512,128]{1,0:T(8,128)S(1)}, f32[512,128]{1,0:T(8,128)S(1)}, u32[]{:S(2)}, u32[]{:S(2)}) collective-permute-start(f32[512,128]{1,0:T(8,128)S(1)} %get-tuple-element.23), channel_id=1, source_target_pairs={{0,2},{1,3},{2,0},{3,1},{4,6},{5,7},{6,4},{7,5},{8,10},{9,11},{10,... | collective-permute-start | bytes 786440 | tf_op jit(solution)/shard_map/ppermute | solution.py:51
  74.7 1.0 collective-permute-start.9
  75.7 6.6 %collective-permute-done.10 = f32[512,128]{1,0:T(8,128)S(1)} collective-permute-done((f32[512,128]{1,0:T(8,128)S(1)}, f32[512,128]{1,0:T(8,128)S(1)}, u32[]{:S(2)}, u32[]{:S(2)}) %collective-permute-start.10) | collective-permute-done | bytes 262176 | tf_op jit(solution)/shard_map/ppermute | solution.py:51
  82.3 4.4 %collective-permute-done.8 = f32[512,128]{1,0:T(8,128)S(1)} collective-permute-done((f32[512,128]{1,0:T(8,128)S(1)}, f32[512,128]{1,0:T(8,128)S(1)}, u32[]{:S(2)}, u32[]{:S(2)}) %collective-permute-start.8) | collective-permute-done | bytes 262176 | tf_op jit(solution)/shard_map/ppermute | solution.py:51
  86.7 0.4 collective-permute-done.9
  87.1 0.7 slice_add_fusion.4
  87.8 0.0 collective-permute-start.11
  87.8 1.2 %collective-permute-start.12 = (f32[128,128]{1,0:T(8,128)S(1)}, f32[128,128]{1,0:T(8,128)S(1)}, u32[]{:S(2)}, u32[]{:S(2)}) collective-permute-start(f32[128,128]{1,0:T(8,128)S(1)} %get-tuple-element.25), channel_id=1, source_target_pairs={{0,16},{1,17},{2,18},{3,19},{4,20},{5,21},{6,22},{7,23},{8,24},{9,... | collective-permute-start | bytes 196616 | tf_op jit(solution)/shard_map/ppermute | solution.py:51
  89.1 3.1 %collective-permute-start.13 = (f32[128,128]{1,0:T(8,128)S(1)}, f32[128,128]{1,0:T(8,128)S(1)}, u32[]{:S(2)}, u32[]{:S(2)}) collective-permute-start(f32[128,128]{1,0:T(8,128)S(1)} %get-tuple-element.24), channel_id=1, source_target_pairs={{0,24},{1,25},{2,26},{3,27},{4,28},{5,29},{6,30},{7,31},{8,16},{9,... | collective-permute-start | bytes 196616 | tf_op jit(solution)/shard_map/ppermute | solution.py:51
  92.2 0.7 collective-permute-done.11.refs_1_
  92.9 0.0 copy-start.2
  92.9 3.3 %collective-permute-done.12.refs_2_ = f32[128,128]{1,0:T(8,128)S(1)} collective-permute-done((f32[128,128]{1,0:T(8,128)S(1)}, f32[128,128]{1,0:T(8,128)S(1)}, u32[]{:S(2)}, u32[]{:S(2)}) %collective-permute-start.12) | collective-permute-done | bytes 65568 | tf_op jit(solution)/shard_map/ppermute | solution.py:51
  96.2 0.0 copy-start.3
  96.2 0.0 collective-permute-done.13.refs_3_
  96.2 0.0 copy-start.4
  96.2 0.0 copy-done.2
  96.3 0.6 copy-done.3
  96.9 0.0 copy-done.4
  96.9 5.4 %shard_map.135 = f32[32,8,128]{2,1,0:T(8,128)} custom-call(f32[128,128]{1,0:T(8,128)} %get-tuple-element.27.refs_0_, f32[128,128]{1,0:T(8,128)} %copy-done.2, f32[128,128]{1,0:T(8,128)} %copy-done.3, f32[128,128]{1,0:T(8,128)} %copy-done.4, bf16[2,2048,1024]{2,1,0:T(8,128)(2,1)} %refs_4_.1), custom_call_target="tpu_custom_call" | custom-call | tf_op jit(solution)/shard_map/pallas_call | solution.py:483
  102.2 2.9 %all-to-all-start = ((f32[32,8,128]{2,1,0:T(8,128)}), f32[32,8,128]{2,1,0:T(8,128)S(1)}, u32[]{:S(2)}, u32[]{:S(2)}) async-start(f32[32,8,128]{2,1,0:T(8,128)} %shard_map.135), calls=%async_computation | async-start | bytes 262144 | tf_op jit(solution)/shard_map/all_to_all | solution.py:494
  105.2 8.2 %all-to-all-done = f32[32,8,128]{2,1,0:T(8,128)S(1)} async-done(((f32[32,8,128]{2,1,0:T(8,128)}), f32[32,8,128]{2,1,0:T(8,128)S(1)}, u32[]{:S(2)}, u32[]{:S(2)}) %all-to-all-start) | async-done | bytes 131104 | tf_op jit(solution)/shard_map/all_to_all | solution.py:494
  113.5 0.7 constant_dynamic-slice_fusion
  (1 shorter events, 0.0 us)
Async XLA Ops:
  2.1 5.7 %collective-permute-start = (f32[1,5,16,128]{3,2,1,0:T(8,128)}, f32[1,5,16,128]{3,2,1,0:T(8,128)S(1)}, u32[]{:S(2)}, u32[]{:S(2)}) collective-permute-start(f32[1,5,16,128]{3,2,1,0:T(8,128)} %bitcast.9), channel_id=1, source_target_pairs={{0,8},{1,9},{2,10},{3,11},{4,12},{5,13},{6,14},{7,15},{8,0},{9,1},... | collective-permute-start | bytes 122888 | tf_op jit(solution)/shard_map/ppermute | solution.py:51
  5.2 5.9 %collective-permute-start.1 = (f32[1,5,16,128]{3,2,1,0:T(8,128)}, f32[1,5,16,128]{3,2,1,0:T(8,128)S(1)}, u32[]{:S(2)}, u32[]{:S(2)}) collective-permute-start(f32[1,5,16,128]{3,2,1,0:T(8,128)} %bitcast.10), channel_id=1, source_target_pairs={{0,16},{1,17},{2,18},{3,19},{4,20},{5,21},{6,22},{7,23},{8,24},{9,... | collective-permute-start | bytes 122888 | tf_op jit(solution)/shard_map/ppermute | solution.py:51
  7.7 6.0 %collective-permute-start.2 = (f32[1,5,16,128]{3,2,1,0:T(8,128)}, f32[1,5,16,128]{3,2,1,0:T(8,128)S(1)}, u32[]{:S(2)}, u32[]{:S(2)}) collective-permute-start(f32[1,5,16,128]{3,2,1,0:T(8,128)} %bitcast.11), channel_id=1, source_target_pairs={{0,24},{1,25},{2,26},{3,27},{4,28},{5,29},{6,30},{7,31},{8,16},{9,... | collective-permute-start | bytes 122888 | tf_op jit(solution)/shard_map/ppermute | solution.py:51
  14.6 6.8 %collective-permute-start.3 = (f32[4,5,16,128]{3,2,1,0:T(8,128)S(1)}, f32[4,5,16,128]{3,2,1,0:T(8,128)S(1)}, u32[]{:S(2)}, u32[]{:S(2)}) collective-permute-start(f32[4,5,16,128]{3,2,1,0:T(8,128)S(1)} %pad_maximum_fusion.refs_0_), channel_id=1, source_target_pairs={{0,2},{1,3},{2,0},{3,1},{4,6},{5,7},{6,4},{7,5},{8,10},{9,11},{10,... | collective-permute-start | bytes 491528 | tf_op jit(solution)/shard_map/ppermute | solution.py:51
  16.1 8.2 %collective-permute-start.4 = (f32[4,5,16,128]{3,2,1,0:T(8,128)S(1)}, f32[4,5,16,128]{3,2,1,0:T(8,128)S(1)}, u32[]{:S(2)}, u32[]{:S(2)}) collective-permute-start(f32[4,5,16,128]{3,2,1,0:T(8,128)S(1)} %pad_maximum_fusion.refs_0_), channel_id=1, source_target_pairs={{0,4},{1,5},{2,6},{3,7},{4,0},{5,1},{6,2},{7,3},{8,12},{9,13},{10,... | collective-permute-start | bytes 491528 | tf_op jit(solution)/shard_map/ppermute | solution.py:51
  17.6 6.7 %collective-permute-start.5 = (f32[4,5,16,128]{3,2,1,0:T(8,128)S(1)}, f32[4,5,16,128]{3,2,1,0:T(8,128)S(1)}, u32[]{:S(2)}, u32[]{:S(2)}) collective-permute-start(f32[4,5,16,128]{3,2,1,0:T(8,128)S(1)} %pad_maximum_fusion.refs_0_), channel_id=1, source_target_pairs={{0,6},{1,7},{2,4},{3,5},{4,2},{5,3},{6,0},{7,1},{8,14},{9,15},{10,... | collective-permute-start | bytes 491528 | tf_op jit(solution)/shard_map/ppermute | solution.py:51
  26.6 2.7 %copy-start = (f32[2048,128]{1,0:T(8,128)}, f32[2048,128]{1,0:T(8,128)S(1)}, u32[]{:S(2)}) copy-start(f32[2048,128]{1,0:T(8,128)S(1)} %shard_map.133.refs_6_) | copy-start | bytes 3145732
  26.6 2.7 %collective-permute-start.6 = (f32[2048,128]{1,0:T(8,128)S(1)}, f32[2048,128]{1,0:T(8,128)S(1)}, u32[]{:S(2)}, u32[]{:S(2)}) collective-permute-start(f32[2048,128]{1,0:T(8,128)S(1)} %shard_map.133.refs_6_), channel_id=1, source_target_pairs={{0,1},{1,0},{2,3},{3,2},{4,5},{5,4},{6,7},{7,6},{8,9},{9,8},{10,11... | collective-permute-start | bytes 3145736 | tf_op jit(solution)/shard_map/ppermute | solution.py:51
  29.3 1.0 copy-start.1
  67.9 2.9 %collective-permute-start.7 = (f32[2048,128]{1,0:T(8,128)}, f32[2048,128]{1,0:T(8,128)S(1)}, u32[]{:S(2)}, u32[]{:S(2)}) collective-permute-start(f32[2048,128]{1,0:T(8,128)} %get-tuple-element.18), channel_id=1, source_target_pairs={{0,1},{1,0},{2,3},{3,2},{4,5},{5,4},{6,7},{7,6},{8,9},{9,8},{10,11... | collective-permute-start | bytes 3145736 | tf_op jit(solution)/shard_map/ppermute | solution.py:51
  72.2 10.2 %collective-permute-start.10 = (f32[512,128]{1,0:T(8,128)S(1)}, f32[512,128]{1,0:T(8,128)S(1)}, u32[]{:S(2)}, u32[]{:S(2)}) collective-permute-start(f32[512,128]{1,0:T(8,128)S(1)} %get-tuple-element.21), channel_id=1, source_target_pairs={{0,6},{1,7},{2,4},{3,5},{4,2},{5,3},{6,0},{7,1},{8,14},{9,15},{10,... | collective-permute-start | bytes 786440 | tf_op jit(solution)/shard_map/ppermute | solution.py:51
  73.1 13.6 %collective-permute-start.8 = (f32[512,128]{1,0:T(8,128)S(1)}, f32[512,128]{1,0:T(8,128)S(1)}, u32[]{:S(2)}, u32[]{:S(2)}) collective-permute-start(f32[512,128]{1,0:T(8,128)S(1)} %get-tuple-element.23), channel_id=1, source_target_pairs={{0,2},{1,3},{2,0},{3,1},{4,6},{5,7},{6,4},{7,5},{8,10},{9,11},{10,... | collective-permute-start | bytes 786440 | tf_op jit(solution)/shard_map/ppermute | solution.py:51
  74.7 12.4 %collective-permute-start.9 = (f32[512,128]{1,0:T(8,128)S(1)}, f32[512,128]{1,0:T(8,128)S(1)}, u32[]{:S(2)}, u32[]{:S(2)}) collective-permute-start(f32[512,128]{1,0:T(8,128)S(1)} %get-tuple-element.22), channel_id=1, source_target_pairs={{0,4},{1,5},{2,6},{3,7},{4,0},{5,1},{6,2},{7,3},{8,12},{9,13},{10,... | collective-permute-start | bytes 786440 | tf_op jit(solution)/shard_map/ppermute | solution.py:51
  87.8 5.1 %collective-permute-start.11 = (f32[128,128]{1,0:T(8,128)S(1)}, f32[128,128]{1,0:T(8,128)S(1)}, u32[]{:S(2)}, u32[]{:S(2)}) collective-permute-start(f32[128,128]{1,0:T(8,128)S(1)} %get-tuple-element.26), channel_id=1, source_target_pairs={{0,8},{1,9},{2,10},{3,11},{4,12},{5,13},{6,14},{7,15},{8,0},{9,1},... | collective-permute-start | bytes 196616 | tf_op jit(solution)/shard_map/ppermute | solution.py:51
  87.8 8.4 %collective-permute-start.12 = (f32[128,128]{1,0:T(8,128)S(1)}, f32[128,128]{1,0:T(8,128)S(1)}, u32[]{:S(2)}, u32[]{:S(2)}) collective-permute-start(f32[128,128]{1,0:T(8,128)S(1)} %get-tuple-element.25), channel_id=1, source_target_pairs={{0,16},{1,17},{2,18},{3,19},{4,20},{5,21},{6,22},{7,23},{8,24},{9,... | collective-permute-start | bytes 196616 | tf_op jit(solution)/shard_map/ppermute | solution.py:51
  89.1 7.2 %collective-permute-start.13 = (f32[128,128]{1,0:T(8,128)S(1)}, f32[128,128]{1,0:T(8,128)S(1)}, u32[]{:S(2)}, u32[]{:S(2)}) collective-permute-start(f32[128,128]{1,0:T(8,128)S(1)} %get-tuple-element.24), channel_id=1, source_target_pairs={{0,24},{1,25},{2,26},{3,27},{4,28},{5,29},{6,30},{7,31},{8,16},{9,... | collective-permute-start | bytes 196616 | tf_op jit(solution)/shard_map/ppermute | solution.py:51
  92.9 3.4 %copy-start.2 = (f32[128,128]{1,0:T(8,128)}, f32[128,128]{1,0:T(8,128)S(1)}, u32[]{:S(2)}) copy-start(f32[128,128]{1,0:T(8,128)S(1)} %collective-permute-done.11.refs_1_) | copy-start | bytes 196612
  96.2 0.6 copy-start.3
  96.2 0.6 copy-start.4
  102.2 11.2 %all-to-all-start = ((f32[32,8,128]{2,1,0:T(8,128)}), f32[32,8,128]{2,1,0:T(8,128)S(1)}, u32[]{:S(2)}, u32[]{:S(2)}) async-start(f32[32,8,128]{2,1,0:T(8,128)} %shard_map.135), calls=%async_computation | async-start | bytes 262144 | tf_op jit(solution)/shard_map/all_to_all | solution.py:494

commit v3 on v2

--- a/solution.py
+++ b/solution.py
@@ -9,6 +9,7 @@
 
 BOUNCES = 4
 MOST_COPIES = 8
+SLOTS = 8
 SMALL = 4 * 2**20
 LARGE = 60 * 2**20
 CHUNKS = 8
@@ -16,7 +17,6 @@
 VALUES = 8
 GROUPS = LANES // VALUES
 VMEM = pl.BlockSpec(memory_space=pltpu.VMEM)
-SMEM = pl.BlockSpec(memory_space=pltpu.SMEM)
 ANY = pl.BlockSpec(memory_space=pl.ANY)
 F32 = jnp.float32
 
@@ -190,8 +190,11 @@
     part_refs = refs[6 + shares : 6 + shares + parts]
     exit_ref = refs[6 + shares + parts]
     scratch = refs[7 + shares + parts :]
-    even, odd, even_held, odd_held, picked, fields, flat, arrive, leave = scratch[:9]
-    sums = scratch[9:]
+    buffers = [scratch[0:2], scratch[2:4]]
+    picked, fields, flat, arrive, leave, fill = scratch[4:10]
+    slots = scratch[10 : 10 + SLOTS]
+    sums = scratch[10 + SLOTS :]
+    pairs = BOUNCES * blocks // 2
     total = sums[0].shape[0]
     count = BOUNCES * blocks
 
@@ -216,12 +219,17 @@
 
     lax.fori_loop(0, total // clear, wipe, 0)
 
+    def refill(pair, q):
+        return pltpu.make_async_copy(rows_ref.at[pair], slots[q], fill.at[q])
+
+    for q in range(SLOTS):
+        refill(q, q).start()
     for load in loads:
         load.wait()
 
-    def fetch(block, into):
+    def fetch(slot, first, into):
         for u in range(LANES):
-            into[u : u + 1, :] = flat[pl.ds(rows_ref[block * LANES + u], 1), :]
+            into[u : u + 1, :] = flat[pl.ds(slot[0, first + u], 1), :]
 
     def group_of(block):
         return jnp.broadcast_to(group_ref[pl.ds(block, 1), :], (VALUES, LANES))
@@ -238,17 +246,20 @@
         picked[pl.ds(pl.multiple_of((block + 2) * VALUES, VALUES), VALUES), :] = left[0]
 
     def gather(i, carry):
-        pick(2 * i - 2, even_held)
-        pick(2 * i - 1, odd_held)
-        fetch(2 * i, even)
-        fetch(2 * i + 1, odd)
-        even_held[...] = even[...]
-        odd_held[...] = odd[...]
+        for q in range(SLOTS):
+            pair = i * SLOTS + q
+            before, now = buffers[(q + 1) % 2], buffers[q % 2]
+            refill(pair, q).wait()
+            for n in range(2):
+                pick(2 * pair - 2 + n, before[n])
+            for n in range(2):
+                fetch(slots[q], n * LANES, now[n])
+            refill(lax.rem(pair + SLOTS, pairs), q).start()
         return carry
 
-    lax.fori_loop(0, count // 2, gather, 0)
-    pick(count - 2, even_held)
-    pick(count - 1, odd_held)
+    lax.fori_loop(0, pairs // SLOTS, gather, 0)
+    for n in range(2):
+        pick(count - 2 + n, buffers[1][n])
 
     field = [field_ref[c * blocks : (c + 1) * blocks, :] for c in range(8)]
     heading = [heading_ref[c * blocks : (c + 1) * blocks, :] for c in range(3)]
@@ -272,25 +283,33 @@
         tall = jnp.concatenate([jnp.where(group == j, own, 0.0) for j in range(GROUPS)], axis=0)
         into[...] = tall.T
 
-    def add(block, source):
+    def add(slot, first, source):
         for u in range(0, LANES, copies):
             fresh = []
             for c in range(copies):
-                row = rows_ref[block * LANES + u + c]
+                row = slot[0, first + u + c]
                 fresh.append((row, sums[c][pl.ds(row, 1), :] + source[u + c : u + c + 1, :]))
             for c in range(copies):
                 sums[c][pl.ds(fresh[c][0], 1), :] = fresh[c][1]
 
-    widen(0, even)
+    for n in range(2):
+        widen(n, buffers[0][n])
 
     def scatter(i, carry):
-        widen(2 * i + 1, odd)
-        add(2 * i, even)
-        widen(jnp.minimum(2 * i + 2, count - 1), even)
-        add(2 * i + 1, odd)
+        for q in range(SLOTS):
+            pair = i * SLOTS + q
+            now, after = buffers[q % 2], buffers[(q + 1) % 2]
+            refill(pair, q).wait()
+            for n in range(2):
+                widen(jnp.minimum(2 * pair + 2, count - 2) + n, after[n])
+            for n in range(2):
+                add(slots[q], n * LANES, now[n])
+            refill(lax.rem(pair + SLOTS, pairs), q).start()
         return carry
 
-    lax.fori_loop(0, count // 2, scatter, 0)
+    lax.fori_loop(0, pairs // SLOTS, scatter, 0)
+    for q in range(SLOTS):
+        refill(q, q).wait()
 
     size = total // parts
     outs = []
@@ -313,24 +332,26 @@
         out.wait()
 
 
+def hold_kernel(source, out, arrive):
+    size = source.shape[1] // CHUNKS
+    loads = [
+        pltpu.make_async_copy(
+            source.at[h, pl.ds(i * size, size), :],
+            out.at[h, pl.ds(i * size, size), :],
+            arrive.at[i, h],
+        )
+        for i in range(CHUNKS)
+        for h in range(2)
+    ]
+    for load in loads:
+        load.start()
+    for load in loads:
+        load.wait()
+
+
 def field_kernel(meta, *refs):
-    (terms, tiles, chunks) = meta
-    kernel_ref, out, stream, arrive = refs[terms:]
-    size = kernel_ref.shape[1] // chunks
-    loads = [
-        [
-            pltpu.make_async_copy(
-                kernel_ref.at[h, pl.ds(i * size, size), :],
-                stream.at[h, pl.ds(i * size, size), :],
-                arrive.at[i, h],
-            )
-            for h in range(2)
-        ]
-        for i in range(chunks)
-    ]
-    for pair in loads:
-        for load in pair:
-            load.start()
+    (terms, tiles) = meta
+    kernel_ref, out = refs[terms:]
     total = functools.reduce(lambda a, b: a + b, [ref[...] for ref in refs[:terms]])
     depth = total.shape[0]
     rounded = []
@@ -342,14 +363,8 @@
         for m in range(depth // LANES):
             rounded.append(tall[m][j])
     left = jnp.concatenate(rounded, axis=1).astype(jnp.bfloat16)
-    real = jnp.zeros((VALUES, kernel_ref.shape[2]), F32)
-    imag = real
-    for i in range(chunks):
-        for load in loads[i]:
-            load.wait()
-        piece = left[:, i * size : (i + 1) * size]
-        real += jnp.dot(piece, stream[0, i * size : (i + 1) * size, :], preferred_element_type=F32)
-        imag += jnp.dot(piece, stream[1, i * size : (i + 1) * size, :], preferred_element_type=F32)
+    real = jnp.dot(left, kernel_ref[0], preferred_element_type=F32)
+    imag = jnp.dot(left, kernel_ref[1], preferred_element_type=F32)
     far = jnp.concatenate([real[0:4] - imag[4:8], imag[0:4] + real[4:8]], axis=0)
     count = out.shape[0]
     for i in range(count):
@@ -455,21 +470,36 @@
         functools.partial(trace_kernel, meta),
         out_shape=[jax.ShapeDtypeStruct((total // parts, LANES), F32)] * parts
         + [jax.ShapeDtypeStruct((8, tubes), F32)],
-        in_specs=[SMEM] + [VMEM] * 5 + [ANY] * len(tables),
+        in_specs=[ANY] + [VMEM] * 5 + [ANY] * len(tables),
         out_specs=[ANY] * parts + [VMEM],
         scratch_shapes=[pltpu.VMEM(*buffer) for buffer in buffers]
         + [
             pltpu.SemaphoreType.DMA((len(tables),)),
             pltpu.SemaphoreType.DMA((parts,)),
+            pltpu.SemaphoreType.DMA((SLOTS,)),
         ]
+        + [pltpu.SMEM((1, 2 * LANES), jnp.int32)] * SLOTS
         + [pltpu.VMEM(*buffer) for buffer in sum_buffers],
         compiler_params=pltpu.CompilerParams(vmem_limit_bytes=LARGE),
-    )(hit_rows.reshape(rows * LANES), *prepared, *tables)
+    )(hit_rows.reshape(rows // 2, 1, 2 * LANES), *prepared, *tables)
+
+    later, *sums = lax.optimization_barrier((kernel, *sums))
+    near = pl.pallas_call(
+        hold_kernel,
+        out_shape=jax.ShapeDtypeStruct(kernel.shape, kernel.dtype),
+        in_specs=[ANY],
+        out_specs=ANY,
+        scratch_shapes=[pltpu.SemaphoreType.DMA((CHUNKS, 2))],
+        compiler_params=pltpu.CompilerParams(vmem_limit_bytes=SMALL),
+        cost_estimate=pl.CostEstimate(flops=0, bytes_accessed=4 * kernel.size, transcendentals=0),
+    )(later)
 
     for n, phase_bits in enumerate(phases):
         terms = [sums[0]] + [
             send(sums[d], spread(d, phase_bits), axes, count) for d in range(1, len(sums))
         ]
+        if n + 2 == len(phases):
+            near, *terms = lax.optimization_barrier((near, *terms))
         if n + 1 < len(phases):
             parts = 1 << len(phases[n + 1])
             size = terms[0].shape[0] // parts
@@ -481,16 +511,12 @@
     columns = kernel.shape[2]
     tiles = columns // LANES
     partial = pl.pallas_call(
-        functools.partial(field_kernel, (len(terms), tiles, CHUNKS)),
+        functools.partial(field_kernel, (len(terms), tiles)),
         out_shape=jax.ShapeDtypeStruct((count, 8, LANES), F32),
-        in_specs=[VMEM] * len(terms) + [ANY],
+        in_specs=[VMEM] * (len(terms) + 1),
         out_specs=VMEM,
-        scratch_shapes=[
-            pltpu.VMEM(kernel.shape, kernel.dtype),
-            pltpu.SemaphoreType.DMA((CHUNKS, 2)),
-        ],
-        compiler_params=pltpu.CompilerParams(vmem_limit_bytes=LARGE),
-    )(*terms, kernel)
+        compiler_params=pltpu.CompilerParams(vmem_limit_bytes=2 * SMALL),
+    )(*terms, near)
     tile = jnp.sum(lax.all_to_all(partial, axes, 0, 0, tiled=True), axis=0)
     width = columns // count
     far_field = lax.dynamic_slice_in_dim(tile, (me & (count // tiles - 1)) * width, width, 1)

time: 115 us -> 102 us (0.89)
  Pallas kernels: 49 us -> 39 us
  waiting for transfers between devices: 38.9 us -> 32.8 us
  local copies, waits for them, and re-layouts: 2.28 us -> 5.03 us
  starting transfers between devices: 20.4 us -> 21.7 us
    pallas_call x1, Pallas kernels: 37.6 us -> 30.3 us  [body(): pl.pallas_call(functools.partial(trace_kernel, meta), out_shape=[jax.Shap...]
    ppermute x14, waiting for transfers between devices: 30.7 us -> 24.6 us  [send(): return lax.ppermute(value, axes, [(i, i ^ mask) for i in range(count)])]
    unnamed x10 -> x6, local copies, waits for them, and re-layouts: 1.61 us -> 4.36 us
    pallas_call x1 -> x2, Pallas kernels: 5.35 us -> 2.64 us  [the longest x1 1.9 us: body(): pl.pallas_call(functools.partial(field_kernel, (len(terms), tiles)), out_...]
  transfers between devices with their start and end apart: 15 -> 15, of which waited for: 12 -> 12; matrix products, arithmetic and copies ran while one was open for 0% -> 0% of each run, Pallas kernels for 2% -> 3%
where the time goes in v3:
time: 102 us; the launch traced here: 101 us
  Pallas kernels  39 us (38%)
  waiting for transfers between devices  32.8 us (32%)
  starting transfers between devices  21.7 us (21%)
  local copies, waits for them, and re-layouts  5.03 us (5%)
  other arithmetic  2.19 us (2%)
    pallas_call x1, Pallas kernels, body(): pl.pallas_call(functools.partial(trace_kernel, meta), out_shape=[jax.Shap...  30.3 us
    ppermute x14, waiting for transfers between devices, send(): return lax.ppermute(value, axes, [(i, i ^ mask) for i in range(count)])  24.6 us
    ppermute x14, starting transfers between devices, send(): return lax.ppermute(value, axes, [(i, i ^ mask) for i in range(count)])  17.6 us
    all_to_all x1, waiting for transfers between devices, body(): tile = jnp.sum(lax.all_to_all(partial, axes, 0, 0, tiled=True), axis=0)  8.22 us
    unnamed x6, local copies, waits for them, and re-layouts  4.36 us
    all_to_all x1, starting transfers between devices, body(): tile = jnp.sum(lax.all_to_all(partial, axes, 0, 0, tiled=True), axis=0)  4.08 us
    pallas_call x1, Pallas kernels, body(): pl.pallas_call(functools.partial(prepare_kernel, (owned, bins, depth, pha...  2.36 us
    pallas_call x1, Pallas kernels, body(): pl.pallas_call(functools.partial(build_kernel, depth), out_shape=jax.Shap...  2.25 us
  transfers between devices with their start and end apart: 15, of which 12 were waited for; matrix products, arithmetic and copies ran while one was open for 0% of the time, Pallas kernels for 3%

profile of v3, /device:TPU:0, one launch (start us, length us, event | category | flops | bytes accessed | tf_op | source)
XLA Modules:
  0.0 101.4 jit_solution(2737368382531826405)
XLA Ops:
  0.6 1.4 %shard_map.132 = f32[5,16,128]{2,1,0:T(8,128)} custom-call(f32[64,128]{1,0:T(8,128)} %bitcast.15, f32[64,128]{1,0:T(8,128)} %bitcast.16, f32[64,128]{1,0:T(8,128)} %bitcast.17, f32[64,128]{1,0:T(8,128)} %bitcast.18, f32[64,128]{1,0:T(8,128)} %bitcast.19), custom_call_target="tpu_custom_call" | custom-call | tf_op jit(solution)/shard_map/pallas_call | solution.py:404
  2.1 5.1 %collective-permute-start.2 = (f32[1,5,16,128]{3,2,1,0:T(8,128)}, f32[1,5,16,128]{3,2,1,0:T(8,128)S(1)}, u32[]{:S(2)}, u32[]{:S(2)}) collective-permute-start(f32[1,5,16,128]{3,2,1,0:T(8,128)} %bitcast.9), channel_id=1, source_target_pairs={{0,24},{1,25},{2,26},{3,27},{4,28},{5,29},{6,30},{7,31},{8,16},{9,... | collective-permute-start | bytes 122888 | tf_op jit(solution)/shard_map/ppermute | solution.py:51
  7.2 0.0 collective-permute-start.1
  7.2 0.6 collective-permute-start
  7.8 1.6 %collective-permute-done.2 = f32[1,5,16,128]{3,2,1,0:T(8,128)S(1)} collective-permute-done((f32[1,5,16,128]{3,2,1,0:T(8,128)}, f32[1,5,16,128]{3,2,1,0:T(8,128)S(1)}, u32[]{:S(2)}, u32[]{:S(2)}) %collective-permute-start.2) | collective-permute-done | bytes 40992 | tf_op jit(solution)/shard_map/ppermute | solution.py:51
  9.4 2.9 %collective-permute-done.1 = f32[1,5,16,128]{3,2,1,0:T(8,128)S(1)} collective-permute-done((f32[1,5,16,128]{3,2,1,0:T(8,128)}, f32[1,5,16,128]{3,2,1,0:T(8,128)S(1)}, u32[]{:S(2)}, u32[]{:S(2)}) %collective-permute-start.1) | collective-permute-done | bytes 40992 | tf_op jit(solution)/shard_map/ppermute | solution.py:51
  12.3 0.0 collective-permute-done
  12.3 0.8 pad_maximum_fusion.refs_0_
  13.1 2.5 %collective-permute-start.5 = (f32[4,5,16,128]{3,2,1,0:T(8,128)S(1)}, f32[4,5,16,128]{3,2,1,0:T(8,128)S(1)}, u32[]{:S(2)}, u32[]{:S(2)}) collective-permute-start(f32[4,5,16,128]{3,2,1,0:T(8,128)S(1)} %pad_maximum_fusion.refs_0_), channel_id=1, source_target_pairs={{0,6},{1,7},{2,4},{3,5},{4,2},{5,3},{6,0},{7,1},{8,14},{9,15},{10,... | collective-permute-start | bytes 491528 | tf_op jit(solution)/shard_map/ppermute | solution.py:51
  15.6 0.5 collective-permute-start.4
  16.1 0.5 collective-permute-start.3
  16.6 4.5 %collective-permute-done.5.refs_3_ = f32[4,5,16,128]{3,2,1,0:T(8,128)S(1)} collective-permute-done((f32[4,5,16,128]{3,2,1,0:T(8,128)S(1)}, f32[4,5,16,128]{3,2,1,0:T(8,128)S(1)}, u32[]{:S(2)}, u32[]{:S(2)}) %collective-permute-start.5) | collective-permute-done | bytes 163872 | tf_op jit(solution)/shard_map/ppermute | solution.py:51
  21.1 1.0 collective-permute-done.4.refs_2_
  22.1 0.1 collective-permute-done.3.refs_1_
  22.1 2.2 %shard_map.133.refs_6_ = f32[2048,128]{1,0:T(8,128)S(1)} custom-call(f32[4,5,16,128]{3,2,1,0:T(8,128)S(1)} %pad_maximum_fusion.refs_0_, f32[4,5,16,128]{3,2,1,0:T(8,128)S(1)} %collective-permute-done.3.refs_1_, f32[4,5,16,128]{3,2,1,0:T(8,128)S(1)} %collective-permute-done.4.refs_2_, f32[4,5,16,128]{3,2,1,0:T(8,128)S(1)} %collective-permute-done.5.refs_3_), custom_call_target="tpu_custom_call" | custom-call | tf_op jit(solution)/shard_map/pallas_call | solution.py:419
  24.4 0.0 copy-start.1
  24.4 0.1 collective-permute-start.6
  24.5 2.4 %shard_map.131 = (s32[128,128]{1,0:T(8,128)}, s32[128,128]{1,0:T(8,128)}, f32[128,128]{1,0:T(8,128)}, f32[128,128]{1,0:T(8,128)}, f32[256,128]{1,0:T(8,128)}, /*index=5*/f32[96,128]{1,0:T(8,128)}) custom-call(s32[32,128]{1,0:T(8,128)} %bitcast.20, s32[96,128]{1,0:T(8,128)} %bitcast.14, s32[4,4096]{1,0:T(4,128)} %hit.1, f32[4,4096]{1,0:T(4,128)} %angle.1, ...), custom_call_target="tpu_custom_call" | custom-call | tf_op jit(solution)/shard_map/pallas_call | solution.py:432
  26.8 0.3 collective-permute-done.6.refs_7_
  27.1 0.0 copy-start.2
  27.1 0.0 copy-done.1
  27.1 1.0 copy-done.2
  28.1 30.3 %shard_map.134 = (f32[2048,128]{1,0:T(8,128)}, f32[2048,128]{1,0:T(8,128)}, f32[8,4096]{1,0:T(8,128)}) custom-call(s32[64,1,256]{2,1,0:T(1,128)} %bitcast.13, s32[128,128]{1,0:T(8,128)} %get-tuple-element.20.refs_1_, f32[128,128]{1,0:T(8,128)} %get-tuple-element.21.refs_2_, f32[128,128]{1,0:T(8,128)} %get-tuple-element.22.refs_3_, ...), custom_call_target="tpu_custom_call" | custom-call | tf_op jit(solution)/shard_map/pallas_call | solution.py:469
  58.5 0.2 collective-permute-start.7
  58.7 2.7 %collective-permute-done.7 = f32[2048,128]{1,0:T(8,128)S(1)} collective-permute-done((f32[2048,128]{1,0:T(8,128)}, f32[2048,128]{1,0:T(8,128)S(1)}, u32[]{:S(2)}, u32[]{:S(2)}) %collective-permute-start.7) | collective-permute-done | bytes 1048608 | tf_op jit(solution)/shard_map/ppermute | solution.py:51
  61.4 1.3 %slice_add_fusion = (f32[512,128]{1,0:T(8,128)S(1)}, f32[512,128]{1,0:T(8,128)S(1)}, f32[512,128]{1,0:T(8,128)S(1)}, f32[512,128]{1,0:T(8,128)S(1)}) fusion(f32[2048,128]{1,0:T(8,128)S(1)} %collective-permute-done.7, f32[2048,128]{1,0:T(8,128)} %get-tuple-element.28), kind=kLoop, calls=%fused_computation | loop fusion | flops 262144 | bytes 3145728 | tf_op jit(solution)/shard_map/add | solution.py:507
  62.7 1.7 %collective-permute-start.10 = (f32[512,128]{1,0:T(8,128)S(1)}, f32[512,128]{1,0:T(8,128)S(1)}, u32[]{:S(2)}, u32[]{:S(2)}) collective-permute-start(f32[512,128]{1,0:T(8,128)S(1)} %get-tuple-element.36), channel_id=1, source_target_pairs={{0,6},{1,7},{2,4},{3,5},{4,2},{5,3},{6,0},{7,1},{8,14},{9,15},{10,... | collective-permute-start | bytes 786440 | tf_op jit(solution)/shard_map/ppermute | solution.py:51
  64.4 1.3 %collective-permute-start.9 = (f32[512,128]{1,0:T(8,128)S(1)}, f32[512,128]{1,0:T(8,128)S(1)}, u32[]{:S(2)}, u32[]{:S(2)}) collective-permute-start(f32[512,128]{1,0:T(8,128)S(1)} %get-tuple-element.37), channel_id=1, source_target_pairs={{0,4},{1,5},{2,6},{3,7},{4,0},{5,1},{6,2},{7,3},{8,12},{9,13},{10,... | collective-permute-start | bytes 786440 | tf_op jit(solution)/shard_map/ppermute | solution.py:51
  65.7 0.5 collective-permute-start.8
  66.2 0.0 copy-start
  66.2 3.4 %copy-done = bf16[2,2048,1024]{2,1,0:T(8,128)(2,1)S(1)} copy-done((bf16[2,2048,1024]{2,1,0:T(8,128)(2,1)S(1)}, bf16[2,2048,1024]{2,1,0:T(8,128)(2,1)}, u32[]{:S(2)}) %copy-start) | copy-done | bytes 8388632
  69.6 0.7 shard_map.135.refs_4_
  70.4 2.5 %collective-permute-done.10 = f32[512,128]{1,0:T(8,128)S(1)} collective-permute-done((f32[512,128]{1,0:T(8,128)S(1)}, f32[512,128]{1,0:T(8,128)S(1)}, u32[]{:S(2)}, u32[]{:S(2)}) %collective-permute-start.10) | collective-permute-done | bytes 262176 | tf_op jit(solution)/shard_map/ppermute | solution.py:51
  72.8 4.8 %collective-permute-done.9 = f32[512,128]{1,0:T(8,128)S(1)} collective-permute-done((f32[512,128]{1,0:T(8,128)S(1)}, f32[512,128]{1,0:T(8,128)S(1)}, u32[]{:S(2)}, u32[]{:S(2)}) %collective-permute-start.9) | collective-permute-done | bytes 262176 | tf_op jit(solution)/shard_map/ppermute | solution.py:51
  77.6 0.0 collective-permute-done.8
  77.6 0.1 slice_add_fusion.4
  77.7 2.1 %collective-permute-start.13 = (f32[128,128]{1,0:T(8,128)S(1)}, f32[128,128]{1,0:T(8,128)S(1)}, u32[]{:S(2)}, u32[]{:S(2)}) collective-permute-start(f32[128,128]{1,0:T(8,128)S(1)} %get-tuple-element.40), channel_id=1, source_target_pairs={{0,24},{1,25},{2,26},{3,27},{4,28},{5,29},{6,30},{7,31},{8,16},{9,... | collective-permute-start | bytes 196616 | tf_op jit(solution)/shard_map/ppermute | solution.py:51
  79.8 0.1 collective-permute-start.12
  79.9 2.3 %collective-permute-start.11 = (f32[128,128]{1,0:T(8,128)S(1)}, f32[128,128]{1,0:T(8,128)S(1)}, u32[]{:S(2)}, u32[]{:S(2)}) collective-permute-start(f32[128,128]{1,0:T(8,128)S(1)} %get-tuple-element.42), channel_id=1, source_target_pairs={{0,8},{1,9},{2,10},{3,11},{4,12},{5,13},{6,14},{7,15},{8,0},{9,1},... | collective-permute-start | bytes 196616 | tf_op jit(solution)/shard_map/ppermute | solution.py:51
  82.2 2.4 %collective-permute-done.13.refs_3_ = f32[128,128]{1,0:T(8,128)S(1)} collective-permute-done((f32[128,128]{1,0:T(8,128)S(1)}, f32[128,128]{1,0:T(8,128)S(1)}, u32[]{:S(2)}, u32[]{:S(2)}) %collective-permute-start.13) | collective-permute-done | bytes 65568 | tf_op jit(solution)/shard_map/ppermute | solution.py:51
  84.6 1.9 %collective-permute-done.12.refs_2_ = f32[128,128]{1,0:T(8,128)S(1)} collective-permute-done((f32[128,128]{1,0:T(8,128)S(1)}, f32[128,128]{1,0:T(8,128)S(1)}, u32[]{:S(2)}, u32[]{:S(2)}) %collective-permute-start.12) | collective-permute-done | bytes 65568 | tf_op jit(solution)/shard_map/ppermute | solution.py:51
  86.5 0.0 collective-permute-done.11.refs_1_
  86.5 1.9 %shard_map.136 = f32[32,8,128]{2,1,0:T(8,128)} custom-call(f32[128,128]{1,0:T(8,128)S(1)} %get-tuple-element.43.refs_0_, f32[128,128]{1,0:T(8,128)S(1)} %collective-permute-done.11.refs_1_, f32[128,128]{1,0:T(8,128)S(1)} %collective-permute-done.12.refs_2_, f32[128,128]{1,0:T(8,128)S(1)} %collective-permute-done.13.refs_3_, ...), custom_call_target="tpu_custom_call" | custom-call | tf_op jit(solution)/shard_map/pallas_call | solution.py:513
  88.4 4.1 %all-to-all-start = ((f32[32,8,128]{2,1,0:T(8,128)}), f32[32,8,128]{2,1,0:T(8,128)S(1)}, u32[]{:S(2)}, u32[]{:S(2)}) async-start(f32[32,8,128]{2,1,0:T(8,128)} %shard_map.136), calls=%async_computation | async-start | bytes 262144 | tf_op jit(solution)/shard_map/all_to_all | solution.py:520
  92.5 8.2 %all-to-all-done = f32[32,8,128]{2,1,0:T(8,128)S(1)} async-done(((f32[32,8,128]{2,1,0:T(8,128)}), f32[32,8,128]{2,1,0:T(8,128)S(1)}, u32[]{:S(2)}, u32[]{:S(2)}) %all-to-all-start) | async-done | bytes 131104 | tf_op jit(solution)/shard_map/all_to_all | solution.py:520
  100.7 0.7 constant_dynamic-slice_fusion
  (1 shorter events, 0.0 us)
Async XLA Ops:
  2.1 7.3 %collective-permute-start.2 = (f32[1,5,16,128]{3,2,1,0:T(8,128)}, f32[1,5,16,128]{3,2,1,0:T(8,128)S(1)}, u32[]{:S(2)}, u32[]{:S(2)}) collective-permute-start(f32[1,5,16,128]{3,2,1,0:T(8,128)} %bitcast.9), channel_id=1, source_target_pairs={{0,24},{1,25},{2,26},{3,27},{4,28},{5,29},{6,30},{7,31},{8,16},{9,... | collective-permute-start | bytes 122888 | tf_op jit(solution)/shard_map/ppermute | solution.py:51
  7.2 5.1 %collective-permute-start.1 = (f32[1,5,16,128]{3,2,1,0:T(8,128)}, f32[1,5,16,128]{3,2,1,0:T(8,128)S(1)}, u32[]{:S(2)}, u32[]{:S(2)}) collective-permute-start(f32[1,5,16,128]{3,2,1,0:T(8,128)} %bitcast.10), channel_id=1, source_target_pairs={{0,16},{1,17},{2,18},{3,19},{4,20},{5,21},{6,22},{7,23},{8,24},{9,... | collective-permute-start | bytes 122888 | tf_op jit(solution)/shard_map/ppermute | solution.py:51
  7.2 5.1 %collective-permute-start = (f32[1,5,16,128]{3,2,1,0:T(8,128)}, f32[1,5,16,128]{3,2,1,0:T(8,128)S(1)}, u32[]{:S(2)}, u32[]{:S(2)}) collective-permute-start(f32[1,5,16,128]{3,2,1,0:T(8,128)} %bitcast.11), channel_id=1, source_target_pairs={{0,8},{1,9},{2,10},{3,11},{4,12},{5,13},{6,14},{7,15},{8,0},{9,1},... | collective-permute-start | bytes 122888 | tf_op jit(solution)/shard_map/ppermute | solution.py:51
  13.1 8.0 %collective-permute-start.5 = (f32[4,5,16,128]{3,2,1,0:T(8,128)S(1)}, f32[4,5,16,128]{3,2,1,0:T(8,128)S(1)}, u32[]{:S(2)}, u32[]{:S(2)}) collective-permute-start(f32[4,5,16,128]{3,2,1,0:T(8,128)S(1)} %pad_maximum_fusion.refs_0_), channel_id=1, source_target_pairs={{0,6},{1,7},{2,4},{3,5},{4,2},{5,3},{6,0},{7,1},{8,14},{9,15},{10,... | collective-permute-start | bytes 491528 | tf_op jit(solution)/shard_map/ppermute | solution.py:51
  15.6 6.5 %collective-permute-start.4 = (f32[4,5,16,128]{3,2,1,0:T(8,128)S(1)}, f32[4,5,16,128]{3,2,1,0:T(8,128)S(1)}, u32[]{:S(2)}, u32[]{:S(2)}) collective-permute-start(f32[4,5,16,128]{3,2,1,0:T(8,128)S(1)} %pad_maximum_fusion.refs_0_), channel_id=1, source_target_pairs={{0,4},{1,5},{2,6},{3,7},{4,0},{5,1},{6,2},{7,3},{8,12},{9,13},{10,... | collective-permute-start | bytes 491528 | tf_op jit(solution)/shard_map/ppermute | solution.py:51
  16.1 6.0 %collective-permute-start.3 = (f32[4,5,16,128]{3,2,1,0:T(8,128)S(1)}, f32[4,5,16,128]{3,2,1,0:T(8,128)S(1)}, u32[]{:S(2)}, u32[]{:S(2)}) collective-permute-start(f32[4,5,16,128]{3,2,1,0:T(8,128)S(1)} %pad_maximum_fusion.refs_0_), channel_id=1, source_target_pairs={{0,2},{1,3},{2,0},{3,1},{4,6},{5,7},{6,4},{7,5},{8,10},{9,11},{10,... | collective-permute-start | bytes 491528 | tf_op jit(solution)/shard_map/ppermute | solution.py:51
  24.4 2.7 %copy-start.1 = (f32[2048,128]{1,0:T(8,128)}, f32[2048,128]{1,0:T(8,128)S(1)}, u32[]{:S(2)}) copy-start(f32[2048,128]{1,0:T(8,128)S(1)} %shard_map.133.refs_6_) | copy-start | bytes 3145732
  24.4 2.7 %collective-permute-start.6 = (f32[2048,128]{1,0:T(8,128)S(1)}, f32[2048,128]{1,0:T(8,128)S(1)}, u32[]{:S(2)}, u32[]{:S(2)}) collective-permute-start(f32[2048,128]{1,0:T(8,128)S(1)} %shard_map.133.refs_6_), channel_id=1, source_target_pairs={{0,1},{1,0},{2,3},{3,2},{4,5},{5,4},{6,7},{7,6},{8,9},{9,8},{10,11... | collective-permute-start | bytes 3145736 | tf_op jit(solution)/shard_map/ppermute | solution.py:51
  27.1 1.0 copy-start.2
  58.5 2.9 %collective-permute-start.7 = (f32[2048,128]{1,0:T(8,128)}, f32[2048,128]{1,0:T(8,128)S(1)}, u32[]{:S(2)}, u32[]{:S(2)}) collective-permute-start(f32[2048,128]{1,0:T(8,128)} %get-tuple-element.29), channel_id=1, source_target_pairs={{0,1},{1,0},{2,3},{3,2},{4,5},{5,4},{6,7},{7,6},{8,9},{9,8},{10,11... | collective-permute-start | bytes 3145736 | tf_op jit(solution)/shard_map/ppermute | solution.py:51
  62.7 10.2 %collective-permute-start.10 = (f32[512,128]{1,0:T(8,128)S(1)}, f32[512,128]{1,0:T(8,128)S(1)}, u32[]{:S(2)}, u32[]{:S(2)}) collective-permute-start(f32[512,128]{1,0:T(8,128)S(1)} %get-tuple-element.36), channel_id=1, source_target_pairs={{0,6},{1,7},{2,4},{3,5},{4,2},{5,3},{6,0},{7,1},{8,14},{9,15},{10,... | collective-permute-start | bytes 786440 | tf_op jit(solution)/shard_map/ppermute | solution.py:51
  64.4 13.2 %collective-permute-start.9 = (f32[512,128]{1,0:T(8,128)S(1)}, f32[512,128]{1,0:T(8,128)S(1)}, u32[]{:S(2)}, u32[]{:S(2)}) collective-permute-start(f32[512,128]{1,0:T(8,128)S(1)} %get-tuple-element.37), channel_id=1, source_target_pairs={{0,4},{1,5},{2,6},{3,7},{4,0},{5,1},{6,2},{7,3},{8,12},{9,13},{10,... | collective-permute-start | bytes 786440 | tf_op jit(solution)/shard_map/ppermute | solution.py:51
  65.7 11.9 %collective-permute-start.8 = (f32[512,128]{1,0:T(8,128)S(1)}, f32[512,128]{1,0:T(8,128)S(1)}, u32[]{:S(2)}, u32[]{:S(2)}) collective-permute-start(f32[512,128]{1,0:T(8,128)S(1)} %get-tuple-element.38), channel_id=1, source_target_pairs={{0,2},{1,3},{2,0},{3,1},{4,6},{5,7},{6,4},{7,5},{8,10},{9,11},{10,... | collective-permute-start | bytes 786440 | tf_op jit(solution)/shard_map/ppermute | solution.py:51
  66.2 3.4 %copy-start = (bf16[2,2048,1024]{2,1,0:T(8,128)(2,1)S(1)}, bf16[2,2048,1024]{2,1,0:T(8,128)(2,1)}, u32[]{:S(2)}) copy-start(bf16[2,2048,1024]{2,1,0:T(8,128)(2,1)} %source) | copy-start | bytes 25165828
  77.7 6.9 %collective-permute-start.13 = (f32[128,128]{1,0:T(8,128)S(1)}, f32[128,128]{1,0:T(8,128)S(1)}, u32[]{:S(2)}, u32[]{:S(2)}) collective-permute-start(f32[128,128]{1,0:T(8,128)S(1)} %get-tuple-element.40), channel_id=1, source_target_pairs={{0,24},{1,25},{2,26},{3,27},{4,28},{5,29},{6,30},{7,31},{8,16},{9,... | collective-permute-start | bytes 196616 | tf_op jit(solution)/shard_map/ppermute | solution.py:51
  79.8 6.7 %collective-permute-start.12 = (f32[128,128]{1,0:T(8,128)S(1)}, f32[128,128]{1,0:T(8,128)S(1)}, u32[]{:S(2)}, u32[]{:S(2)}) collective-permute-start(f32[128,128]{1,0:T(8,128)S(1)} %get-tuple-element.41), channel_id=1, source_target_pairs={{0,16},{1,17},{2,18},{3,19},{4,20},{5,21},{6,22},{7,23},{8,24},{9,... | collective-permute-start | bytes 196616 | tf_op jit(solution)/shard_map/ppermute | solution.py:51
  79.9 6.6 %collective-permute-start.11 = (f32[128,128]{1,0:T(8,128)S(1)}, f32[128,128]{1,0:T(8,128)S(1)}, u32[]{:S(2)}, u32[]{:S(2)}) collective-permute-start(f32[128,128]{1,0:T(8,128)S(1)} %get-tuple-element.42), channel_id=1, source_target_pairs={{0,8},{1,9},{2,10},{3,11},{4,12},{5,13},{6,14},{7,15},{8,0},{9,1},... | collective-permute-start | bytes 196616 | tf_op jit(solution)/shard_map/ppermute | solution.py:51
  88.4 12.3 %all-to-all-start = ((f32[32,8,128]{2,1,0:T(8,128)}), f32[32,8,128]{2,1,0:T(8,128)S(1)}, u32[]{:S(2)}, u32[]{:S(2)}) async-start(f32[32,8,128]{2,1,0:T(8,128)} %shard_map.136), calls=%async_computation | async-start | bytes 262144 | tf_op jit(solution)/shard_map/all_to_all | solution.py:520

commit v4 on v3

--- a/solution.py
+++ b/solution.py
@@ -185,7 +185,7 @@
 
 def trace_kernel(meta, *refs):
     (blocks, shares, parts, copies) = meta
-    rows_ref, group_ref, sine_ref, cosine_ref, field_ref, heading_ref = refs[:6]
+    rows_ref, *given = refs[:6]
     share_refs = refs[6 : 6 + shares]
     part_refs = refs[6 + shares : 6 + shares + parts]
     exit_ref = refs[6 + shares + parts]
@@ -193,7 +193,9 @@
     buffers = [scratch[0:2], scratch[2:4]]
     picked, fields, flat, arrive, leave, fill = scratch[4:10]
     slots = scratch[10 : 10 + SLOTS]
-    sums = scratch[10 + SLOTS :]
+    exit_held, entering, *inner = scratch[10 + SLOTS : 17 + SLOTS]
+    group_ref, sine_ref, cosine_ref, field_ref, heading_ref = inner
+    sums = scratch[17 + SLOTS :]
     pairs = BOUNCES * blocks // 2
     total = sums[0].shape[0]
     count = BOUNCES * blocks
@@ -208,6 +210,11 @@
     ]
     for load in loads:
         load.start()
+    enters = [pltpu.make_async_copy(given[i], inner[i], entering.at[i]) for i in range(5)]
+    for enter in enters:
+        enter.start()
+    for q in range(SLOTS):
+        pltpu.make_async_copy(rows_ref.at[q], slots[q], fill.at[q]).start()
 
     clear = 64
     zeros = jnp.zeros((clear, LANES), F32)
@@ -222,10 +229,9 @@
     def refill(pair, q):
         return pltpu.make_async_copy(rows_ref.at[pair], slots[q], fill.at[q])
 
-    for q in range(SLOTS):
-        refill(q, q).start()
     for load in loads:
         load.wait()
+    enters[0].wait()
 
     def fetch(slot, first, into):
         for u in range(LANES):
@@ -261,6 +267,8 @@
     for n in range(2):
         pick(count - 2 + n, buffers[1][n])
 
+    for enter in enters[1:]:
+        enter.wait()
     field = [field_ref[c * blocks : (c + 1) * blocks, :] for c in range(8)]
     heading = [heading_ref[c * blocks : (c + 1) * blocks, :] for c in range(3)]
     for bounce in range(BOUNCES):
@@ -273,9 +281,11 @@
         for c in range(VALUES):
             fields[bounce, c * blocks : (c + 1) * blocks, :] = field[c]
     for k in range(blocks):
-        exit_ref[:, k * LANES : (k + 1) * LANES] = fields[
+        exit_held[:, k * LANES : (k + 1) * LANES] = fields[
             BOUNCES - 1, pl.ds(k, VALUES, stride=blocks), :
         ]
+    leaving = pltpu.make_async_copy(exit_held, exit_ref, entering.at[5])
+    leaving.start()
 
     def widen(block, into):
         own = fields[block // blocks, pl.ds(block % blocks, VALUES, stride=blocks), :]
@@ -285,12 +295,11 @@
 
     def add(slot, first, source):
         for u in range(0, LANES, copies):
-            fresh = []
+            at = [slot[0, first + u + c] for c in range(copies)]
+            fresh = [sums[c][pl.ds(at[c], 1), :] for c in range(copies)]
+            extra = [source[u + c : u + c + 1, :] for c in range(copies)]
             for c in range(copies):
-                row = slot[0, first + u + c]
-                fresh.append((row, sums[c][pl.ds(row, 1), :] + source[u + c : u + c + 1, :]))
-            for c in range(copies):
-                sums[c][pl.ds(fresh[c][0], 1), :] = fresh[c][1]
+                sums[c][pl.ds(at[c], 1), :] = fresh[c] + extra[c]
 
     for n in range(2):
         widen(n, buffers[0][n])
@@ -330,6 +339,7 @@
         outs[-1].start()
     for out in outs:
         out.wait()
+    leaving.wait()
 
 
 def hold_kernel(source, out, arrive):
@@ -453,7 +463,7 @@
     )
 
     copies = 1
-    while copies < MOST_COPIES and copies * 2 * total * LANES * 4 <= 16 * 2**20:
+    while copies < MOST_COPIES and copies * 2 * total * LANES * 4 <= 32 * 2**20:
         copies *= 2
     meta = (blocks, len(tables), parts, copies)
     buffers = [
@@ -470,8 +480,8 @@
         functools.partial(trace_kernel, meta),
         out_shape=[jax.ShapeDtypeStruct((total // parts, LANES), F32)] * parts
         + [jax.ShapeDtypeStruct((8, tubes), F32)],
-        in_specs=[ANY] + [VMEM] * 5 + [ANY] * len(tables),
-        out_specs=[ANY] * parts + [VMEM],
+        in_specs=[ANY] * (6 + len(tables)),
+        out_specs=[ANY] * (parts + 1),
         scratch_shapes=[pltpu.VMEM(*buffer) for buffer in buffers]
         + [
             pltpu.SemaphoreType.DMA((len(tables),)),
@@ -479,6 +489,8 @@
             pltpu.SemaphoreType.DMA((SLOTS,)),
         ]
         + [pltpu.SMEM((1, 2 * LANES), jnp.int32)] * SLOTS
+        + [pltpu.VMEM((8, tubes), F32), pltpu.SemaphoreType.DMA((6,))]
+        + [pltpu.VMEM(value.shape, value.dtype) for value in prepared]
         + [pltpu.VMEM(*buffer) for buffer in sum_buffers],
         compiler_params=pltpu.CompilerParams(vmem_limit_bytes=LARGE),
     )(hit_rows.reshape(rows // 2, 1, 2 * LANES), *prepared, *tables)

time: 102 us -> 99.8 us (0.978)
  Pallas kernels: 39 us -> 37 us
    pallas_call x1, Pallas kernels: 30.3 us -> 28.3 us  [body(): pl.pallas_call(functools.partial(trace_kernel, meta), out_shape=[jax.Shap...]
  transfers between devices with their start and end apart: 15 -> 15, of which waited for: 12 -> 13; matrix products, arithmetic and copies ran while one was open for 0% -> 0% of each run, Pallas kernels for 3% -> 3%
where the time goes in v4:
time: 99.8 us; the launch traced here: 99.4 us
  Pallas kernels  37 us (37%)
  waiting for transfers between devices  32.8 us (33%)
  starting transfers between devices  21.7 us (22%)
  local copies, waits for them, and re-layouts  5.03 us (5%)
  other arithmetic  2.19 us (2%)
    pallas_call x1, Pallas kernels, body(): pl.pallas_call(functools.partial(trace_kernel, meta), out_shape=[jax.Shap...  28.3 us
    ppermute x14, waiting for transfers between devices, send(): return lax.ppermute(value, axes, [(i, i ^ mask) for i in range(count)])  24.6 us
    ppermute x14, starting transfers between devices, send(): return lax.ppermute(value, axes, [(i, i ^ mask) for i in range(count)])  17.6 us
    all_to_all x1, waiting for transfers between devices, body(): tile = jnp.sum(lax.all_to_all(partial, axes, 0, 0, tiled=True), axis=0)  8.22 us
    unnamed x6, local copies, waits for them, and re-layouts  4.36 us
    all_to_all x1, starting transfers between devices, body(): tile = jnp.sum(lax.all_to_all(partial, axes, 0, 0, tiled=True), axis=0)  4.1 us
    pallas_call x1, Pallas kernels, body(): pl.pallas_call(functools.partial(prepare_kernel, (owned, bins, depth, pha...  2.36 us
    pallas_call x1, Pallas kernels, body(): pl.pallas_call(functools.partial(build_kernel, depth), out_shape=jax.Shap...  2.25 us
  transfers between devices with their start and end apart: 15, of which 13 were waited for; matrix products, arithmetic and copies ran while one was open for 0% of the time, Pallas kernels for 3%

profile of v4, /device:TPU:0, one launch (start us, length us, event | category | flops | bytes accessed | tf_op | source)
XLA Modules:
  0.0 99.4 jit_solution(18049823908582640480)
XLA Ops:
  0.6 1.4 %shard_map.132 = f32[5,16,128]{2,1,0:T(8,128)} custom-call(f32[64,128]{1,0:T(8,128)} %bitcast.15, f32[64,128]{1,0:T(8,128)} %bitcast.16, f32[64,128]{1,0:T(8,128)} %bitcast.17, f32[64,128]{1,0:T(8,128)} %bitcast.18, f32[64,128]{1,0:T(8,128)} %bitcast.19), custom_call_target="tpu_custom_call" | custom-call | tf_op jit(solution)/shard_map/pallas_call | solution.py:414
  2.1 5.1 %collective-permute-start.2 = (f32[1,5,16,128]{3,2,1,0:T(8,128)}, f32[1,5,16,128]{3,2,1,0:T(8,128)S(1)}, u32[]{:S(2)}, u32[]{:S(2)}) collective-permute-start(f32[1,5,16,128]{3,2,1,0:T(8,128)} %bitcast.9), channel_id=1, source_target_pairs={{0,24},{1,25},{2,26},{3,27},{4,28},{5,29},{6,30},{7,31},{8,16},{9,... | collective-permute-start | bytes 122888 | tf_op jit(solution)/shard_map/ppermute | solution.py:51
  7.2 0.0 collective-permute-start.1
  7.2 0.6 collective-permute-start
  7.8 1.6 %collective-permute-done.2 = f32[1,5,16,128]{3,2,1,0:T(8,128)S(1)} collective-permute-done((f32[1,5,16,128]{3,2,1,0:T(8,128)}, f32[1,5,16,128]{3,2,1,0:T(8,128)S(1)}, u32[]{:S(2)}, u32[]{:S(2)}) %collective-permute-start.2) | collective-permute-done | bytes 40992 | tf_op jit(solution)/shard_map/ppermute | solution.py:51
  9.4 2.9 %collective-permute-done.1 = f32[1,5,16,128]{3,2,1,0:T(8,128)S(1)} collective-permute-done((f32[1,5,16,128]{3,2,1,0:T(8,128)}, f32[1,5,16,128]{3,2,1,0:T(8,128)S(1)}, u32[]{:S(2)}, u32[]{:S(2)}) %collective-permute-start.1) | collective-permute-done | bytes 40992 | tf_op jit(solution)/shard_map/ppermute | solution.py:51
  12.3 0.0 collective-permute-done
  12.3 0.8 pad_maximum_fusion.refs_0_
  13.1 2.5 %collective-permute-start.5 = (f32[4,5,16,128]{3,2,1,0:T(8,128)S(1)}, f32[4,5,16,128]{3,2,1,0:T(8,128)S(1)}, u32[]{:S(2)}, u32[]{:S(2)}) collective-permute-start(f32[4,5,16,128]{3,2,1,0:T(8,128)S(1)} %pad_maximum_fusion.refs_0_), channel_id=1, source_target_pairs={{0,6},{1,7},{2,4},{3,5},{4,2},{5,3},{6,0},{7,1},{8,14},{9,15},{10,... | collective-permute-start | bytes 491528 | tf_op jit(solution)/shard_map/ppermute | solution.py:51
  15.6 0.5 collective-permute-start.4
  16.1 0.5 collective-permute-start.3
  16.6 4.5 %collective-permute-done.5.refs_3_ = f32[4,5,16,128]{3,2,1,0:T(8,128)S(1)} collective-permute-done((f32[4,5,16,128]{3,2,1,0:T(8,128)S(1)}, f32[4,5,16,128]{3,2,1,0:T(8,128)S(1)}, u32[]{:S(2)}, u32[]{:S(2)}) %collective-permute-start.5) | collective-permute-done | bytes 163872 | tf_op jit(solution)/shard_map/ppermute | solution.py:51
  21.1 1.0 collective-permute-done.4.refs_2_
  22.1 0.1 collective-permute-done.3.refs_1_
  22.1 2.2 %shard_map.133.refs_6_ = f32[2048,128]{1,0:T(8,128)S(1)} custom-call(f32[4,5,16,128]{3,2,1,0:T(8,128)S(1)} %pad_maximum_fusion.refs_0_, f32[4,5,16,128]{3,2,1,0:T(8,128)S(1)} %collective-permute-done.3.refs_1_, f32[4,5,16,128]{3,2,1,0:T(8,128)S(1)} %collective-permute-done.4.refs_2_, f32[4,5,16,128]{3,2,1,0:T(8,128)S(1)} %collective-permute-done.5.refs_3_), custom_call_target="tpu_custom_call" | custom-call | tf_op jit(solution)/shard_map/pallas_call | solution.py:429
  24.4 0.0 copy-start.1
  24.4 0.1 collective-permute-start.6
  24.5 2.4 %shard_map.131 = (s32[128,128]{1,0:T(8,128)}, s32[128,128]{1,0:T(8,128)}, f32[128,128]{1,0:T(8,128)}, f32[128,128]{1,0:T(8,128)}, f32[256,128]{1,0:T(8,128)}, /*index=5*/f32[96,128]{1,0:T(8,128)}) custom-call(s32[32,128]{1,0:T(8,128)} %bitcast.20, s32[96,128]{1,0:T(8,128)} %bitcast.14, s32[4,4096]{1,0:T(4,128)} %hit.1, f32[4,4096]{1,0:T(4,128)} %angle.1, ...), custom_call_target="tpu_custom_call" | custom-call | tf_op jit(solution)/shard_map/pallas_call | solution.py:442
  26.8 0.3 collective-permute-done.6.refs_7_
  27.1 0.0 copy-start.2
  27.1 0.0 copy-done.1
  27.1 1.0 copy-done.2
  28.1 28.3 %shard_map.134 = (f32[2048,128]{1,0:T(8,128)}, f32[2048,128]{1,0:T(8,128)}, f32[8,4096]{1,0:T(8,128)}) custom-call(s32[64,1,256]{2,1,0:T(1,128)} %bitcast.13, s32[128,128]{1,0:T(8,128)} %get-tuple-element.20.refs_1_, f32[128,128]{1,0:T(8,128)} %get-tuple-element.21.refs_2_, f32[128,128]{1,0:T(8,128)} %get-tuple-element.22.refs_3_, ...), custom_call_target="tpu_custom_call" | custom-call | tf_op jit(solution)/shard_map/pallas_call | solution.py:479
  56.4 0.2 collective-permute-start.7
  56.6 2.7 %collective-permute-done.7 = f32[2048,128]{1,0:T(8,128)S(1)} collective-permute-done((f32[2048,128]{1,0:T(8,128)}, f32[2048,128]{1,0:T(8,128)S(1)}, u32[]{:S(2)}, u32[]{:S(2)}) %collective-permute-start.7) | collective-permute-done | bytes 1048608 | tf_op jit(solution)/shard_map/ppermute | solution.py:51
  59.3 1.3 %slice_add_fusion = (f32[512,128]{1,0:T(8,128)S(1)}, f32[512,128]{1,0:T(8,128)S(1)}, f32[512,128]{1,0:T(8,128)S(1)}, f32[512,128]{1,0:T(8,128)S(1)}) fusion(f32[2048,128]{1,0:T(8,128)S(1)} %collective-permute-done.7, f32[2048,128]{1,0:T(8,128)} %get-tuple-element.28), kind=kLoop, calls=%fused_computation | loop fusion | flops 262144 | bytes 3145728 | tf_op jit(solution)/shard_map/add | solution.py:519
  60.6 1.8 %collective-permute-start.10 = (f32[512,128]{1,0:T(8,128)S(1)}, f32[512,128]{1,0:T(8,128)S(1)}, u32[]{:S(2)}, u32[]{:S(2)}) collective-permute-start(f32[512,128]{1,0:T(8,128)S(1)} %get-tuple-element.36), channel_id=1, source_target_pairs={{0,6},{1,7},{2,4},{3,5},{4,2},{5,3},{6,0},{7,1},{8,14},{9,15},{10,... | collective-permute-start | bytes 786440 | tf_op jit(solution)/shard_map/ppermute | solution.py:51
  62.4 1.3 %collective-permute-start.9 = (f32[512,128]{1,0:T(8,128)S(1)}, f32[512,128]{1,0:T(8,128)S(1)}, u32[]{:S(2)}, u32[]{:S(2)}) collective-permute-start(f32[512,128]{1,0:T(8,128)S(1)} %get-tuple-element.37), channel_id=1, source_target_pairs={{0,4},{1,5},{2,6},{3,7},{4,0},{5,1},{6,2},{7,3},{8,12},{9,13},{10,... | collective-permute-start | bytes 786440 | tf_op jit(solution)/shard_map/ppermute | solution.py:51
  63.7 0.5 collective-permute-start.8
  64.2 0.0 copy-start
  64.2 3.4 %copy-done = bf16[2,2048,1024]{2,1,0:T(8,128)(2,1)S(1)} copy-done((bf16[2,2048,1024]{2,1,0:T(8,128)(2,1)S(1)}, bf16[2,2048,1024]{2,1,0:T(8,128)(2,1)}, u32[]{:S(2)}) %copy-start) | copy-done | bytes 8388632
  67.6 0.7 shard_map.135.refs_4_
  68.3 2.5 %collective-permute-done.10 = f32[512,128]{1,0:T(8,128)S(1)} collective-permute-done((f32[512,128]{1,0:T(8,128)S(1)}, f32[512,128]{1,0:T(8,128)S(1)}, u32[]{:S(2)}, u32[]{:S(2)}) %collective-permute-start.10) | collective-permute-done | bytes 262176 | tf_op jit(solution)/shard_map/ppermute | solution.py:51
  70.8 4.8 %collective-permute-done.9 = f32[512,128]{1,0:T(8,128)S(1)} collective-permute-done((f32[512,128]{1,0:T(8,128)S(1)}, f32[512,128]{1,0:T(8,128)S(1)}, u32[]{:S(2)}, u32[]{:S(2)}) %collective-permute-start.9) | collective-permute-done | bytes 262176 | tf_op jit(solution)/shard_map/ppermute | solution.py:51
  75.6 0.1 collective-permute-done.8
  75.6 0.1 slice_add_fusion.4
  75.7 2.1 %collective-permute-start.13 = (f32[128,128]{1,0:T(8,128)S(1)}, f32[128,128]{1,0:T(8,128)S(1)}, u32[]{:S(2)}, u32[]{:S(2)}) collective-permute-start(f32[128,128]{1,0:T(8,128)S(1)} %get-tuple-element.40), channel_id=1, source_target_pairs={{0,24},{1,25},{2,26},{3,27},{4,28},{5,29},{6,30},{7,31},{8,16},{9,... | collective-permute-start | bytes 196616 | tf_op jit(solution)/shard_map/ppermute | solution.py:51
  77.8 0.1 collective-permute-start.12
  77.9 2.3 %collective-permute-start.11 = (f32[128,128]{1,0:T(8,128)S(1)}, f32[128,128]{1,0:T(8,128)S(1)}, u32[]{:S(2)}, u32[]{:S(2)}) collective-permute-start(f32[128,128]{1,0:T(8,128)S(1)} %get-tuple-element.42), channel_id=1, source_target_pairs={{0,8},{1,9},{2,10},{3,11},{4,12},{5,13},{6,14},{7,15},{8,0},{9,1},... | collective-permute-start | bytes 196616 | tf_op jit(solution)/shard_map/ppermute | solution.py:51
  80.2 2.4 %collective-permute-done.13.refs_3_ = f32[128,128]{1,0:T(8,128)S(1)} collective-permute-done((f32[128,128]{1,0:T(8,128)S(1)}, f32[128,128]{1,0:T(8,128)S(1)}, u32[]{:S(2)}, u32[]{:S(2)}) %collective-permute-start.13) | collective-permute-done | bytes 65568 | tf_op jit(solution)/shard_map/ppermute | solution.py:51
  82.6 1.9 %collective-permute-done.12.refs_2_ = f32[128,128]{1,0:T(8,128)S(1)} collective-permute-done((f32[128,128]{1,0:T(8,128)S(1)}, f32[128,128]{1,0:T(8,128)S(1)}, u32[]{:S(2)}, u32[]{:S(2)}) %collective-permute-start.12) | collective-permute-done | bytes 65568 | tf_op jit(solution)/shard_map/ppermute | solution.py:51
  84.5 0.0 collective-permute-done.11.refs_1_
  84.5 1.9 %shard_map.136 = f32[32,8,128]{2,1,0:T(8,128)} custom-call(f32[128,128]{1,0:T(8,128)S(1)} %get-tuple-element.43.refs_0_, f32[128,128]{1,0:T(8,128)S(1)} %collective-permute-done.11.refs_1_, f32[128,128]{1,0:T(8,128)S(1)} %collective-permute-done.12.refs_2_, f32[128,128]{1,0:T(8,128)S(1)} %collective-permute-done.13.refs_3_, ...), custom_call_target="tpu_custom_call" | custom-call | tf_op jit(solution)/shard_map/pallas_call | solution.py:525
  86.4 4.1 %all-to-all-start = ((f32[32,8,128]{2,1,0:T(8,128)}), f32[32,8,128]{2,1,0:T(8,128)S(1)}, u32[]{:S(2)}, u32[]{:S(2)}) async-start(f32[32,8,128]{2,1,0:T(8,128)} %shard_map.136), calls=%async_computation | async-start | bytes 262144 | tf_op jit(solution)/shard_map/all_to_all | solution.py:532
  90.5 8.2 %all-to-all-done = f32[32,8,128]{2,1,0:T(8,128)S(1)} async-done(((f32[32,8,128]{2,1,0:T(8,128)}), f32[32,8,128]{2,1,0:T(8,128)S(1)}, u32[]{:S(2)}, u32[]{:S(2)}) %all-to-all-start) | async-done | bytes 131104 | tf_op jit(solution)/shard_map/all_to_all | solution.py:532
  98.7 0.7 constant_dynamic-slice_fusion
  (1 shorter events, 0.0 us)
Async XLA Ops:
  2.1 7.3 %collective-permute-start.2 = (f32[1,5,16,128]{3,2,1,0:T(8,128)}, f32[1,5,16,128]{3,2,1,0:T(8,128)S(1)}, u32[]{:S(2)}, u32[]{:S(2)}) collective-permute-start(f32[1,5,16,128]{3,2,1,0:T(8,128)} %bitcast.9), channel_id=1, source_target_pairs={{0,24},{1,25},{2,26},{3,27},{4,28},{5,29},{6,30},{7,31},{8,16},{9,... | collective-permute-start | bytes 122888 | tf_op jit(solution)/shard_map/ppermute | solution.py:51
  7.2 5.1 %collective-permute-start.1 = (f32[1,5,16,128]{3,2,1,0:T(8,128)}, f32[1,5,16,128]{3,2,1,0:T(8,128)S(1)}, u32[]{:S(2)}, u32[]{:S(2)}) collective-permute-start(f32[1,5,16,128]{3,2,1,0:T(8,128)} %bitcast.10), channel_id=1, source_target_pairs={{0,16},{1,17},{2,18},{3,19},{4,20},{5,21},{6,22},{7,23},{8,24},{9,... | collective-permute-start | bytes 122888 | tf_op jit(solution)/shard_map/ppermute | solution.py:51
  7.2 5.1 %collective-permute-start = (f32[1,5,16,128]{3,2,1,0:T(8,128)}, f32[1,5,16,128]{3,2,1,0:T(8,128)S(1)}, u32[]{:S(2)}, u32[]{:S(2)}) collective-permute-start(f32[1,5,16,128]{3,2,1,0:T(8,128)} %bitcast.11), channel_id=1, source_target_pairs={{0,8},{1,9},{2,10},{3,11},{4,12},{5,13},{6,14},{7,15},{8,0},{9,1},... | collective-permute-start | bytes 122888 | tf_op jit(solution)/shard_map/ppermute | solution.py:51
  13.1 8.0 %collective-permute-start.5 = (f32[4,5,16,128]{3,2,1,0:T(8,128)S(1)}, f32[4,5,16,128]{3,2,1,0:T(8,128)S(1)}, u32[]{:S(2)}, u32[]{:S(2)}) collective-permute-start(f32[4,5,16,128]{3,2,1,0:T(8,128)S(1)} %pad_maximum_fusion.refs_0_), channel_id=1, source_target_pairs={{0,6},{1,7},{2,4},{3,5},{4,2},{5,3},{6,0},{7,1},{8,14},{9,15},{10,... | collective-permute-start | bytes 491528 | tf_op jit(solution)/shard_map/ppermute | solution.py:51
  15.6 6.5 %collective-permute-start.4 = (f32[4,5,16,128]{3,2,1,0:T(8,128)S(1)}, f32[4,5,16,128]{3,2,1,0:T(8,128)S(1)}, u32[]{:S(2)}, u32[]{:S(2)}) collective-permute-start(f32[4,5,16,128]{3,2,1,0:T(8,128)S(1)} %pad_maximum_fusion.refs_0_), channel_id=1, source_target_pairs={{0,4},{1,5},{2,6},{3,7},{4,0},{5,1},{6,2},{7,3},{8,12},{9,13},{10,... | collective-permute-start | bytes 491528 | tf_op jit(solution)/shard_map/ppermute | solution.py:51
  16.1 6.0 %collective-permute-start.3 = (f32[4,5,16,128]{3,2,1,0:T(8,128)S(1)}, f32[4,5,16,128]{3,2,1,0:T(8,128)S(1)}, u32[]{:S(2)}, u32[]{:S(2)}) collective-permute-start(f32[4,5,16,128]{3,2,1,0:T(8,128)S(1)} %pad_maximum_fusion.refs_0_), channel_id=1, source_target_pairs={{0,2},{1,3},{2,0},{3,1},{4,6},{5,7},{6,4},{7,5},{8,10},{9,11},{10,... | collective-permute-start | bytes 491528 | tf_op jit(solution)/shard_map/ppermute | solution.py:51
  24.4 2.7 %copy-start.1 = (f32[2048,128]{1,0:T(8,128)}, f32[2048,128]{1,0:T(8,128)S(1)}, u32[]{:S(2)}) copy-start(f32[2048,128]{1,0:T(8,128)S(1)} %shard_map.133.refs_6_) | copy-start | bytes 3145732
  24.4 2.7 %collective-permute-start.6 = (f32[2048,128]{1,0:T(8,128)S(1)}, f32[2048,128]{1,0:T(8,128)S(1)}, u32[]{:S(2)}, u32[]{:S(2)}) collective-permute-start(f32[2048,128]{1,0:T(8,128)S(1)} %shard_map.133.refs_6_), channel_id=1, source_target_pairs={{0,1},{1,0},{2,3},{3,2},{4,5},{5,4},{6,7},{7,6},{8,9},{9,8},{10,11... | collective-permute-start | bytes 3145736 | tf_op jit(solution)/shard_map/ppermute | solution.py:51
  27.1 1.0 copy-start.2
  56.4 2.9 %collective-permute-start.7 = (f32[2048,128]{1,0:T(8,128)}, f32[2048,128]{1,0:T(8,128)S(1)}, u32[]{:S(2)}, u32[]{:S(2)}) collective-permute-start(f32[2048,128]{1,0:T(8,128)} %get-tuple-element.29), channel_id=1, source_target_pairs={{0,1},{1,0},{2,3},{3,2},{4,5},{5,4},{6,7},{7,6},{8,9},{9,8},{10,11... | collective-permute-start | bytes 3145736 | tf_op jit(solution)/shard_map/ppermute | solution.py:51
  60.6 10.2 %collective-permute-start.10 = (f32[512,128]{1,0:T(8,128)S(1)}, f32[512,128]{1,0:T(8,128)S(1)}, u32[]{:S(2)}, u32[]{:S(2)}) collective-permute-start(f32[512,128]{1,0:T(8,128)S(1)} %get-tuple-element.36), channel_id=1, source_target_pairs={{0,6},{1,7},{2,4},{3,5},{4,2},{5,3},{6,0},{7,1},{8,14},{9,15},{10,... | collective-permute-start | bytes 786440 | tf_op jit(solution)/shard_map/ppermute | solution.py:51
  62.4 13.2 %collective-permute-start.9 = (f32[512,128]{1,0:T(8,128)S(1)}, f32[512,128]{1,0:T(8,128)S(1)}, u32[]{:S(2)}, u32[]{:S(2)}) collective-permute-start(f32[512,128]{1,0:T(8,128)S(1)} %get-tuple-element.37), channel_id=1, source_target_pairs={{0,4},{1,5},{2,6},{3,7},{4,0},{5,1},{6,2},{7,3},{8,12},{9,13},{10,... | collective-permute-start | bytes 786440 | tf_op jit(solution)/shard_map/ppermute | solution.py:51
  63.7 11.9 %collective-permute-start.8 = (f32[512,128]{1,0:T(8,128)S(1)}, f32[512,128]{1,0:T(8,128)S(1)}, u32[]{:S(2)}, u32[]{:S(2)}) collective-permute-start(f32[512,128]{1,0:T(8,128)S(1)} %get-tuple-element.38), channel_id=1, source_target_pairs={{0,2},{1,3},{2,0},{3,1},{4,6},{5,7},{6,4},{7,5},{8,10},{9,11},{10,... | collective-permute-start | bytes 786440 | tf_op jit(solution)/shard_map/ppermute | solution.py:51
  64.2 3.4 %copy-start = (bf16[2,2048,1024]{2,1,0:T(8,128)(2,1)S(1)}, bf16[2,2048,1024]{2,1,0:T(8,128)(2,1)}, u32[]{:S(2)}) copy-start(bf16[2,2048,1024]{2,1,0:T(8,128)(2,1)} %source) | copy-start | bytes 25165828
  75.7 6.9 %collective-permute-start.13 = (f32[128,128]{1,0:T(8,128)S(1)}, f32[128,128]{1,0:T(8,128)S(1)}, u32[]{:S(2)}, u32[]{:S(2)}) collective-permute-start(f32[128,128]{1,0:T(8,128)S(1)} %get-tuple-element.40), channel_id=1, source_target_pairs={{0,24},{1,25},{2,26},{3,27},{4,28},{5,29},{6,30},{7,31},{8,16},{9,... | collective-permute-start | bytes 196616 | tf_op jit(solution)/shard_map/ppermute | solution.py:51
  77.8 6.7 %collective-permute-start.12 = (f32[128,128]{1,0:T(8,128)S(1)}, f32[128,128]{1,0:T(8,128)S(1)}, u32[]{:S(2)}, u32[]{:S(2)}) collective-permute-start(f32[128,128]{1,0:T(8,128)S(1)} %get-tuple-element.41), channel_id=1, source_target_pairs={{0,16},{1,17},{2,18},{3,19},{4,20},{5,21},{6,22},{7,23},{8,24},{9,... | collective-permute-start | bytes 196616 | tf_op jit(solution)/shard_map/ppermute | solution.py:51
  77.9 6.6 %collective-permute-start.11 = (f32[128,128]{1,0:T(8,128)S(1)}, f32[128,128]{1,0:T(8,128)S(1)}, u32[]{:S(2)}, u32[]{:S(2)}) collective-permute-start(f32[128,128]{1,0:T(8,128)S(1)} %get-tuple-element.42), channel_id=1, source_target_pairs={{0,8},{1,9},{2,10},{3,11},{4,12},{5,13},{6,14},{7,15},{8,0},{9,1},... | collective-permute-start | bytes 196616 | tf_op jit(solution)/shard_map/ppermute | solution.py:51
  86.4 12.3 %all-to-all-start = ((f32[32,8,128]{2,1,0:T(8,128)}), f32[32,8,128]{2,1,0:T(8,128)S(1)}, u32[]{:S(2)}, u32[]{:S(2)}) async-start(f32[32,8,128]{2,1,0:T(8,128)} %shard_map.136), calls=%async_computation | async-start | bytes 262144 | tf_op jit(solution)/shard_map/all_to_all | solution.py:532

commit v5 on v4

--- a/solution.py
+++ b/solution.py
@@ -10,6 +10,7 @@
 BOUNCES = 4
 MOST_COPIES = 8
 SLOTS = 8
+MERGES = 4
 SMALL = 4 * 2**20
 LARGE = 60 * 2**20
 CHUNKS = 8
@@ -154,7 +155,7 @@
                 out[pl.ds(at, LANES), :] = tall.T
             return carry
 
-        lax.fori_loop(0, pieces, build, 0)
+        lax.fori_loop(0, pieces, build, 0, unroll=min(pieces, 4))
         base += pieces
 
 
@@ -321,22 +322,27 @@
         refill(q, q).wait()
 
     size = total // parts
+    chunk = size // MERGES
     outs = []
-    for part in reversed(range(parts)):
-
-        def merge(i, carry, part=part):
-            at = pl.ds(pl.multiple_of(part * size + i * LANES, LANES), LANES)
-            sums[0][at, :] = functools.reduce(lambda a, b: a + b, [ref[at, :] for ref in sums])
-            return carry
-
-        if copies > 1:
-            lax.fori_loop(0, size // LANES, merge, 0)
-        outs.append(
-            pltpu.make_async_copy(
-                sums[0].at[pl.ds(part * size, size), :], part_refs[part], leave.at[part]
+    for n, part in enumerate(reversed(range(parts))):
+        for m in range(MERGES):
+            begin = part * size + m * chunk
+
+            def merge(i, carry, begin=begin):
+                at = pl.ds(pl.multiple_of(begin + i * LANES, LANES), LANES)
+                sums[0][at, :] = functools.reduce(lambda a, b: a + b, [ref[at, :] for ref in sums])
+                return carry
+
+            if copies > 1:
+                lax.fori_loop(0, chunk // LANES, merge, 0)
+            outs.append(
+                pltpu.make_async_copy(
+                    sums[0].at[pl.ds(begin, chunk), :],
+                    part_refs[part].at[pl.ds(m * chunk, chunk), :],
+                    leave.at[n * MERGES + m],
+                )
             )
-        )
-        outs[-1].start()
+            outs[-1].start()
     for out in outs:
         out.wait()
     leaving.wait()
@@ -485,7 +491,7 @@
         scratch_shapes=[pltpu.VMEM(*buffer) for buffer in buffers]
         + [
             pltpu.SemaphoreType.DMA((len(tables),)),
-            pltpu.SemaphoreType.DMA((parts,)),
+            pltpu.SemaphoreType.DMA((parts * MERGES,)),
             pltpu.SemaphoreType.DMA((SLOTS,)),
         ]
         + [pltpu.SMEM((1, 2 * LANES), jnp.int32)] * SLOTS

time: 99.8 us -> 98.2 us (0.984)
  Pallas kernels: 37 us -> 35.4 us
    pallas_call x1, Pallas kernels: 2.25 us -> 0.87 us  [body(): pl.pallas_call(functools.partial(build_kernel, depth), out_shape=jax.Shap...]
where the time goes in v5:
time: 98.2 us; the launch traced here: 97.8 us
  Pallas kernels  35.4 us (36%)
  waiting for transfers between devices  32.8 us (33%)
  starting transfers between devices  21.7 us (22%)
  local copies, waits for them, and re-layouts  5.03 us (5%)
  other arithmetic  2.19 us (2%)
    pallas_call x1, Pallas kernels, body(): pl.pallas_call(functools.partial(trace_kernel, meta), out_shape=[jax.Shap...  28.1 us
    ppermute x14, waiting for transfers between devices, send(): return lax.ppermute(value, axes, [(i, i ^ mask) for i in range(count)])  24.6 us
    ppermute x14, starting transfers between devices, send(): return lax.ppermute(value, axes, [(i, i ^ mask) for i in range(count)])  17.6 us
    all_to_all x1, waiting for transfers between devices, body(): tile = jnp.sum(lax.all_to_all(partial, axes, 0, 0, tiled=True), axis=0)  8.22 us
    unnamed x6, local copies, waits for them, and re-layouts  4.36 us
    all_to_all x1, starting transfers between devices, body(): tile = jnp.sum(lax.all_to_all(partial, axes, 0, 0, tiled=True), axis=0)  4.07 us
    pallas_call x1, Pallas kernels, body(): pl.pallas_call(functools.partial(prepare_kernel, (owned, bins, depth, pha...  2.36 us
  transfers between devices with their start and end apart: 15, of which 13 were waited for; matrix products, arithmetic and copies ran while one was open for 0% of the time, Pallas kernels for 3%

profile of v5, /device:TPU:0, one launch (start us, length us, event | category | flops | bytes accessed | tf_op | source)
XLA Modules:
  0.0 97.8 jit_solution(15577335698023482090)
XLA Ops:
  0.6 1.4 %shard_map.132 = f32[5,16,128]{2,1,0:T(8,128)} custom-call(f32[64,128]{1,0:T(8,128)} %bitcast.15, f32[64,128]{1,0:T(8,128)} %bitcast.16, f32[64,128]{1,0:T(8,128)} %bitcast.17, f32[64,128]{1,0:T(8,128)} %bitcast.18, f32[64,128]{1,0:T(8,128)} %bitcast.19), custom_call_target="tpu_custom_call" | custom-call | tf_op jit(solution)/shard_map/pallas_call | solution.py:420
  2.1 5.1 %collective-permute-start.2 = (f32[1,5,16,128]{3,2,1,0:T(8,128)}, f32[1,5,16,128]{3,2,1,0:T(8,128)S(1)}, u32[]{:S(2)}, u32[]{:S(2)}) collective-permute-start(f32[1,5,16,128]{3,2,1,0:T(8,128)} %bitcast.9), channel_id=1, source_target_pairs={{0,24},{1,25},{2,26},{3,27},{4,28},{5,29},{6,30},{7,31},{8,16},{9,... | collective-permute-start | bytes 122888 | tf_op jit(solution)/shard_map/ppermute | solution.py:52
  7.2 0.0 collective-permute-start.1
  7.2 0.6 collective-permute-start
  7.8 1.6 %collective-permute-done.2 = f32[1,5,16,128]{3,2,1,0:T(8,128)S(1)} collective-permute-done((f32[1,5,16,128]{3,2,1,0:T(8,128)}, f32[1,5,16,128]{3,2,1,0:T(8,128)S(1)}, u32[]{:S(2)}, u32[]{:S(2)}) %collective-permute-start.2) | collective-permute-done | bytes 40992 | tf_op jit(solution)/shard_map/ppermute | solution.py:52
  9.4 2.9 %collective-permute-done.1 = f32[1,5,16,128]{3,2,1,0:T(8,128)S(1)} collective-permute-done((f32[1,5,16,128]{3,2,1,0:T(8,128)}, f32[1,5,16,128]{3,2,1,0:T(8,128)S(1)}, u32[]{:S(2)}, u32[]{:S(2)}) %collective-permute-start.1) | collective-permute-done | bytes 40992 | tf_op jit(solution)/shard_map/ppermute | solution.py:52
  12.3 0.0 collective-permute-done
  12.3 0.8 pad_maximum_fusion.refs_0_
  13.1 2.5 %collective-permute-start.5 = (f32[4,5,16,128]{3,2,1,0:T(8,128)S(1)}, f32[4,5,16,128]{3,2,1,0:T(8,128)S(1)}, u32[]{:S(2)}, u32[]{:S(2)}) collective-permute-start(f32[4,5,16,128]{3,2,1,0:T(8,128)S(1)} %pad_maximum_fusion.refs_0_), channel_id=1, source_target_pairs={{0,6},{1,7},{2,4},{3,5},{4,2},{5,3},{6,0},{7,1},{8,14},{9,15},{10,... | collective-permute-start | bytes 491528 | tf_op jit(solution)/shard_map/ppermute | solution.py:52
  15.6 0.5 collective-permute-start.4
  16.1 0.5 collective-permute-start.3
  16.6 4.5 %collective-permute-done.5.refs_3_ = f32[4,5,16,128]{3,2,1,0:T(8,128)S(1)} collective-permute-done((f32[4,5,16,128]{3,2,1,0:T(8,128)S(1)}, f32[4,5,16,128]{3,2,1,0:T(8,128)S(1)}, u32[]{:S(2)}, u32[]{:S(2)}) %collective-permute-start.5) | collective-permute-done | bytes 163872 | tf_op jit(solution)/shard_map/ppermute | solution.py:52
  21.1 1.0 collective-permute-done.4.refs_2_
  22.1 0.1 collective-permute-done.3.refs_1_
  22.1 0.9 shard_map.133.refs_6_
  23.0 0.0 copy-start.1
  23.0 0.1 collective-permute-start.6
  23.1 2.4 %shard_map.131 = (s32[128,128]{1,0:T(8,128)}, s32[128,128]{1,0:T(8,128)}, f32[128,128]{1,0:T(8,128)}, f32[128,128]{1,0:T(8,128)}, f32[256,128]{1,0:T(8,128)}, /*index=5*/f32[96,128]{1,0:T(8,128)}) custom-call(s32[32,128]{1,0:T(8,128)} %bitcast.20, s32[96,128]{1,0:T(8,128)} %bitcast.14, s32[4,4096]{1,0:T(4,128)} %hit.1, f32[4,4096]{1,0:T(4,128)} %angle.1, ...), custom_call_target="tpu_custom_call" | custom-call | tf_op jit(solution)/shard_map/pallas_call | solution.py:448
  25.5 0.3 collective-permute-done.6.refs_7_
  25.8 0.0 copy-start.2
  25.8 0.0 copy-done.1
  25.8 1.0 copy-done.2
  26.7 28.1 %shard_map.134 = (f32[2048,128]{1,0:T(8,128)}, f32[2048,128]{1,0:T(8,128)}, f32[8,4096]{1,0:T(8,128)}) custom-call(s32[64,1,256]{2,1,0:T(1,128)} %bitcast.13, s32[128,128]{1,0:T(8,128)} %get-tuple-element.20.refs_1_, f32[128,128]{1,0:T(8,128)} %get-tuple-element.21.refs_2_, f32[128,128]{1,0:T(8,128)} %get-tuple-element.22.refs_3_, ...), custom_call_target="tpu_custom_call" | custom-call | tf_op jit(solution)/shard_map/pallas_call | solution.py:485
  54.8 0.2 collective-permute-start.7
  55.0 2.7 %collective-permute-done.7 = f32[2048,128]{1,0:T(8,128)S(1)} collective-permute-done((f32[2048,128]{1,0:T(8,128)}, f32[2048,128]{1,0:T(8,128)S(1)}, u32[]{:S(2)}, u32[]{:S(2)}) %collective-permute-start.7) | collective-permute-done | bytes 1048608 | tf_op jit(solution)/shard_map/ppermute | solution.py:52
  57.7 1.3 %slice_add_fusion = (f32[512,128]{1,0:T(8,128)S(1)}, f32[512,128]{1,0:T(8,128)S(1)}, f32[512,128]{1,0:T(8,128)S(1)}, f32[512,128]{1,0:T(8,128)S(1)}) fusion(f32[2048,128]{1,0:T(8,128)S(1)} %collective-permute-done.7, f32[2048,128]{1,0:T(8,128)} %get-tuple-element.28), kind=kLoop, calls=%fused_computation | loop fusion | flops 262144 | bytes 3145728 | tf_op jit(solution)/shard_map/add | solution.py:525
  59.0 1.8 %collective-permute-start.10 = (f32[512,128]{1,0:T(8,128)S(1)}, f32[512,128]{1,0:T(8,128)S(1)}, u32[]{:S(2)}, u32[]{:S(2)}) collective-permute-start(f32[512,128]{1,0:T(8,128)S(1)} %get-tuple-element.36), channel_id=1, source_target_pairs={{0,6},{1,7},{2,4},{3,5},{4,2},{5,3},{6,0},{7,1},{8,14},{9,15},{10,... | collective-permute-start | bytes 786440 | tf_op jit(solution)/shard_map/ppermute | solution.py:52
  60.8 1.3 %collective-permute-start.9 = (f32[512,128]{1,0:T(8,128)S(1)}, f32[512,128]{1,0:T(8,128)S(1)}, u32[]{:S(2)}, u32[]{:S(2)}) collective-permute-start(f32[512,128]{1,0:T(8,128)S(1)} %get-tuple-element.37), channel_id=1, source_target_pairs={{0,4},{1,5},{2,6},{3,7},{4,0},{5,1},{6,2},{7,3},{8,12},{9,13},{10,... | collective-permute-start | bytes 786440 | tf_op jit(solution)/shard_map/ppermute | solution.py:52
  62.1 0.5 collective-permute-start.8
  62.6 0.0 copy-start
  62.6 3.4 %copy-done = bf16[2,2048,1024]{2,1,0:T(8,128)(2,1)S(1)} copy-done((bf16[2,2048,1024]{2,1,0:T(8,128)(2,1)S(1)}, bf16[2,2048,1024]{2,1,0:T(8,128)(2,1)}, u32[]{:S(2)}) %copy-start) | copy-done | bytes 8388632
  66.0 0.7 shard_map.135.refs_4_
  66.7 2.5 %collective-permute-done.10 = f32[512,128]{1,0:T(8,128)S(1)} collective-permute-done((f32[512,128]{1,0:T(8,128)S(1)}, f32[512,128]{1,0:T(8,128)S(1)}, u32[]{:S(2)}, u32[]{:S(2)}) %collective-permute-start.10) | collective-permute-done | bytes 262176 | tf_op jit(solution)/shard_map/ppermute | solution.py:52
  69.2 4.8 %collective-permute-done.9 = f32[512,128]{1,0:T(8,128)S(1)} collective-permute-done((f32[512,128]{1,0:T(8,128)S(1)}, f32[512,128]{1,0:T(8,128)S(1)}, u32[]{:S(2)}, u32[]{:S(2)}) %collective-permute-start.9) | collective-permute-done | bytes 262176 | tf_op jit(solution)/shard_map/ppermute | solution.py:52
  74.0 0.1 collective-permute-done.8
  74.0 0.1 slice_add_fusion.4
  74.1 2.0 %collective-permute-start.13 = (f32[128,128]{1,0:T(8,128)S(1)}, f32[128,128]{1,0:T(8,128)S(1)}, u32[]{:S(2)}, u32[]{:S(2)}) collective-permute-start(f32[128,128]{1,0:T(8,128)S(1)} %get-tuple-element.40), channel_id=1, source_target_pairs={{0,24},{1,25},{2,26},{3,27},{4,28},{5,29},{6,30},{7,31},{8,16},{9,... | collective-permute-start | bytes 196616 | tf_op jit(solution)/shard_map/ppermute | solution.py:52
  76.2 0.1 collective-permute-start.12
  76.3 2.3 %collective-permute-start.11 = (f32[128,128]{1,0:T(8,128)S(1)}, f32[128,128]{1,0:T(8,128)S(1)}, u32[]{:S(2)}, u32[]{:S(2)}) collective-permute-start(f32[128,128]{1,0:T(8,128)S(1)} %get-tuple-element.42), channel_id=1, source_target_pairs={{0,8},{1,9},{2,10},{3,11},{4,12},{5,13},{6,14},{7,15},{8,0},{9,1},... | collective-permute-start | bytes 196616 | tf_op jit(solution)/shard_map/ppermute | solution.py:52
  78.6 2.4 %collective-permute-done.13.refs_3_ = f32[128,128]{1,0:T(8,128)S(1)} collective-permute-done((f32[128,128]{1,0:T(8,128)S(1)}, f32[128,128]{1,0:T(8,128)S(1)}, u32[]{:S(2)}, u32[]{:S(2)}) %collective-permute-start.13) | collective-permute-done | bytes 65568 | tf_op jit(solution)/shard_map/ppermute | solution.py:52
  81.0 1.9 %collective-permute-done.12.refs_2_ = f32[128,128]{1,0:T(8,128)S(1)} collective-permute-done((f32[128,128]{1,0:T(8,128)S(1)}, f32[128,128]{1,0:T(8,128)S(1)}, u32[]{:S(2)}, u32[]{:S(2)}) %collective-permute-start.12) | collective-permute-done | bytes 65568 | tf_op jit(solution)/shard_map/ppermute | solution.py:52
  82.9 0.0 collective-permute-done.11.refs_1_
  82.9 1.9 %shard_map.136 = f32[32,8,128]{2,1,0:T(8,128)} custom-call(f32[128,128]{1,0:T(8,128)S(1)} %get-tuple-element.43.refs_0_, f32[128,128]{1,0:T(8,128)S(1)} %collective-permute-done.11.refs_1_, f32[128,128]{1,0:T(8,128)S(1)} %collective-permute-done.12.refs_2_, f32[128,128]{1,0:T(8,128)S(1)} %collective-permute-done.13.refs_3_, ...), custom_call_target="tpu_custom_call" | custom-call | tf_op jit(solution)/shard_map/pallas_call | solution.py:531
  84.8 4.1 %all-to-all-start = ((f32[32,8,128]{2,1,0:T(8,128)}), f32[32,8,128]{2,1,0:T(8,128)S(1)}, u32[]{:S(2)}, u32[]{:S(2)}) async-start(f32[32,8,128]{2,1,0:T(8,128)} %shard_map.136), calls=%async_computation | async-start | bytes 262144 | tf_op jit(solution)/shard_map/all_to_all | solution.py:538
  88.9 8.2 %all-to-all-done = f32[32,8,128]{2,1,0:T(8,128)S(1)} async-done(((f32[32,8,128]{2,1,0:T(8,128)}), f32[32,8,128]{2,1,0:T(8,128)S(1)}, u32[]{:S(2)}, u32[]{:S(2)}) %all-to-all-start) | async-done | bytes 131104 | tf_op jit(solution)/shard_map/all_to_all | solution.py:538
  97.1 0.7 constant_dynamic-slice_fusion
  (1 shorter events, 0.0 us)
Async XLA Ops:
  2.1 7.3 %collective-permute-start.2 = (f32[1,5,16,128]{3,2,1,0:T(8,128)}, f32[1,5,16,128]{3,2,1,0:T(8,128)S(1)}, u32[]{:S(2)}, u32[]{:S(2)}) collective-permute-start(f32[1,5,16,128]{3,2,1,0:T(8,128)} %bitcast.9), channel_id=1, source_target_pairs={{0,24},{1,25},{2,26},{3,27},{4,28},{5,29},{6,30},{7,31},{8,16},{9,... | collective-permute-start | bytes 122888 | tf_op jit(solution)/shard_map/ppermute | solution.py:52
  7.2 5.1 %collective-permute-start.1 = (f32[1,5,16,128]{3,2,1,0:T(8,128)}, f32[1,5,16,128]{3,2,1,0:T(8,128)S(1)}, u32[]{:S(2)}, u32[]{:S(2)}) collective-permute-start(f32[1,5,16,128]{3,2,1,0:T(8,128)} %bitcast.10), channel_id=1, source_target_pairs={{0,16},{1,17},{2,18},{3,19},{4,20},{5,21},{6,22},{7,23},{8,24},{9,... | collective-permute-start | bytes 122888 | tf_op jit(solution)/shard_map/ppermute | solution.py:52
  7.2 5.1 %collective-permute-start = (f32[1,5,16,128]{3,2,1,0:T(8,128)}, f32[1,5,16,128]{3,2,1,0:T(8,128)S(1)}, u32[]{:S(2)}, u32[]{:S(2)}) collective-permute-start(f32[1,5,16,128]{3,2,1,0:T(8,128)} %bitcast.11), channel_id=1, source_target_pairs={{0,8},{1,9},{2,10},{3,11},{4,12},{5,13},{6,14},{7,15},{8,0},{9,1},... | collective-permute-start | bytes 122888 | tf_op jit(solution)/shard_map/ppermute | solution.py:52
  13.1 8.0 %collective-permute-start.5 = (f32[4,5,16,128]{3,2,1,0:T(8,128)S(1)}, f32[4,5,16,128]{3,2,1,0:T(8,128)S(1)}, u32[]{:S(2)}, u32[]{:S(2)}) collective-permute-start(f32[4,5,16,128]{3,2,1,0:T(8,128)S(1)} %pad_maximum_fusion.refs_0_), channel_id=1, source_target_pairs={{0,6},{1,7},{2,4},{3,5},{4,2},{5,3},{6,0},{7,1},{8,14},{9,15},{10,... | collective-permute-start | bytes 491528 | tf_op jit(solution)/shard_map/ppermute | solution.py:52
  15.6 6.5 %collective-permute-start.4 = (f32[4,5,16,128]{3,2,1,0:T(8,128)S(1)}, f32[4,5,16,128]{3,2,1,0:T(8,128)S(1)}, u32[]{:S(2)}, u32[]{:S(2)}) collective-permute-start(f32[4,5,16,128]{3,2,1,0:T(8,128)S(1)} %pad_maximum_fusion.refs_0_), channel_id=1, source_target_pairs={{0,4},{1,5},{2,6},{3,7},{4,0},{5,1},{6,2},{7,3},{8,12},{9,13},{10,... | collective-permute-start | bytes 491528 | tf_op jit(solution)/shard_map/ppermute | solution.py:52
  16.1 6.0 %collective-permute-start.3 = (f32[4,5,16,128]{3,2,1,0:T(8,128)S(1)}, f32[4,5,16,128]{3,2,1,0:T(8,128)S(1)}, u32[]{:S(2)}, u32[]{:S(2)}) collective-permute-start(f32[4,5,16,128]{3,2,1,0:T(8,128)S(1)} %pad_maximum_fusion.refs_0_), channel_id=1, source_target_pairs={{0,2},{1,3},{2,0},{3,1},{4,6},{5,7},{6,4},{7,5},{8,10},{9,11},{10,... | collective-permute-start | bytes 491528 | tf_op jit(solution)/shard_map/ppermute | solution.py:52
  23.0 2.7 %copy-start.1 = (f32[2048,128]{1,0:T(8,128)}, f32[2048,128]{1,0:T(8,128)S(1)}, u32[]{:S(2)}) copy-start(f32[2048,128]{1,0:T(8,128)S(1)} %shard_map.133.refs_6_) | copy-start | bytes 3145732
  23.0 2.7 %collective-permute-start.6 = (f32[2048,128]{1,0:T(8,128)S(1)}, f32[2048,128]{1,0:T(8,128)S(1)}, u32[]{:S(2)}, u32[]{:S(2)}) collective-permute-start(f32[2048,128]{1,0:T(8,128)S(1)} %shard_map.133.refs_6_), channel_id=1, source_target_pairs={{0,1},{1,0},{2,3},{3,2},{4,5},{5,4},{6,7},{7,6},{8,9},{9,8},{10,11... | collective-permute-start | bytes 3145736 | tf_op jit(solution)/shard_map/ppermute | solution.py:52
  25.8 1.0 %copy-start.2 = (f32[2048,128]{1,0:T(8,128)}, f32[2048,128]{1,0:T(8,128)S(1)}, u32[]{:S(2)}) copy-start(f32[2048,128]{1,0:T(8,128)S(1)} %collective-permute-done.6.refs_7_) | copy-start | bytes 3145732
  54.8 2.9 %collective-permute-start.7 = (f32[2048,128]{1,0:T(8,128)}, f32[2048,128]{1,0:T(8,128)S(1)}, u32[]{:S(2)}, u32[]{:S(2)}) collective-permute-start(f32[2048,128]{1,0:T(8,128)} %get-tuple-element.29), channel_id=1, source_target_pairs={{0,1},{1,0},{2,3},{3,2},{4,5},{5,4},{6,7},{7,6},{8,9},{9,8},{10,11... | collective-permute-start | bytes 3145736 | tf_op jit(solution)/shard_map/ppermute | solution.py:52
  59.0 10.2 %collective-permute-start.10 = (f32[512,128]{1,0:T(8,128)S(1)}, f32[512,128]{1,0:T(8,128)S(1)}, u32[]{:S(2)}, u32[]{:S(2)}) collective-permute-start(f32[512,128]{1,0:T(8,128)S(1)} %get-tuple-element.36), channel_id=1, source_target_pairs={{0,6},{1,7},{2,4},{3,5},{4,2},{5,3},{6,0},{7,1},{8,14},{9,15},{10,... | collective-permute-start | bytes 786440 | tf_op jit(solution)/shard_map/ppermute | solution.py:52
  60.8 13.2 %collective-permute-start.9 = (f32[512,128]{1,0:T(8,128)S(1)}, f32[512,128]{1,0:T(8,128)S(1)}, u32[]{:S(2)}, u32[]{:S(2)}) collective-permute-start(f32[512,128]{1,0:T(8,128)S(1)} %get-tuple-element.37), channel_id=1, source_target_pairs={{0,4},{1,5},{2,6},{3,7},{4,0},{5,1},{6,2},{7,3},{8,12},{9,13},{10,... | collective-permute-start | bytes 786440 | tf_op jit(solution)/shard_map/ppermute | solution.py:52
  62.1 11.9 %collective-permute-start.8 = (f32[512,128]{1,0:T(8,128)S(1)}, f32[512,128]{1,0:T(8,128)S(1)}, u32[]{:S(2)}, u32[]{:S(2)}) collective-permute-start(f32[512,128]{1,0:T(8,128)S(1)} %get-tuple-element.38), channel_id=1, source_target_pairs={{0,2},{1,3},{2,0},{3,1},{4,6},{5,7},{6,4},{7,5},{8,10},{9,11},{10,... | collective-permute-start | bytes 786440 | tf_op jit(solution)/shard_map/ppermute | solution.py:52
  62.6 3.4 %copy-start = (bf16[2,2048,1024]{2,1,0:T(8,128)(2,1)S(1)}, bf16[2,2048,1024]{2,1,0:T(8,128)(2,1)}, u32[]{:S(2)}) copy-start(bf16[2,2048,1024]{2,1,0:T(8,128)(2,1)} %source) | copy-start | bytes 25165828
  74.1 6.9 %collective-permute-start.13 = (f32[128,128]{1,0:T(8,128)S(1)}, f32[128,128]{1,0:T(8,128)S(1)}, u32[]{:S(2)}, u32[]{:S(2)}) collective-permute-start(f32[128,128]{1,0:T(8,128)S(1)} %get-tuple-element.40), channel_id=1, source_target_pairs={{0,24},{1,25},{2,26},{3,27},{4,28},{5,29},{6,30},{7,31},{8,16},{9,... | collective-permute-start | bytes 196616 | tf_op jit(solution)/shard_map/ppermute | solution.py:52
  76.2 6.7 %collective-permute-start.12 = (f32[128,128]{1,0:T(8,128)S(1)}, f32[128,128]{1,0:T(8,128)S(1)}, u32[]{:S(2)}, u32[]{:S(2)}) collective-permute-start(f32[128,128]{1,0:T(8,128)S(1)} %get-tuple-element.41), channel_id=1, source_target_pairs={{0,16},{1,17},{2,18},{3,19},{4,20},{5,21},{6,22},{7,23},{8,24},{9,... | collective-permute-start | bytes 196616 | tf_op jit(solution)/shard_map/ppermute | solution.py:52
  76.3 6.6 %collective-permute-start.11 = (f32[128,128]{1,0:T(8,128)S(1)}, f32[128,128]{1,0:T(8,128)S(1)}, u32[]{:S(2)}, u32[]{:S(2)}) collective-permute-start(f32[128,128]{1,0:T(8,128)S(1)} %get-tuple-element.42), channel_id=1, source_target_pairs={{0,8},{1,9},{2,10},{3,11},{4,12},{5,13},{6,14},{7,15},{8,0},{9,1},... | collective-permute-start | bytes 196616 | tf_op jit(solution)/shard_map/ppermute | solution.py:52
  84.8 12.3 %all-to-all-start = ((f32[32,8,128]{2,1,0:T(8,128)}), f32[32,8,128]{2,1,0:T(8,128)S(1)}, u32[]{:S(2)}, u32[]{:S(2)}) async-start(f32[32,8,128]{2,1,0:T(8,128)} %shard_map.136), calls=%async_computation | async-start | bytes 262144 | tf_op jit(solution)/shard_map/all_to_all | solution.py:538

commit v6 on v5

--- a/solution.py
+++ b/solution.py
@@ -225,7 +225,7 @@
             ref[pl.ds(pl.multiple_of(i * clear, clear), clear), :] = zeros
         return carry
 
-    lax.fori_loop(0, total // clear, wipe, 0)
+    lax.fori_loop(0, total // clear, wipe, 0, unroll=2)
 
     def refill(pair, q):
         return pltpu.make_async_copy(rows_ref.at[pair], slots[q], fill.at[q])
@@ -334,7 +334,7 @@
                 return carry
 
             if copies > 1:
-                lax.fori_loop(0, chunk // LANES, merge, 0)
+                lax.fori_loop(0, chunk // LANES, merge, 0, unroll=2)
             outs.append(
                 pltpu.make_async_copy(
                     sums[0].at[pl.ds(begin, chunk), :],

time: 98.2 us -> 98.1 us (level)
  transfers between devices with their start and end apart: 15 -> 15, of which waited for: 13 -> 12; matrix products, arithmetic and copies ran while one was open for 0% -> 0% of each run, Pallas kernels for 3% -> 3%
where the time goes in v6:
time: 98.1 us; the launch traced here: 97.7 us
  Pallas kernels  35.2 us (36%)
  waiting for transfers between devices  32.8 us (33%)
  starting transfers between devices  21.7 us (22%)
  local copies, waits for them, and re-layouts  5.03 us (5%)
  other arithmetic  2.19 us (2%)
    pallas_call x1, Pallas kernels, body(): pl.pallas_call(functools.partial(trace_kernel, meta), out_shape=[jax.Shap...  27.9 us
    ppermute x14, waiting for transfers between devices, send(): return lax.ppermute(value, axes, [(i, i ^ mask) for i in range(count)])  24.6 us
    ppermute x14, starting transfers between devices, send(): return lax.ppermute(value, axes, [(i, i ^ mask) for i in range(count)])  17.6 us
    all_to_all x1, waiting for transfers between devices, body(): tile = jnp.sum(lax.all_to_all(partial, axes, 0, 0, tiled=True), axis=0)  8.22 us
    unnamed x6, local copies, waits for them, and re-layouts  4.36 us
    all_to_all x1, starting transfers between devices, body(): tile = jnp.sum(lax.all_to_all(partial, axes, 0, 0, tiled=True), axis=0)  4.09 us
    pallas_call x1, Pallas kernels, body(): pl.pallas_call(functools.partial(prepare_kernel, (owned, bins, depth, pha...  2.36 us
  transfers between devices with their start and end apart: 15, of which 12 were waited for; matrix products, arithmetic and copies ran while one was open for 0% of the time, Pallas kernels for 3%

profile of v6, /device:TPU:0, one launch (start us, length us, event | category | flops | bytes accessed | tf_op | source)
XLA Modules:
  0.0 97.7 jit_solution(688037275834301138)
XLA Ops:
  0.6 1.4 %shard_map.132 = f32[5,16,128]{2,1,0:T(8,128)} custom-call(f32[64,128]{1,0:T(8,128)} %bitcast.15, f32[64,128]{1,0:T(8,128)} %bitcast.16, f32[64,128]{1,0:T(8,128)} %bitcast.17, f32[64,128]{1,0:T(8,128)} %bitcast.18, f32[64,128]{1,0:T(8,128)} %bitcast.19), custom_call_target="tpu_custom_call" | custom-call | tf_op jit(solution)/shard_map/pallas_call | solution.py:420
  2.1 5.1 %collective-permute-start.2 = (f32[1,5,16,128]{3,2,1,0:T(8,128)}, f32[1,5,16,128]{3,2,1,0:T(8,128)S(1)}, u32[]{:S(2)}, u32[]{:S(2)}) collective-permute-start(f32[1,5,16,128]{3,2,1,0:T(8,128)} %bitcast.9), channel_id=1, source_target_pairs={{0,24},{1,25},{2,26},{3,27},{4,28},{5,29},{6,30},{7,31},{8,16},{9,... | collective-permute-start | bytes 122888 | tf_op jit(solution)/shard_map/ppermute | solution.py:52
  7.2 0.0 collective-permute-start.1
  7.2 0.6 collective-permute-start
  7.8 1.6 %collective-permute-done.2 = f32[1,5,16,128]{3,2,1,0:T(8,128)S(1)} collective-permute-done((f32[1,5,16,128]{3,2,1,0:T(8,128)}, f32[1,5,16,128]{3,2,1,0:T(8,128)S(1)}, u32[]{:S(2)}, u32[]{:S(2)}) %collective-permute-start.2) | collective-permute-done | bytes 40992 | tf_op jit(solution)/shard_map/ppermute | solution.py:52
  9.4 2.9 %collective-permute-done.1 = f32[1,5,16,128]{3,2,1,0:T(8,128)S(1)} collective-permute-done((f32[1,5,16,128]{3,2,1,0:T(8,128)}, f32[1,5,16,128]{3,2,1,0:T(8,128)S(1)}, u32[]{:S(2)}, u32[]{:S(2)}) %collective-permute-start.1) | collective-permute-done | bytes 40992 | tf_op jit(solution)/shard_map/ppermute | solution.py:52
  12.3 0.0 collective-permute-done
  12.3 0.8 pad_maximum_fusion.refs_0_
  13.1 2.5 %collective-permute-start.5 = (f32[4,5,16,128]{3,2,1,0:T(8,128)S(1)}, f32[4,5,16,128]{3,2,1,0:T(8,128)S(1)}, u32[]{:S(2)}, u32[]{:S(2)}) collective-permute-start(f32[4,5,16,128]{3,2,1,0:T(8,128)S(1)} %pad_maximum_fusion.refs_0_), channel_id=1, source_target_pairs={{0,6},{1,7},{2,4},{3,5},{4,2},{5,3},{6,0},{7,1},{8,14},{9,15},{10,... | collective-permute-start | bytes 491528 | tf_op jit(solution)/shard_map/ppermute | solution.py:52
  15.6 0.5 collective-permute-start.4
  16.1 0.5 collective-permute-start.3
  16.6 4.5 %collective-permute-done.5.refs_3_ = f32[4,5,16,128]{3,2,1,0:T(8,128)S(1)} collective-permute-done((f32[4,5,16,128]{3,2,1,0:T(8,128)S(1)}, f32[4,5,16,128]{3,2,1,0:T(8,128)S(1)}, u32[]{:S(2)}, u32[]{:S(2)}) %collective-permute-start.5) | collective-permute-done | bytes 163872 | tf_op jit(solution)/shard_map/ppermute | solution.py:52
  21.1 1.0 collective-permute-done.4.refs_2_
  22.1 0.1 collective-permute-done.3.refs_1_
  22.1 0.9 shard_map.133.refs_6_
  23.0 0.0 copy-start.1
  23.0 0.1 collective-permute-start.6
  23.1 2.4 %shard_map.131 = (s32[128,128]{1,0:T(8,128)}, s32[128,128]{1,0:T(8,128)}, f32[128,128]{1,0:T(8,128)}, f32[128,128]{1,0:T(8,128)}, f32[256,128]{1,0:T(8,128)}, /*index=5*/f32[96,128]{1,0:T(8,128)}) custom-call(s32[32,128]{1,0:T(8,128)} %bitcast.20, s32[96,128]{1,0:T(8,128)} %bitcast.14, s32[4,4096]{1,0:T(4,128)} %hit.1, f32[4,4096]{1,0:T(4,128)} %angle.1, ...), custom_call_target="tpu_custom_call" | custom-call | tf_op jit(solution)/shard_map/pallas_call | solution.py:448
  25.5 0.3 collective-permute-done.6.refs_7_
  25.8 0.0 copy-start.2
  25.8 0.0 copy-done.1
  25.8 1.0 copy-done.2
  26.7 27.9 %shard_map.134 = (f32[2048,128]{1,0:T(8,128)}, f32[2048,128]{1,0:T(8,128)}, f32[8,4096]{1,0:T(8,128)}) custom-call(s32[64,1,256]{2,1,0:T(1,128)} %bitcast.13, s32[128,128]{1,0:T(8,128)} %get-tuple-element.20.refs_1_, f32[128,128]{1,0:T(8,128)} %get-tuple-element.21.refs_2_, f32[128,128]{1,0:T(8,128)} %get-tuple-element.22.refs_3_, ...), custom_call_target="tpu_custom_call" | custom-call | tf_op jit(solution)/shard_map/pallas_call | solution.py:485
  54.7 0.2 collective-permute-start.7
  54.9 2.7 %collective-permute-done.7 = f32[2048,128]{1,0:T(8,128)S(1)} collective-permute-done((f32[2048,128]{1,0:T(8,128)}, f32[2048,128]{1,0:T(8,128)S(1)}, u32[]{:S(2)}, u32[]{:S(2)}) %collective-permute-start.7) | collective-permute-done | bytes 1048608 | tf_op jit(solution)/shard_map/ppermute | solution.py:52
  57.6 1.3 %slice_add_fusion = (f32[512,128]{1,0:T(8,128)S(1)}, f32[512,128]{1,0:T(8,128)S(1)}, f32[512,128]{1,0:T(8,128)S(1)}, f32[512,128]{1,0:T(8,128)S(1)}) fusion(f32[2048,128]{1,0:T(8,128)S(1)} %collective-permute-done.7, f32[2048,128]{1,0:T(8,128)} %get-tuple-element.28), kind=kLoop, calls=%fused_computation | loop fusion | flops 262144 | bytes 3145728 | tf_op jit(solution)/shard_map/add | solution.py:525
  58.9 1.8 %collective-permute-start.10 = (f32[512,128]{1,0:T(8,128)S(1)}, f32[512,128]{1,0:T(8,128)S(1)}, u32[]{:S(2)}, u32[]{:S(2)}) collective-permute-start(f32[512,128]{1,0:T(8,128)S(1)} %get-tuple-element.36), channel_id=1, source_target_pairs={{0,6},{1,7},{2,4},{3,5},{4,2},{5,3},{6,0},{7,1},{8,14},{9,15},{10,... | collective-permute-start | bytes 786440 | tf_op jit(solution)/shard_map/ppermute | solution.py:52
  60.7 1.3 %collective-permute-start.9 = (f32[512,128]{1,0:T(8,128)S(1)}, f32[512,128]{1,0:T(8,128)S(1)}, u32[]{:S(2)}, u32[]{:S(2)}) collective-permute-start(f32[512,128]{1,0:T(8,128)S(1)} %get-tuple-element.37), channel_id=1, source_target_pairs={{0,4},{1,5},{2,6},{3,7},{4,0},{5,1},{6,2},{7,3},{8,12},{9,13},{10,... | collective-permute-start | bytes 786440 | tf_op jit(solution)/shard_map/ppermute | solution.py:52
  62.0 0.5 collective-permute-start.8
  62.5 0.0 copy-start
  62.5 3.4 %copy-done = bf16[2,2048,1024]{2,1,0:T(8,128)(2,1)S(1)} copy-done((bf16[2,2048,1024]{2,1,0:T(8,128)(2,1)S(1)}, bf16[2,2048,1024]{2,1,0:T(8,128)(2,1)}, u32[]{:S(2)}) %copy-start) | copy-done | bytes 8388632
  65.9 0.7 shard_map.135.refs_4_
  66.6 2.5 %collective-permute-done.10 = f32[512,128]{1,0:T(8,128)S(1)} collective-permute-done((f32[512,128]{1,0:T(8,128)S(1)}, f32[512,128]{1,0:T(8,128)S(1)}, u32[]{:S(2)}, u32[]{:S(2)}) %collective-permute-start.10) | collective-permute-done | bytes 262176 | tf_op jit(solution)/shard_map/ppermute | solution.py:52
  69.1 4.8 %collective-permute-done.9 = f32[512,128]{1,0:T(8,128)S(1)} collective-permute-done((f32[512,128]{1,0:T(8,128)S(1)}, f32[512,128]{1,0:T(8,128)S(1)}, u32[]{:S(2)}, u32[]{:S(2)}) %collective-permute-start.9) | collective-permute-done | bytes 262176 | tf_op jit(solution)/shard_map/ppermute | solution.py:52
  73.9 0.0 collective-permute-done.8
  73.9 0.1 slice_add_fusion.4
  74.0 2.1 %collective-permute-start.13 = (f32[128,128]{1,0:T(8,128)S(1)}, f32[128,128]{1,0:T(8,128)S(1)}, u32[]{:S(2)}, u32[]{:S(2)}) collective-permute-start(f32[128,128]{1,0:T(8,128)S(1)} %get-tuple-element.40), channel_id=1, source_target_pairs={{0,24},{1,25},{2,26},{3,27},{4,28},{5,29},{6,30},{7,31},{8,16},{9,... | collective-permute-start | bytes 196616 | tf_op jit(solution)/shard_map/ppermute | solution.py:52
  76.0 0.1 collective-permute-start.12
  76.2 2.3 %collective-permute-start.11 = (f32[128,128]{1,0:T(8,128)S(1)}, f32[128,128]{1,0:T(8,128)S(1)}, u32[]{:S(2)}, u32[]{:S(2)}) collective-permute-start(f32[128,128]{1,0:T(8,128)S(1)} %get-tuple-element.42), channel_id=1, source_target_pairs={{0,8},{1,9},{2,10},{3,11},{4,12},{5,13},{6,14},{7,15},{8,0},{9,1},... | collective-permute-start | bytes 196616 | tf_op jit(solution)/shard_map/ppermute | solution.py:52
  78.4 2.4 %collective-permute-done.13.refs_3_ = f32[128,128]{1,0:T(8,128)S(1)} collective-permute-done((f32[128,128]{1,0:T(8,128)S(1)}, f32[128,128]{1,0:T(8,128)S(1)}, u32[]{:S(2)}, u32[]{:S(2)}) %collective-permute-start.13) | collective-permute-done | bytes 65568 | tf_op jit(solution)/shard_map/ppermute | solution.py:52
  80.9 1.9 %collective-permute-done.12.refs_2_ = f32[128,128]{1,0:T(8,128)S(1)} collective-permute-done((f32[128,128]{1,0:T(8,128)S(1)}, f32[128,128]{1,0:T(8,128)S(1)}, u32[]{:S(2)}, u32[]{:S(2)}) %collective-permute-start.12) | collective-permute-done | bytes 65568 | tf_op jit(solution)/shard_map/ppermute | solution.py:52
  82.7 0.0 collective-permute-done.11.refs_1_
  82.7 1.9 %shard_map.136 = f32[32,8,128]{2,1,0:T(8,128)} custom-call(f32[128,128]{1,0:T(8,128)S(1)} %get-tuple-element.43.refs_0_, f32[128,128]{1,0:T(8,128)S(1)} %collective-permute-done.11.refs_1_, f32[128,128]{1,0:T(8,128)S(1)} %collective-permute-done.12.refs_2_, f32[128,128]{1,0:T(8,128)S(1)} %collective-permute-done.13.refs_3_, ...), custom_call_target="tpu_custom_call" | custom-call | tf_op jit(solution)/shard_map/pallas_call | solution.py:531
  84.6 4.1 %all-to-all-start = ((f32[32,8,128]{2,1,0:T(8,128)}), f32[32,8,128]{2,1,0:T(8,128)S(1)}, u32[]{:S(2)}, u32[]{:S(2)}) async-start(f32[32,8,128]{2,1,0:T(8,128)} %shard_map.136), calls=%async_computation | async-start | bytes 262144 | tf_op jit(solution)/shard_map/all_to_all | solution.py:538
  88.7 8.2 %all-to-all-done = f32[32,8,128]{2,1,0:T(8,128)S(1)} async-done(((f32[32,8,128]{2,1,0:T(8,128)}), f32[32,8,128]{2,1,0:T(8,128)S(1)}, u32[]{:S(2)}, u32[]{:S(2)}) %all-to-all-start) | async-done | bytes 131104 | tf_op jit(solution)/shard_map/all_to_all | solution.py:538
  97.0 0.7 constant_dynamic-slice_fusion
  (1 shorter events, 0.0 us)
Async XLA Ops:
  2.1 7.3 %collective-permute-start.2 = (f32[1,5,16,128]{3,2,1,0:T(8,128)}, f32[1,5,16,128]{3,2,1,0:T(8,128)S(1)}, u32[]{:S(2)}, u32[]{:S(2)}) collective-permute-start(f32[1,5,16,128]{3,2,1,0:T(8,128)} %bitcast.9), channel_id=1, source_target_pairs={{0,24},{1,25},{2,26},{3,27},{4,28},{5,29},{6,30},{7,31},{8,16},{9,... | collective-permute-start | bytes 122888 | tf_op jit(solution)/shard_map/ppermute | solution.py:52
  7.2 5.1 %collective-permute-start.1 = (f32[1,5,16,128]{3,2,1,0:T(8,128)}, f32[1,5,16,128]{3,2,1,0:T(8,128)S(1)}, u32[]{:S(2)}, u32[]{:S(2)}) collective-permute-start(f32[1,5,16,128]{3,2,1,0:T(8,128)} %bitcast.10), channel_id=1, source_target_pairs={{0,16},{1,17},{2,18},{3,19},{4,20},{5,21},{6,22},{7,23},{8,24},{9,... | collective-permute-start | bytes 122888 | tf_op jit(solution)/shard_map/ppermute | solution.py:52
  7.2 5.1 %collective-permute-start = (f32[1,5,16,128]{3,2,1,0:T(8,128)}, f32[1,5,16,128]{3,2,1,0:T(8,128)S(1)}, u32[]{:S(2)}, u32[]{:S(2)}) collective-permute-start(f32[1,5,16,128]{3,2,1,0:T(8,128)} %bitcast.11), channel_id=1, source_target_pairs={{0,8},{1,9},{2,10},{3,11},{4,12},{5,13},{6,14},{7,15},{8,0},{9,1},... | collective-permute-start | bytes 122888 | tf_op jit(solution)/shard_map/ppermute | solution.py:52
  13.1 8.0 %collective-permute-start.5 = (f32[4,5,16,128]{3,2,1,0:T(8,128)S(1)}, f32[4,5,16,128]{3,2,1,0:T(8,128)S(1)}, u32[]{:S(2)}, u32[]{:S(2)}) collective-permute-start(f32[4,5,16,128]{3,2,1,0:T(8,128)S(1)} %pad_maximum_fusion.refs_0_), channel_id=1, source_target_pairs={{0,6},{1,7},{2,4},{3,5},{4,2},{5,3},{6,0},{7,1},{8,14},{9,15},{10,... | collective-permute-start | bytes 491528 | tf_op jit(solution)/shard_map/ppermute | solution.py:52
  15.6 6.5 %collective-permute-start.4 = (f32[4,5,16,128]{3,2,1,0:T(8,128)S(1)}, f32[4,5,16,128]{3,2,1,0:T(8,128)S(1)}, u32[]{:S(2)}, u32[]{:S(2)}) collective-permute-start(f32[4,5,16,128]{3,2,1,0:T(8,128)S(1)} %pad_maximum_fusion.refs_0_), channel_id=1, source_target_pairs={{0,4},{1,5},{2,6},{3,7},{4,0},{5,1},{6,2},{7,3},{8,12},{9,13},{10,... | collective-permute-start | bytes 491528 | tf_op jit(solution)/shard_map/ppermute | solution.py:52
  16.1 6.0 %collective-permute-start.3 = (f32[4,5,16,128]{3,2,1,0:T(8,128)S(1)}, f32[4,5,16,128]{3,2,1,0:T(8,128)S(1)}, u32[]{:S(2)}, u32[]{:S(2)}) collective-permute-start(f32[4,5,16,128]{3,2,1,0:T(8,128)S(1)} %pad_maximum_fusion.refs_0_), channel_id=1, source_target_pairs={{0,2},{1,3},{2,0},{3,1},{4,6},{5,7},{6,4},{7,5},{8,10},{9,11},{10,... | collective-permute-start | bytes 491528 | tf_op jit(solution)/shard_map/ppermute | solution.py:52
  23.0 2.7 %copy-start.1 = (f32[2048,128]{1,0:T(8,128)}, f32[2048,128]{1,0:T(8,128)S(1)}, u32[]{:S(2)}) copy-start(f32[2048,128]{1,0:T(8,128)S(1)} %shard_map.133.refs_6_) | copy-start | bytes 3145732
  23.0 2.7 %collective-permute-start.6 = (f32[2048,128]{1,0:T(8,128)S(1)}, f32[2048,128]{1,0:T(8,128)S(1)}, u32[]{:S(2)}, u32[]{:S(2)}) collective-permute-start(f32[2048,128]{1,0:T(8,128)S(1)} %shard_map.133.refs_6_), channel_id=1, source_target_pairs={{0,1},{1,0},{2,3},{3,2},{4,5},{5,4},{6,7},{7,6},{8,9},{9,8},{10,11... | collective-permute-start | bytes 3145736 | tf_op jit(solution)/shard_map/ppermute | solution.py:52
  25.8 1.0 %copy-start.2 = (f32[2048,128]{1,0:T(8,128)}, f32[2048,128]{1,0:T(8,128)S(1)}, u32[]{:S(2)}) copy-start(f32[2048,128]{1,0:T(8,128)S(1)} %collective-permute-done.6.refs_7_) | copy-start | bytes 3145732
  54.7 2.9 %collective-permute-start.7 = (f32[2048,128]{1,0:T(8,128)}, f32[2048,128]{1,0:T(8,128)S(1)}, u32[]{:S(2)}, u32[]{:S(2)}) collective-permute-start(f32[2048,128]{1,0:T(8,128)} %get-tuple-element.29), channel_id=1, source_target_pairs={{0,1},{1,0},{2,3},{3,2},{4,5},{5,4},{6,7},{7,6},{8,9},{9,8},{10,11... | collective-permute-start | bytes 3145736 | tf_op jit(solution)/shard_map/ppermute | solution.py:52
  58.9 10.2 %collective-permute-start.10 = (f32[512,128]{1,0:T(8,128)S(1)}, f32[512,128]{1,0:T(8,128)S(1)}, u32[]{:S(2)}, u32[]{:S(2)}) collective-permute-start(f32[512,128]{1,0:T(8,128)S(1)} %get-tuple-element.36), channel_id=1, source_target_pairs={{0,6},{1,7},{2,4},{3,5},{4,2},{5,3},{6,0},{7,1},{8,14},{9,15},{10,... | collective-permute-start | bytes 786440 | tf_op jit(solution)/shard_map/ppermute | solution.py:52
  60.7 13.2 %collective-permute-start.9 = (f32[512,128]{1,0:T(8,128)S(1)}, f32[512,128]{1,0:T(8,128)S(1)}, u32[]{:S(2)}, u32[]{:S(2)}) collective-permute-start(f32[512,128]{1,0:T(8,128)S(1)} %get-tuple-element.37), channel_id=1, source_target_pairs={{0,4},{1,5},{2,6},{3,7},{4,0},{5,1},{6,2},{7,3},{8,12},{9,13},{10,... | collective-permute-start | bytes 786440 | tf_op jit(solution)/shard_map/ppermute | solution.py:52
  62.0 11.9 %collective-permute-start.8 = (f32[512,128]{1,0:T(8,128)S(1)}, f32[512,128]{1,0:T(8,128)S(1)}, u32[]{:S(2)}, u32[]{:S(2)}) collective-permute-start(f32[512,128]{1,0:T(8,128)S(1)} %get-tuple-element.38), channel_id=1, source_target_pairs={{0,2},{1,3},{2,0},{3,1},{4,6},{5,7},{6,4},{7,5},{8,10},{9,11},{10,... | collective-permute-start | bytes 786440 | tf_op jit(solution)/shard_map/ppermute | solution.py:52
  62.5 3.4 %copy-start = (bf16[2,2048,1024]{2,1,0:T(8,128)(2,1)S(1)}, bf16[2,2048,1024]{2,1,0:T(8,128)(2,1)}, u32[]{:S(2)}) copy-start(bf16[2,2048,1024]{2,1,0:T(8,128)(2,1)} %source) | copy-start | bytes 25165828
  74.0 6.9 %collective-permute-start.13 = (f32[128,128]{1,0:T(8,128)S(1)}, f32[128,128]{1,0:T(8,128)S(1)}, u32[]{:S(2)}, u32[]{:S(2)}) collective-permute-start(f32[128,128]{1,0:T(8,128)S(1)} %get-tuple-element.40), channel_id=1, source_target_pairs={{0,24},{1,25},{2,26},{3,27},{4,28},{5,29},{6,30},{7,31},{8,16},{9,... | collective-permute-start | bytes 196616 | tf_op jit(solution)/shard_map/ppermute | solution.py:52
  76.0 6.7 %collective-permute-start.12 = (f32[128,128]{1,0:T(8,128)S(1)}, f32[128,128]{1,0:T(8,128)S(1)}, u32[]{:S(2)}, u32[]{:S(2)}) collective-permute-start(f32[128,128]{1,0:T(8,128)S(1)} %get-tuple-element.41), channel_id=1, source_target_pairs={{0,16},{1,17},{2,18},{3,19},{4,20},{5,21},{6,22},{7,23},{8,24},{9,... | collective-permute-start | bytes 196616 | tf_op jit(solution)/shard_map/ppermute | solution.py:52
  76.2 6.6 %collective-permute-start.11 = (f32[128,128]{1,0:T(8,128)S(1)}, f32[128,128]{1,0:T(8,128)S(1)}, u32[]{:S(2)}, u32[]{:S(2)}) collective-permute-start(f32[128,128]{1,0:T(8,128)S(1)} %get-tuple-element.42), channel_id=1, source_target_pairs={{0,8},{1,9},{2,10},{3,11},{4,12},{5,13},{6,14},{7,15},{8,0},{9,1},... | collective-permute-start | bytes 196616 | tf_op jit(solution)/shard_map/ppermute | solution.py:52
  84.6 12.3 %all-to-all-start = ((f32[32,8,128]{2,1,0:T(8,128)}), f32[32,8,128]{2,1,0:T(8,128)S(1)}, u32[]{:S(2)}, u32[]{:S(2)}) async-start(f32[32,8,128]{2,1,0:T(8,128)} %shard_map.136), calls=%async_computation | async-start | bytes 262144 | tf_op jit(solution)/shard_map/all_to_all | solution.py:538
